TPU v7x, 256 devices: a whole 4x4x8 slice. The times are simulated.
256 devices in a mesh: rows: 32 (over y, z), cols: 8 (over x, core).
Axes of the slice: x: 4, y: 4, z: 8, core: 2. Of those that a mesh axis runs over, the one named last changes fastest.
Arguments:
- features: bfloat16 [4, 256, 1280, 128], P(None, 'rows', 'cols'), may hold values from -60 to 60
- conv_first: bfloat16 [3, 3, 3, 128, 128], replicated, may hold values from -0.109375 to 0.109375
- first_reduce_kernel: bfloat16 [3, 3, 128, 256], replicated, may hold values from -0.1875 to 0.1875
- conv_second: bfloat16 [3, 3, 3, 256, 256], replicated, may hold values from -0.078125 to 0.078125
- second_reduce_kernel: bfloat16 [3, 3, 256, 512], replicated, may hold values from -0.125 to 0.125
- conv_last: bfloat16 [3, 3, 3, 512, 32], replicated, may hold values from -0.0546875 to 0.0546875
- gain_first: float32 [128], replicated, may hold values from 0.5 to 1.5
- shift_first: float32 [128], replicated, may hold values from -0.5 to 0.5
- gain_second: float32 [256], replicated, may hold values from 0.5 to 1.5
- shift_second: float32 [256], replicated, may hold values from -0.5 to 0.5
- gain_third: float32 [512], replicated, may hold values from 0.5 to 1.5
- shift_third: float32 [512], replicated, may hold values from -0.5 to 0.5
Outputs:
- moments: bfloat16 [4, 64, 320, 32], P(None, 'rows', 'cols')
All inputs are finite; a program needn't handle non-finite values.
Results may differ from a plain program's by a relative error of at most 0.01.
Values may be sent and summed in bfloat16 or wider, within the bound.
No kernel may reach another device: no remote copies, remote signals or barrier semaphores. Data moves between devices by JAX's collectives and lax.ppermute only.
A program may use at most 64 MiB of HBM per device.

v0:
```python
import jax
import jax.numpy as jnp
from jax import lax
from jax.sharding import Mesh
from jax.sharding import PartitionSpec as P

GROUPS = 32
ROWS_COLS = ("rows_0", "rows_1", "cols_0", "cols_1")
ROWS = ("rows_0", "rows_1")
COLS = ("cols_0", "cols_1")


epsilon = 1e-06


def shortened(array):
    return jax.tree.map(lambda a: a.astype(jnp.bfloat16) if a.dtype == jnp.float32 else a, array)


def extended_2(array, sides, width):
    for axis, dim in sides:
        peers, length = (lax.axis_size(axis), array.shape[dim])
        up = [(i, (i + 1) % peers) for i in range(peers - 1)]
        down = [(j, i) for i, j in up]
        last = lax.slice_in_dim(array, length - width, length, axis=dim)
        first = lax.slice_in_dim(array, 0, width, axis=dim)
        before = lax.ppermute(last, axis, up)
        after = lax.ppermute(first, axis, down)
        array = jnp.concatenate([before, array, after], axis=dim)
    return array


def one_axis_at_a_time(array, axes):
    for axis in axes:
        array = lax.psum(array, axis)
    return array


def dilated(input_video, weight_tables, strides):
    return lax.conv_general_dilated(
        input_video[None],
        weight_tables,
        strides,
        "VALID",
        dimension_numbers=("NDHWC", "DHWIO", "NDHWC"),
        preferred_element_type=jnp.float32,
    )[0]


def causal_conv(padding, weight_tables):
    widened = jnp.concatenate([padding[:1], padding[:1], padding], axis=0)
    return dilated(widened, weight_tables, (1, 1, 1))


def rimmed(input_video, margin):
    return extended_2(shortened(input_video), ((ROWS, 1), (COLS, 2)), margin).astype(
        input_video.dtype
    )


def moments(values, members):
    grouped = values.reshape(values.shape[:3] + (GROUPS, -1))
    summed, squares = (
        one_axis_at_a_time(jnp.sum(grouped, axis=(0, 1, 2, 4)), ROWS_COLS),
        one_axis_at_a_time(jnp.sum(jnp.square(grouped), axis=(0, 1, 2, 4)), ROWS_COLS),
    )
    mean_value = summed / members
    variance = jnp.maximum(squares / members - mean_value * mean_value, 0.0)
    return (mean_value, variance)


def activate(values, mean_value, variance, norm_gain, norm_shift):
    extent = values.shape
    grouped = values.reshape(extent[:3] + (GROUPS, -1))
    result = ((grouped - mean_value[:, None]) / jnp.sqrt(variance[:, None] + epsilon)).reshape(
        extent
    ) * norm_gain + norm_shift
    return jax.nn.silu(result).astype(jnp.bfloat16)


def group_members(frames, row_count, col_count, channels):
    return float(
        frames
        * row_count
        * col_count
        * lax.axis_size(ROWS)
        * lax.axis_size(COLS)
        * (channels // GROUPS)
    )


def encode_level(input_video, conv_weights, down_weights, norm_gain, norm_shift):
    frames, row_count, col_count = input_video.shape[:3]
    members = group_members(frames, row_count, col_count, conv_weights.shape[4])
    hidden = causal_conv(rimmed(input_video, 2)[:, 1:, 1:], conv_weights)
    mean_value, variance = moments(hidden[:, :row_count, :col_count], members)
    activated = activate(hidden, mean_value, variance, norm_gain, norm_shift)
    row_ids = lax.broadcasted_iota(jnp.int32, (1, row_count + 1, col_count + 1, 1), 1)
    col_ids = lax.broadcasted_iota(jnp.int32, (1, row_count + 1, col_count + 1, 1), 2)
    last_row = lax.axis_index(ROWS) == lax.axis_size(ROWS) - 1
    last_col = lax.axis_index(COLS) == lax.axis_size(COLS) - 1
    outside = (row_ids == row_count) & last_row | (col_ids == col_count) & last_col
    extended = jnp.where(outside, jnp.zeros((), jnp.bfloat16), activated)
    return dilated(extended, down_weights[None], (1, 2, 2)).astype(jnp.bfloat16)


def shards(
    features,
    conv_first,
    first_reduce_kernel,
    conv_second,
    second_reduce_kernel,
    conv_last,
    gain_first,
    shift_first,
    gain_second,
    shift_second,
    gain_third,
    shift_third,
):
    middle_level_features = encode_level(
        features, conv_first, first_reduce_kernel, gain_first, shift_first
    )
    coarsest_level_features = encode_level(
        middle_level_features, conv_second, second_reduce_kernel, gain_second, shift_second
    )
    frames, row_count, col_count, channels = coarsest_level_features.shape
    members = group_members(frames, row_count, col_count, channels)
    values = coarsest_level_features.astype(jnp.float32)
    mean_value, variance = moments(values, members)
    activated = activate(values, mean_value, variance, gain_third, shift_third)
    return causal_conv(rimmed(activated, 1), conv_last).astype(jnp.bfloat16)


def solution(mesh):
    split = Mesh(mesh.devices.reshape(4, 8, 4, 2), ("rows_0", "rows_1", "cols_0", "cols_1"))
    return jax.shard_map(
        shards,
        mesh=split,
        in_specs=(P(None, ROWS, COLS, None), P(), P(), P(), P(), P(), P(), P(), P(), P(), P(), P()),
        out_specs=P(None, ROWS, COLS, None),
        check_vma=False,
    )
```

profile of v0, /device:TPU:1, one launch (start us, length us, event | category | flops | bytes accessed | tf_op | source)
XLA Modules:
  0.0 256.2 jit_solution(17263411504774354062)
XLA Ops:
  2.1 5.1 %collective-permute-start = (bf16[4,2,160,128]{3,2,1,0:T(8,128)(2,1)}, bf16[4,2,160,128]{3,2,1,0:T(8,128)(2,1)}, u32[]{:S(2)}, u32[]{:S(2)}) collective-permute-start(bf16[4,2,160,128]{3,2,1,0:T(8,128)(2,1)} %get-tuple-element.40), channel_id=1, source_target_pairs={{0,8},{8,16},{16,24},{24,32},{32,40},{40,48},{48,56},{56,64},{64,7... | collective-permute-start | bytes 983048 | tf_op jit(solution)/shard_map/ppermute | solution.py:27
  8.5 4.6 %collective-permute-done = bf16[4,2,160,128]{3,2,1,0:T(8,128)(2,1)} collective-permute-done((bf16[4,2,160,128]{3,2,1,0:T(8,128)(2,1)}, bf16[4,2,160,128]{3,2,1,0:T(8,128)(2,1)}, u32[]{:S(2)}, u32[]{:S(2)}) %collective-permute-start) | collective-permute-done | bytes 327712 | tf_op jit(solution)/shard_map/ppermute | solution.py:27
  18.7 4.9 %collective-permute-start.2 = (bf16[4,12,2,128]{3,2,1,0:T(2,128)(2,1)S(1)}, bf16[4,12,2,128]{3,2,1,0:T(2,128)(2,1)S(1)}, u32[]{:S(2)}, u32[]{:S(2)}) collective-permute-start(bf16[4,12,2,128]{3,2,1,0:T(2,128)(2,1)S(1)} %get-tuple-element.35), channel_id=1, source_target_pairs={{0,1},{1,2},{2,3},{3,4},{4,5},{5,6},{6,7},{8,9},{9,10},{10,11},{11... | collective-permute-start | bytes 73736 | tf_op jit(solution)/shard_map/ppermute | solution.py:27
  33.2 5.7 %reshape.107 = bf16[6,11,1,8,21,128]{5,4,3,1,0,2:T(8,128)(2,1)} reshape(bf16[6,11,1,168,128]{4,3,1,0,2:T(8,128)(2,1)} %pad) | data formatting | bytes 5677056 | tf_op jit(solution)/shard_map/conv_general_dilated | solution.py:40
  41.6 11.6 %fusion.32 = f32[4,9,8,21,128]{4,2,3,1,0:T(8,128)S(1)} fusion(bf16[3,3,3,128,128]{4,3,2,1,0:T(8,128)(2,1)S(1)} %copy-done.10, bf16[6,11,1,7,2,128]{5,3,4,1,0,2:T(8,128)(2,1)S(1)} %slice.95, bf16[6,11,1,8,21,128]{5,3,4,1,0,2:T(8,128)(2,1)S(1)} %copy.32, pred[8,21]{0,1:T(8,128)(4,1)S(1)} %copy-done.13), kind=kOutput, calls=%fused_computation.45 | convolution fusion | flops 5360984064 | bytes 7056552 | tf_op jit(solution)/shard_map/conv_general_dilated | solution.py:40
  60.7 11.3 %all-reduce.8 = (f32[32]{0:T(128)S(1)}, f32[32]{0:T(128)S(1)}) all-reduce(f32[32]{0:T(128)S(1)} %reduce_sum.77, f32[32]{0:T(128)} %reduce_sum.74), channel_id=1, replica_groups=mesh['rows_0'=4,'rows_1'=8,'cols_0'=4,'cols_1'=2] {'rows_0'}, use_global_device_ids=true, to_apply=%region_8.0 | all-reduce | flops 64 | bytes 512 | tf_op jit(solution)/shard_map/psum | solution.py:35
  72.0 12.1 %all-reduce.2 = (f32[32]{0:T(128)S(1)}, f32[32]{0:T(128)S(1)}) all-reduce(f32[32]{0:T(128)S(1)} %get-tuple-element.27, f32[32]{0:T(128)S(1)} %get-tuple-element.28), channel_id=1, replica_groups=mesh['rows_0'=4,'rows_1'=8,'cols_0'=4,'cols_1'=2] {'rows_1'}, use_global_device_ids=true, to_apply=%region_9.0 | all-reduce | flops 64 | bytes 512 | tf_op jit(solution)/shard_map/psum | solution.py:35
  84.1 7.8 %all-reduce.5 = (f32[32]{0:T(128)S(1)}, f32[32]{0:T(128)}) all-reduce(f32[32]{0:T(128)S(1)} %get-tuple-element.15, f32[32]{0:T(128)S(1)} %get-tuple-element.16), channel_id=1, replica_groups=mesh['rows_0'=4,'rows_1'=8,'cols_0'=4,'cols_1'=2] {'cols_0'}, use_global_device_ids=true, to_apply=%region_10.11 | all-reduce | flops 64 | bytes 512 | tf_op jit(solution)/shard_map/psum | solution.py:35
  91.9 10.0 %all-reduce.11 = (f32[32]{0:T(128)S(1)}, f32[32]{0:T(128)S(1)}) all-reduce(f32[32]{0:T(128)S(1)} %get-tuple-element.21, f32[32]{0:T(128)} %get-tuple-element.22), channel_id=1, replica_groups=mesh['rows_0'=4,'rows_1'=8,'cols_0'=4,'cols_1'=2] {'cols_1'}, use_global_device_ids=true, to_apply=%region_11.12 | all-reduce | flops 64 | bytes 512 | tf_op jit(solution)/shard_map/psum | solution.py:35
  117.5 5.4 %collective-permute-done.4 = bf16[4,2,80,256]{3,1,2,0:T(2,128)(2,1)S(1)} collective-permute-done((bf16[4,2,80,256]{3,1,2,0:T(2,128)(2,1)S(1)}, bf16[4,2,80,256]{3,1,2,0:T(2,128)(2,1)S(1)}, u32[]{:S(2)}, u32[]{:S(2)}) %collective-permute-start.4) | collective-permute-done | bytes 327712 | tf_op jit(solution)/shard_map/ppermute | solution.py:27
  122.9 3.8 %collective-permute-done.5 = bf16[4,2,80,256]{3,1,2,0:T(2,128)(2,1)S(1)} collective-permute-done((bf16[4,2,80,256]{3,1,2,0:T(2,128)(2,1)S(1)}, bf16[4,2,80,256]{3,1,2,0:T(2,128)(2,1)S(1)}, u32[]{:S(2)}, u32[]{:S(2)}) %collective-permute-start.5) | collective-permute-done | bytes 327712 | tf_op jit(solution)/shard_map/ppermute | solution.py:28
  137.8 7.3 %fusion.43 = f32[4,5,8,11,256]{4,2,3,1,0:T(8,128)S(1)} fusion(bf16[3,3,3,256,256]{4,3,2,1,0:T(8,128)(2,1)S(1)} %copy-done, bf16[6,7,1,7,2,256]{5,3,4,1,0,2:T(8,128)(2,1)S(1)} %slice.103, bf16[6,7,1,8,11,256]{5,3,4,1,0,2:T(8,128)(2,1)S(1)} %copy.39, pred[8,11]{0,1:T(8,128)(4,1)S(1)} %copy-done.14), kind=kOutput, calls=%fused_computation.55 | convolution fusion | flops 6235701248 | bytes 7534680 | tf_op jit(solution)/shard_map/conv_general_dilated | solution.py:40
  147.2 7.9 %all-reduce.7 = (f32[32]{0:T(128)S(1)}, f32[32]{0:T(128)S(1)}) all-reduce(f32[32]{0:T(128)S(1)} %reduce_sum.89, f32[32]{0:T(128)S(1)} %reduce_sum.83), channel_id=1, replica_groups=mesh['rows_0'=4,'rows_1'=8,'cols_0'=4,'cols_1'=2] {'rows_0'}, use_global_device_ids=true, to_apply=%region_20.21 | all-reduce | flops 64 | bytes 512 | tf_op jit(solution)/shard_map/psum | solution.py:35
  155.1 13.8 %all-reduce.1 = (f32[32]{0:T(128)S(1)}, f32[32]{0:T(128)S(1)}) all-reduce(f32[32]{0:T(128)S(1)} %get-tuple-element.25, f32[32]{0:T(128)S(1)} %get-tuple-element.26), channel_id=1, replica_groups=mesh['rows_0'=4,'rows_1'=8,'cols_0'=4,'cols_1'=2] {'rows_1'}, use_global_device_ids=true, to_apply=%region_21.22 | all-reduce | flops 64 | bytes 512 | tf_op jit(solution)/shard_map/psum | solution.py:35
  168.9 6.9 %all-reduce.4 = (f32[32]{0:T(128)S(1)}, f32[32]{0:T(128)S(1)}) all-reduce(f32[32]{0:T(128)S(1)} %get-tuple-element.13, f32[32]{0:T(128)S(1)} %get-tuple-element.14), channel_id=1, replica_groups=mesh['rows_0'=4,'rows_1'=8,'cols_0'=4,'cols_1'=2] {'cols_0'}, use_global_device_ids=true, to_apply=%region_22.23 | all-reduce | flops 64 | bytes 512 | tf_op jit(solution)/shard_map/psum | solution.py:35
  175.8 9.0 %all-reduce.10 = (f32[32]{0:T(128)S(1)}, f32[32]{0:T(128)S(1)}) all-reduce(f32[32]{0:T(128)S(1)} %get-tuple-element.19, f32[32]{0:T(128)S(1)} %get-tuple-element.20), channel_id=1, replica_groups=mesh['rows_0'=4,'rows_1'=8,'cols_0'=4,'cols_1'=2] {'cols_1'}, use_global_device_ids=true, to_apply=%region_23.24 | all-reduce | flops 64 | bytes 512 | tf_op jit(solution)/shard_map/psum | solution.py:35
  192.0 7.7 %all-reduce.6 = (f32[32]{0:T(128)S(1)}, f32[32]{0:T(128)S(1)}) all-reduce(f32[32]{0:T(128)S(1)} %reduce_sum.113, f32[32]{0:T(128)S(1)} %reduce_sum.110), channel_id=1, replica_groups=mesh['rows_0'=4,'rows_1'=8,'cols_0'=4,'cols_1'=2] {'rows_0'}, use_global_device_ids=true, to_apply=%region_32.33 | all-reduce | flops 64 | bytes 512 | tf_op jit(solution)/shard_map/psum | solution.py:35
  199.7 10.7 %all-reduce = (f32[32]{0:T(128)S(1)}, f32[32]{0:T(128)S(1)}) all-reduce(f32[32]{0:T(128)S(1)} %get-tuple-element.23, f32[32]{0:T(128)S(1)} %get-tuple-element.24), channel_id=1, replica_groups=mesh['rows_0'=4,'rows_1'=8,'cols_0'=4,'cols_1'=2] {'rows_1'}, use_global_device_ids=true, to_apply=%region_33.34 | all-reduce | flops 64 | bytes 512 | tf_op jit(solution)/shard_map/psum | solution.py:35
  210.3 6.1 %all-reduce.3 = (f32[32]{0:T(128)S(1)}, f32[32]{0:T(128)S(1)}) all-reduce(f32[32]{0:T(128)S(1)} %get-tuple-element.11, f32[32]{0:T(128)S(1)} %get-tuple-element.12), channel_id=1, replica_groups=mesh['rows_0'=4,'rows_1'=8,'cols_0'=4,'cols_1'=2] {'cols_0'}, use_global_device_ids=true, to_apply=%region_34.35 | all-reduce | flops 64 | bytes 512 | tf_op jit(solution)/shard_map/psum | solution.py:35
  216.5 10.0 %all-reduce.9 = (f32[32]{0:T(128)S(1)}, f32[32]{0:T(128)S(1)}) all-reduce(f32[32]{0:T(128)S(1)} %get-tuple-element.17, f32[32]{0:T(128)S(1)} %get-tuple-element.18), channel_id=1, replica_groups=mesh['rows_0'=4,'rows_1'=8,'cols_0'=4,'cols_1'=2] {'cols_1'}, use_global_device_ids=true, to_apply=%region_35.36 | all-reduce | flops 64 | bytes 512 | tf_op jit(solution)/shard_map/psum | solution.py:35
  227.7 3.6 %collective-permute-start.8 = (bf16[4,1,40,512]{3,2,1,0:T(8,128)(2,1)S(1)}, bf16[4,1,40,512]{3,2,1,0:T(8,128)(2,1)S(1)}, u32[]{:S(2)}, u32[]{:S(2)}) collective-permute-start(bf16[4,1,40,512]{3,2,1,0:T(8,128)(2,1)S(1)} %get-tuple-element.45), channel_id=1, source_target_pairs={{0,8},{8,16},{16,24},{24,32},{32,40},{40,48},{48,56},{56,64},{64,7... | collective-permute-start | bytes 491528 | tf_op jit(solution)/shard_map/ppermute | solution.py:27
  234.6 3.8 %collective-permute-done.9 = bf16[4,1,40,512]{3,2,1,0:T(8,128)(2,1)S(1)} collective-permute-done((bf16[4,1,40,512]{3,2,1,0:T(8,128)(2,1)S(1)}, bf16[4,1,40,512]{3,2,1,0:T(8,128)(2,1)S(1)}, u32[]{:S(2)}, u32[]{:S(2)}) %collective-permute-start.9) | collective-permute-done | bytes 163872 | tf_op jit(solution)/shard_map/ppermute | solution.py:28
  238.4 4.6 %collective-permute-start.10 = (bf16[4,4,1,512]{3,2,1,0:T(2,128)(2,1)S(1)}, bf16[4,4,1,512]{3,2,1,0:T(2,128)(2,1)S(1)}, u32[]{:S(2)}, u32[]{:S(2)}) collective-permute-start(bf16[4,4,1,512]{3,2,1,0:T(2,128)(2,1)S(1)} %get-tuple-element.41), channel_id=1, source_target_pairs={{0,1},{1,2},{2,3},{3,4},{4,5},{5,6},{6,7},{8,9},{9,10},{10,11},{11... | collective-permute-start | bytes 49160 | tf_op jit(solution)/shard_map/ppermute | solution.py:27
  245.0 3.3 %collective-permute-done.11 = bf16[4,4,1,512]{3,2,1,0:T(2,128)(2,1)S(1)} collective-permute-done((bf16[4,4,1,512]{3,2,1,0:T(2,128)(2,1)S(1)}, bf16[4,4,1,512]{3,2,1,0:T(2,128)(2,1)S(1)}, u32[]{:S(2)}, u32[]{:S(2)}) %collective-permute-start.11) | collective-permute-done | bytes 16416 | tf_op jit(solution)/shard_map/ppermute | solution.py:28
  (136 shorter events, 78.3 us)
Async XLA Ops:
  0.0 137.6 %copy-start = (bf16[3,3,3,256,256]{4,3,2,1,0:T(8,128)(2,1)S(1)}, bf16[3,3,3,256,256]{4,3,2,1,0:T(8,128)(2,1)}, u32[]{:S(2)}) copy-start(bf16[3,3,3,256,256]{4,3,2,1,0:T(8,128)(2,1)} %param.15) | copy-start | bytes 10616836
  2.1 11.0 %collective-permute-start = (bf16[4,2,160,128]{3,2,1,0:T(8,128)(2,1)}, bf16[4,2,160,128]{3,2,1,0:T(8,128)(2,1)}, u32[]{:S(2)}, u32[]{:S(2)}) collective-permute-start(bf16[4,2,160,128]{3,2,1,0:T(8,128)(2,1)} %get-tuple-element.40), channel_id=1, source_target_pairs={{0,8},{8,16},{16,24},{24,32},{32,40},{40,48},{48,56},{56,64},{64,7... | collective-permute-start | bytes 983048 | tf_op jit(solution)/shard_map/ppermute | solution.py:27
  7.2 10.5 %collective-permute-start.1 = (bf16[4,2,160,128]{3,2,1,0:T(8,128)(2,1)}, bf16[4,2,160,128]{3,2,1,0:T(8,128)(2,1)}, u32[]{:S(2)}, u32[]{:S(2)}) collective-permute-start(bf16[4,2,160,128]{3,2,1,0:T(8,128)(2,1)} %get-tuple-element.39), channel_id=1, source_target_pairs={{8,0},{16,8},{24,16},{32,24},{40,32},{48,40},{56,48},{64,56},{72,6... | collective-permute-start | bytes 983048 | tf_op jit(solution)/shard_map/ppermute | solution.py:28
  18.7 7.5 %collective-permute-start.2 = (bf16[4,12,2,128]{3,2,1,0:T(2,128)(2,1)S(1)}, bf16[4,12,2,128]{3,2,1,0:T(2,128)(2,1)S(1)}, u32[]{:S(2)}, u32[]{:S(2)}) collective-permute-start(bf16[4,12,2,128]{3,2,1,0:T(2,128)(2,1)S(1)} %get-tuple-element.35), channel_id=1, source_target_pairs={{0,1},{1,2},{2,3},{3,4},{4,5},{5,6},{6,7},{8,9},{9,10},{10,11},{11... | collective-permute-start | bytes 73736 | tf_op jit(solution)/shard_map/ppermute | solution.py:27
  23.6 5.1 %collective-permute-start.3 = (bf16[4,12,2,128]{3,2,1,0:T(2,128)(2,1)S(1)}, bf16[4,12,2,128]{3,2,1,0:T(2,128)(2,1)S(1)}, u32[]{:S(2)}, u32[]{:S(2)}) collective-permute-start(bf16[4,12,2,128]{3,2,1,0:T(2,128)(2,1)S(1)} %get-tuple-element.36), channel_id=1, source_target_pairs={{1,0},{2,1},{3,2},{4,3},{5,4},{6,5},{7,6},{9,8},{10,9},{11,10},{12... | collective-permute-start | bytes 73736 | tf_op jit(solution)/shard_map/ppermute | solution.py:28
  39.0 2.6 copy-start.10
  39.0 2.6 copy-start.13
  53.2 1.6 copy-start.2
  114.2 8.7 %collective-permute-start.4 = (bf16[4,2,80,256]{3,1,2,0:T(2,128)(2,1)S(1)}, bf16[4,2,80,256]{3,1,2,0:T(2,128)(2,1)S(1)}, u32[]{:S(2)}, u32[]{:S(2)}) collective-permute-start(bf16[4,2,80,256]{3,1,2,0:T(2,128)(2,1)S(1)} %get-tuple-element.43), channel_id=1, source_target_pairs={{0,8},{8,16},{16,24},{24,32},{32,40},{40,48},{48,56},{56,64},{64,7... | collective-permute-start | bytes 983048 | tf_op jit(solution)/shard_map/ppermute | solution.py:27
  116.2 10.5 %collective-permute-start.5 = (bf16[4,2,80,256]{3,1,2,0:T(2,128)(2,1)S(1)}, bf16[4,2,80,256]{3,1,2,0:T(2,128)(2,1)S(1)}, u32[]{:S(2)}, u32[]{:S(2)}) collective-permute-start(bf16[4,2,80,256]{3,1,2,0:T(2,128)(2,1)S(1)} %get-tuple-element.44), channel_id=1, source_target_pairs={{8,0},{16,8},{24,16},{32,24},{40,32},{48,40},{56,48},{64,56},{72,6... | collective-permute-start | bytes 983048 | tf_op jit(solution)/shard_map/ppermute | solution.py:28
  126.8 4.8 %collective-permute-start.6 = (bf16[4,8,2,256]{3,1,2,0:T(8,128)(2,1)S(1)}, bf16[4,8,2,256]{3,1,2,0:T(8,128)(2,1)S(1)}, u32[]{:S(2)}, u32[]{:S(2)}) collective-permute-start(bf16[4,8,2,256]{3,1,2,0:T(8,128)(2,1)S(1)} %get-tuple-element.37), channel_id=1, source_target_pairs={{0,1},{1,2},{2,3},{3,4},{4,5},{5,6},{6,7},{8,9},{9,10},{10,11},{11... | collective-permute-start | bytes 98312 | tf_op jit(solution)/shard_map/ppermute | solution.py:27
  129.4 5.2 %collective-permute-start.7 = (bf16[4,8,2,256]{3,1,2,0:T(8,128)(2,1)S(1)}, bf16[4,8,2,256]{3,1,2,0:T(8,128)(2,1)S(1)}, u32[]{:S(2)}, u32[]{:S(2)}) collective-permute-start(bf16[4,8,2,256]{3,1,2,0:T(8,128)(2,1)S(1)} %get-tuple-element.38), channel_id=1, source_target_pairs={{1,0},{2,1},{3,2},{4,3},{5,4},{6,5},{7,6},{9,8},{10,9},{11,10},{12... | collective-permute-start | bytes 98312 | tf_op jit(solution)/shard_map/ppermute | solution.py:28
  145.0 1.2 copy-start.3
  145.8 39.4 %copy-start.7 = (f32[256]{0:T(256)S(1)}, f32[256]{0:T(256)}, u32[]{:S(2)}) copy-start(f32[256]{0:T(256)} %param.21) | copy-start | bytes 3076
  145.8 39.4 %copy-start.8 = (f32[256]{0:T(256)S(1)}, f32[256]{0:T(256)}, u32[]{:S(2)}) copy-start(f32[256]{0:T(256)} %param.20) | copy-start | bytes 3076
  188.7 1.7 copy-start.9
  188.7 1.7 copy-start.16
  190.4 37.1 %copy-start.5 = (f32[512]{0:T(512)S(1)}, f32[512]{0:T(512)}, u32[]{:S(2)}) copy-start(f32[512]{0:T(512)} %param.23) | copy-start | bytes 6148
  190.4 37.1 %copy-start.6 = (f32[512]{0:T(512)S(1)}, f32[512]{0:T(512)}, u32[]{:S(2)}) copy-start(f32[512]{0:T(512)} %param.22) | copy-start | bytes 6148
  227.7 6.9 %collective-permute-start.8 = (bf16[4,1,40,512]{3,2,1,0:T(8,128)(2,1)S(1)}, bf16[4,1,40,512]{3,2,1,0:T(8,128)(2,1)S(1)}, u32[]{:S(2)}, u32[]{:S(2)}) collective-permute-start(bf16[4,1,40,512]{3,2,1,0:T(8,128)(2,1)S(1)} %get-tuple-element.45), channel_id=1, source_target_pairs={{0,8},{8,16},{16,24},{24,32},{32,40},{40,48},{48,56},{56,64},{64,7... | collective-permute-start | bytes 491528 | tf_op jit(solution)/shard_map/ppermute | solution.py:27
  231.4 7.0 %collective-permute-start.9 = (bf16[4,1,40,512]{3,2,1,0:T(8,128)(2,1)S(1)}, bf16[4,1,40,512]{3,2,1,0:T(8,128)(2,1)S(1)}, u32[]{:S(2)}, u32[]{:S(2)}) collective-permute-start(bf16[4,1,40,512]{3,2,1,0:T(8,128)(2,1)S(1)} %get-tuple-element.46), channel_id=1, source_target_pairs={{8,0},{16,8},{24,16},{32,24},{40,32},{48,40},{56,48},{64,56},{72,6... | collective-permute-start | bytes 491528 | tf_op jit(solution)/shard_map/ppermute | solution.py:28
  238.4 6.5 %collective-permute-start.10 = (bf16[4,4,1,512]{3,2,1,0:T(2,128)(2,1)S(1)}, bf16[4,4,1,512]{3,2,1,0:T(2,128)(2,1)S(1)}, u32[]{:S(2)}, u32[]{:S(2)}) collective-permute-start(bf16[4,4,1,512]{3,2,1,0:T(2,128)(2,1)S(1)} %get-tuple-element.41), channel_id=1, source_target_pairs={{0,1},{1,2},{2,3},{3,4},{4,5},{5,6},{6,7},{8,9},{9,10},{10,11},{11... | collective-permute-start | bytes 49160 | tf_op jit(solution)/shard_map/ppermute | solution.py:27
  243.0 5.2 %collective-permute-start.11 = (bf16[4,4,1,512]{3,2,1,0:T(2,128)(2,1)S(1)}, bf16[4,4,1,512]{3,2,1,0:T(2,128)(2,1)S(1)}, u32[]{:S(2)}, u32[]{:S(2)}) collective-permute-start(bf16[4,4,1,512]{3,2,1,0:T(2,128)(2,1)S(1)} %get-tuple-element.42), channel_id=1, source_target_pairs={{1,0},{2,1},{3,2},{4,3},{5,4},{6,5},{7,6},{9,8},{10,9},{11,10},{12... | collective-permute-start | bytes 49160 | tf_op jit(solution)/shard_map/ppermute | solution.py:28
  250.7 5.3 %copy-start.1 = (bf16[3,3,3,256,256]{4,3,2,1,0:T(8,128)(2,1)S(1)}, bf16[3,3,3,256,256]{4,3,2,1,0:T(8,128)(2,1)}, u32[]{:S(2)}) copy-start(bf16[3,3,3,256,256]{4,3,2,1,0:T(8,128)(2,1)} %param.15) | copy-start | bytes 10616836
  (5 other events, 4.7 us)
where the time goes:
time: 260 us; the launch traced here: 256 us
  blocking collectives  113 us (43%)
  local copies, waits for them, and re-layouts  35.3 us (14%)
  starting transfers between devices  32.6 us (13%)
  waiting for transfers between devices  30.5 us (12%)
  matrix products  24.1 us (9%)
  other arithmetic  19.6 us (8%)
    psum x12, blocking collectives, one_axis_at_a_time(): array = lax.psum(array, axis)  113 us
    conv_general_dilated x5, matrix products, dilated(): lax.conv_general_dilated(input_video[None], weight_tables, strides, 'VALI...  24.1 us
    ppermute x6, starting transfers between devices, extended_2(): before = lax.ppermute(last, axis, up)  22.8 us
    ppermute x6, waiting for transfers between devices, extended_2(): after = lax.ppermute(first, axis, down)  18.5 us
    ppermute x6, waiting for transfers between devices, extended_2(): before = lax.ppermute(last, axis, up)  11.9 us
    conv_general_dilated x13, local copies, waits for them, and re-layouts, dilated(): lax.conv_general_dilated(input_video[None], weight_tables, strides, 'VALI...  11.9 us
    ppermute x6, starting transfers between devices, extended_2(): after = lax.ppermute(first, axis, down)  9.77 us
    unnamed x37, local copies, waits for them, and re-layouts  6.04 us
  transfers between devices with their start and end apart: 12, of which 9 were waited for; matrix products, arithmetic and copies ran while one was open for 1% of the time, Pallas kernels for 0%

commit v1 on v0

v1 whole, which is shorter than its diff:
```python
import functools

import jax
import jax.numpy as jnp
from jax import lax
from jax.experimental import pallas as pl
from jax.experimental.pallas import tpu as pltpu
from jax.sharding import PartitionSpec as P

GROUPS = 32
EPSILON = 1e-6
FRAMES = 4
ROWS = 8
COLS = 160
C1, C2, C3, OUT = 128, 256, 512, 32
Q = 48
PAD = 2
OWN = COLS // 4
LEFT, RIGHT = 8, 16
LINE = 208
AXES = ("rows", "cols")
F32, BF16 = jnp.float32, jnp.bfloat16
VMEM = pl.BlockSpec(memory_space=pltpu.VMEM)
SMEM = pl.BlockSpec(memory_space=pltpu.SMEM)
ANY = pl.BlockSpec(memory_space=pl.ANY)


def params(mib):
    return pltpu.CompilerParams(vmem_limit_bytes=mib * 1024 * 1024)


def cost(flops, read):
    return pl.CostEstimate(flops=int(flops), bytes_accessed=int(read), transcendentals=0)


def shape(dims, dtype):
    return jax.ShapeDtypeStruct(dims, dtype)


def mm(left, right):
    return jnp.dot(left, right, preferred_element_type=F32)


def exact(left, right):
    return jnp.dot(left, right, preferred_element_type=F32, precision=lax.Precision.HIGHEST)


def weights_kernel(first, second, last, one, two, three):
    zero = jnp.zeros((C1, C1), BF16)
    for b in range(3):
        for e in range(3):
            taps = [first[((a * 3 + b) * 3 + e) * C1 : ((a * 3 + b) * 3 + e + 1) * C1, :] for a in range(3)]
            wide = [k.astype(F32) for k in taps]
            pair = wide[0] + wide[1]
            for s, k in enumerate(taps + [pair.astype(BF16), (pair + wide[2]).astype(BF16)]):
                base = s * 12 * C1 + b * 4 * C1
                one[base + e * C1 : base + (e + 1) * C1, 0:C1] = k
                one[base + (e + 1) * C1 : base + (e + 2) * C1, C1 : 2 * C1] = k
        for s in range(5):
            base = s * 12 * C1 + b * 4 * C1
            one[base + 3 * C1 : base + 4 * C1, 0:C1] = zero
            one[base : base + C1, C1 : 2 * C1] = zero

    def add(i, carry):
        at = pl.ds(pl.multiple_of(i * C2, C2), C2)
        pair = second[0, at, :].astype(F32) + second[1, at, :].astype(F32)
        two[0, at, :] = pair.astype(BF16)
        two[1, at, :] = (pair + second[2, at, :].astype(F32)).astype(BF16)
        return carry

    lax.fori_loop(0, 9, add, 0)

    def pack(i, carry):
        at = pl.ds(pl.multiple_of(i * C3, C3), C3)
        zeros = jnp.zeros((C3, OUT), BF16)
        three[at, :] = jnp.concatenate([last[0, at, :], last[1, at, :], last[2, at, :], zeros], axis=1)
        return carry

    lax.fori_loop(0, 9, pack, 0)


def weights(first, second, last):
    return pl.pallas_call(
        weights_kernel,
        out_shape=(
            shape((5 * 12 * C1, 2 * C1), BF16),
            shape((2, 9 * C2, C2), BF16),
            shape((9 * C3, 4 * OUT), BF16),
        ),
        in_specs=[VMEM] * 3,
        out_specs=(VMEM,) * 3,
        compiler_params=params(40),
        cost_estimate=cost(0, 12e6),
        name="weights",
    )(first.reshape(27 * C1, C1), second.reshape(3, 9 * C2, C2), last.reshape(3, 9 * C3, OUT))


def planes_kernel(left, own, right, planes, top, bottom, line):
    def step(i, carry):
        line[i, 0:8, :] = jnp.zeros((8, C1), F32)
        line[i, 8:16, :] = left[i].astype(F32)
        line[i, 16 : 16 + COLS, :] = own[i].astype(F32)
        line[i, 16 + COLS : 32 + COLS, :] = right[i].astype(F32)
        line[i, 32 + COLS : LINE, :] = jnp.zeros((LINE - 32 - COLS, C1), F32)
        for k in range(6):
            planes[i, :, k * C1 : (k + 1) * C1] = line[i, pl.ds(7 + k, Q, stride=4), :].astype(BF16)
        return carry

    lax.fori_loop(0, FRAMES * ROWS, step, 0)
    for t in range(FRAMES):
        top[t] = planes[t * ROWS, :, C1 : 5 * C1]
        bottom[t] = planes[t * ROWS + ROWS - 1, :, C1 : 5 * C1]


def planes_of(left, own, right):
    lines = FRAMES * ROWS
    return pl.pallas_call(
        planes_kernel,
        out_shape=(
            shape((lines, Q, 6 * C1), BF16),
            shape((FRAMES, Q, 4 * C1), BF16),
            shape((FRAMES, Q, 4 * C1), BF16),
        ),
        in_specs=[VMEM] * 3,
        out_specs=(VMEM,) * 3,
        scratch_shapes=[pltpu.VMEM((lines, LINE, C1), F32)],
        compiler_params=params(24),
        cost_estimate=cost(0, 4e6),
        name="planes",
    )(
        left.reshape(lines, LEFT, C1),
        own.reshape(lines, COLS, C1),
        right.reshape(lines, RIGHT, C1),
    )


def own_entries(rows, lanes):
    at = lax.rem(lax.broadcasted_iota(jnp.int32, (rows, lanes), 0), Q)
    return (at >= PAD) & (at < PAD + OWN)


def sums(values, mask):
    kept = jnp.where(mask, values, 0.0)
    return jnp.sum(kept, axis=0, keepdims=True), jnp.sum(kept * kept, axis=0, keepdims=True)


def frames_conv(frame, weight, size, store):
    cat = lambda parts: jnp.concatenate(parts, axis=1)
    store(0, mm(frame(0), weight(4)))
    store(1, mm(frame(0), weight(3)) + mm(frame(1), weight(2)))
    for t in range(2, FRAMES):
        store(t, mm(frame(t - 2), weight(0)) + mm(frame(t - 1), weight(1)) + mm(frame(t), weight(2)))


def middle_kernel(planes, table, hidden, stats):
    count = ROWS - 2
    rows = count * Q
    mask = own_entries(2 * rows, 2 * C1)
    stats[...] = jnp.zeros(stats.shape, F32)

    def frame(t):
        parts = []
        for b in range(3):
            block = planes[t * ROWS + b : t * ROWS + b + count].reshape(rows, 6 * C1)
            parts.append(jnp.concatenate([block[:, : 4 * C1], block[:, 2 * C1 :]], axis=0))
        return jnp.concatenate(parts, axis=1)

    def store(t, value):
        hidden[t, :, 0:Q, :] = value[:rows].reshape(count, Q, 2 * C1)
        hidden[t, :, Q : 2 * Q, :] = value[rows:].reshape(count, Q, 2 * C1)
        one, two = sums(value, mask)
        stats[0:1, :] += one
        stats[1:2, :] += two

    def weight(s):
        return table[s * 12 * C1 : (s + 1) * 12 * C1, :]

    frames_conv(frame, weight, 0, store)


def middle(planes, table):
    return pl.pallas_call(
        middle_kernel,
        out_shape=(
            shape((FRAMES, ROWS - 2, 2 * Q, 2 * C1), F32),
            shape((8, 2 * C1), F32),
        ),
        in_specs=[VMEM] * 2,
        out_specs=(VMEM,) * 2,
        compiler_params=params(48),
        cost_estimate=cost(6e9, 10e6),
        name="middle",
    )(planes, table)


def group_matrix(channels, shift):
    per = channels // GROUPS
    c = lax.broadcasted_iota(jnp.int32, (channels, 128), 0)
    g = lax.broadcasted_iota(jnp.int32, (channels, 128), 1)
    low = (g - shift) * per
    return jnp.where((c >= low) & (c < low + per), 1.0, 0.0).astype(F32)


def spread_matrix(channels, shift):
    per = channels // GROUPS
    g = lax.broadcasted_iota(jnp.int32, (128, channels), 0)
    c = lax.broadcasted_iota(jnp.int32, (128, channels), 1)
    low = (g - shift) * per
    return jnp.where((c >= low) & (c < low + per), 1.0, 0.0).astype(F32)


def grouped(one, two):
    channels = one.shape[1]
    wide = lambda v: jnp.broadcast_to(v, (8, channels))
    row = exact(wide(one), group_matrix(channels, 0)) + exact(wide(two), group_matrix(channels, GROUPS))
    return row[0:1]


def norm_terms(gathered, gain, shift, members):
    channels = gain.shape[1]
    total = jnp.broadcast_to(jnp.sum(gathered[...], axis=0, keepdims=True), (8, 128))
    mean = exact(total, spread_matrix(channels, 0))[0:1] / members
    square = exact(total, spread_matrix(channels, GROUPS))[0:1] / members
    variance = jnp.maximum(square - mean * mean, 0.0)
    return mean, gain[...] / jnp.sqrt(variance + EPSILON), shift[...]


def edges_kernel(planes, above, below, table, inner, stats, hidden, share, up, down, halo):
    rows = 2 * Q
    lane = 4 * C1
    for t in range(FRAMES):
        for side, ref in enumerate((above, below)):
            whole = ref[t]
            first = pltpu.roll(whole[:, 3 * C1 :].astype(F32), 1, 0).astype(BF16)
            last = pltpu.roll(whole[:, :C1].astype(F32), Q - 1, 0).astype(BF16)
            halo[side, t, :, 0:C1] = first
            halo[side, t, :, C1 : 5 * C1] = whole
            halo[side, t, :, 5 * C1 :] = last

    def frame(t):
        at = t * ROWS
        lines = [
            [halo[0, t], planes[at], planes[at + 1]],
            [planes[at + ROWS - 2], planes[at + ROWS - 1], halo[1, t]],
        ]
        out = []
        for side in range(2):
            for low in (0, 2 * C1):
                out.append(jnp.concatenate([v[:, low : low + lane] for v in lines[side]], axis=1))
        return jnp.concatenate(out, axis=0)

    mask = own_entries(2 * rows, 2 * C1)
    total = [stats[0:1, :], stats[1:2, :]]

    def store(t, value):
        hidden[t, 0] = value[:rows]
        hidden[t, 1] = value[rows:]
        up[t, 0] = value[:rows].astype(BF16)
        down[t, 1] = value[rows:].astype(BF16)
        one, two = sums(value, mask)
        total[0] += one
        total[1] += two

    frames_conv(frame, lambda s: table[s * 12 * C1 : (s + 1) * 12 * C1, :], 0, store)
    for t in range(FRAMES):
        up[t, 1] = inner[t, 0].astype(BF16)
        up[t, 2] = inner[t, 1].astype(BF16)
        down[t, 0] = inner[t, ROWS - 3].astype(BF16)
    one, two = (v[:, :C1] + v[:, C1:] for v in total)
    share[...] = jnp.broadcast_to(grouped(one, two), share.shape)


def edges(planes, above, below, table, inner, stats, devices):
    return pl.pallas_call(
        edges_kernel,
        out_shape=(
            shape((FRAMES, 2, 2 * Q, 2 * C1), F32),
            shape((devices, 128), F32),
            shape((FRAMES, 3, 2 * Q, 2 * C1), BF16),
            shape((FRAMES, 2, 2 * Q, 2 * C1), BF16),
        ),
        in_specs=[VMEM] * 6,
        out_specs=(VMEM,) * 4,
        scratch_shapes=[pltpu.VMEM((2, FRAMES, Q, 6 * C1), BF16)],
        compiler_params=params(48),
        cost_estimate=cost(2e9, 10e6),
        name="edges",
    )(planes, above, below, table, inner, stats)


def silu(values):
    half = 0.5 * values
    return half + half * jnp.tanh(half)


def activate(values, terms):
    mean, scale, shift = terms
    return silu((values - mean) * scale + shift)


def twice(terms):
    return tuple(jnp.concatenate([v, v], axis=1) for v in terms)


def raised(values):
    return pltpu.roll(values, Q - 1, 0)


def lowered(values):
    return pltpu.roll(values, 1, 0)


def second_kernel(
    flags, inner, outer, above, below, gathered, gain, shift, reduce, second, sums2,
    hidden, share, up, down, act, lev, raw, kernels, sem, *, members,
):
    copies = [
        pltpu.make_async_copy(second, kernels.at[pl.ds(0, 3)], sem.at[0]),
        pltpu.make_async_copy(sums2, kernels.at[pl.ds(3, 2)], sem.at[1]),
    ]
    for c in copies:
        c.start()
    first_row, last_row, first_col, last_col = (flags[i] for i in range(4))
    terms = twice(norm_terms(gathered, gain, shift, members))
    entry = lax.broadcasted_iota(jnp.int32, (Q, 1), 0)
    right = jnp.where((entry >= PAD + OWN) & (last_col == 1), 0.0, 1.0)
    outside = jnp.where((entry < PAD) & (first_col == 1), 0.0, right)
    below_in = 1.0 - last_row.astype(F32)
    above_in = 1.0 - first_row.astype(F32)

    def line(t, k, value):
        keep = right * below_in if k >= 10 else right
        a = activate(value[:Q].astype(F32), terms) * keep
        b = activate(value[Q:].astype(F32), terms) * keep
        act[t, k, 0:Q, 0 : 2 * C1] = a.astype(BF16)
        act[t, k, 0:Q, 2 * C1 :] = b[:, :C1].astype(BF16)
        act[t, k, Q:, 0 : 2 * C1] = b.astype(BF16)
        act[t, k, Q:, 2 * C1 :] = raised(a[:, :C1]).astype(BF16)

    def lines(t, carry):
        line(t, 0, above[t, 0])
        line(t, 1, above[t, 1])
        line(t, 2, outer[t, 0])
        for r in range(ROWS - 2):
            line(t, 3 + r, inner[t, r])
        line(t, 9, outer[t, 1])
        for r in range(3):
            line(t, 10 + r, below[t, r])
        value = None
        for b in range(3):
            left = jnp.concatenate([act[t, 2 * i + b] for i in range(6)], axis=0)
            part = mm(left, reduce[b * 3 * C1 : (b + 1) * 3 * C1, :])
            value = part if value is None else value + part
        for i in range(6):
            keep = outside
            if i == 0:
                keep = keep * above_in
            if i == 5:
                keep = keep * below_in
            even = value[i * 2 * Q : i * 2 * Q + Q] * keep
            odd = value[i * 2 * Q + Q : (i + 1) * 2 * Q] * keep
            e, o = even.astype(BF16), odd.astype(BF16)
            lev[t, i, 0:Q, 0:C2] = lowered(odd).astype(BF16)
            lev[t, i, 0:Q, C2 : 2 * C2] = e
            lev[t, i, 0:Q, 2 * C2 :] = o
            lev[t, i, Q:, 0:C2] = e
            lev[t, i, Q:, C2 : 2 * C2] = o
            lev[t, i, Q:, 2 * C2 :] = raised(even).astype(BF16)
        return carry

    lax.fori_loop(0, FRAMES, lines, 0)
    for c in copies:
        c.wait()
    rows = 4 * 2 * Q
    mask = own_entries(rows, C2)
    total = [jnp.zeros((1, C2), F32), jnp.zeros((1, C2), F32)]

    def frame(t):
        return jnp.concatenate([lev[t, b : b + 4].reshape(rows, 3 * C2) for b in range(3)], axis=1)

    def store(t, value):
        full = value.reshape(4, 2 * Q, C2)
        hidden[t] = full
        up[t] = full[0:3].astype(BF16)
        down[t] = full[2:4].astype(BF16)
        one, two = sums(value, mask)
        total[0] += one
        total[1] += two

    frames_conv(frame, lambda s: kernels[s], 0, store)
    share[...] = jnp.broadcast_to(grouped(*total), share.shape)


def second_level(flags, inner, outer, above, below, gathered, gain, shift, reduce, second, sums2, devices):
    return pl.pallas_call(
        functools.partial(second_kernel, members=float(devices * FRAMES * ROWS * COLS * (C1 // GROUPS))),
        out_shape=(
            shape((FRAMES, 4, 2 * Q, C2), F32),
            shape((devices, 128), F32),
            shape((FRAMES, 3, 2 * Q, C2), BF16),
            shape((FRAMES, 2, 2 * Q, C2), BF16),
        ),
        in_specs=[SMEM] + [VMEM] * 8 + [ANY] * 2,
        out_specs=(VMEM,) * 4,
        scratch_shapes=[
            pltpu.VMEM((FRAMES, 14, 2 * Q, 3 * C1), BF16),
            pltpu.VMEM((FRAMES, 6, 2 * Q, 3 * C2), BF16),
            pltpu.VMEM((8, 128), F32),
            pltpu.VMEM((5, 9 * C2, C2), BF16),
            pltpu.SemaphoreType.DMA((2,)),
        ],
        compiler_params=params(48),
        cost_estimate=cost(6e9, 12e6),
        name="second",
    )(
        flags, inner, outer, above, below, gathered,
        gain.reshape(1, C1), shift.reshape(1, C1),
        reduce.reshape(9 * C1, C2), second.reshape(3, 9 * C2, C2), sums2,
    )


def third_kernel(flags, inner, above, below, gathered, gain, shift, reduce, level, share, act, *, members):
    last_row, last_col = flags[1], flags[3]
    terms = norm_terms(gathered, gain, shift, members)
    entry = lax.broadcasted_iota(jnp.int32, (Q, 1), 0)
    right = jnp.where((entry >= PAD + OWN) & (last_col == 1), 0.0, 1.0)
    below_in = 1.0 - last_row.astype(F32)

    def line(t, k, value):
        keep = right * below_in if k >= 6 else right
        even = activate(value[:Q].astype(F32), terms) * keep
        odd = activate(value[Q:].astype(F32), terms) * keep
        act[t, k, :, 0:C2] = even.astype(BF16)
        act[t, k, :, C2 : 2 * C2] = odd.astype(BF16)
        act[t, k, :, 2 * C2 :] = raised(even).astype(BF16)

    def lines(t, carry):
        for r in range(2):
            line(t, r, above[t, r])
        for r in range(4):
            line(t, 2 + r, inner[t, r])
        for r in range(3):
            line(t, 6 + r, below[t, r])
        return carry

    lax.fori_loop(0, FRAMES, lines, 0)
    mask = own_entries(2 * Q, C3)
    total = [jnp.zeros((1, C3), F32), jnp.zeros((1, C3), F32)]
    value = None
    for b in range(3):
        left = jnp.concatenate([act[t, 2 * i + b] for t in range(FRAMES) for i in range(4)], axis=0)
        part = mm(left, reduce[b * 3 * C2 : (b + 1) * 3 * C2, :])
        value = part if value is None else value + part
    rounded = value.astype(BF16)
    level[...] = rounded.reshape(FRAMES, 4, Q, C3)
    wide = rounded.astype(F32)
    for t in range(FRAMES):
        one, two = sums(wide[(4 * t + 1) * Q : (4 * t + 3) * Q], mask)
        total[0] += one
        total[1] += two
    share[...] = jnp.broadcast_to(grouped(*total), share.shape)


def third_level(flags, inner, above, below, gathered, gain, shift, reduce, devices):
    return pl.pallas_call(
        functools.partial(third_kernel, members=float(devices * FRAMES * 4 * 2 * OWN * (C2 // GROUPS))),
        out_shape=(shape((FRAMES, 4, Q, C3), BF16), shape((devices, 128), F32)),
        in_specs=[SMEM] + [VMEM] * 7,
        out_specs=(VMEM,) * 2,
        scratch_shapes=[pltpu.VMEM((FRAMES, 10, Q, 3 * C2), BF16)],
        compiler_params=params(40),
        cost_estimate=cost(2e9, 8e6),
        name="third",
    )(flags, inner, above, below, gathered, gain.reshape(1, C2), shift.reshape(1, C2), reduce.reshape(9 * C2, C3))


def last_kernel(flags, level, gathered, gain, shift, table, result, act, *, members):
    first_row, last_row, first_col, last_col = (flags[i] for i in range(4))
    terms = norm_terms(gathered, gain, shift, members)
    entry = lax.broadcasted_iota(jnp.int32, (Q, 1), 0)
    keep_col = jnp.where((entry >= PAD + OWN) & (last_col == 1), 0.0, 1.0)
    keep_col = jnp.where((entry < PAD) & (first_col == 1), 0.0, keep_col)
    below_in = 1.0 - last_row.astype(F32)
    above_in = 1.0 - first_row.astype(F32)
    for t in range(FRAMES):
        for i in range(4):
            keep = keep_col
            if i == 0:
                keep = keep * above_in
            if i == 3:
                keep = keep * below_in
            v = activate(level[t, i].astype(F32), terms) * keep
            act[t, i, :, 0:C3] = lowered(v).astype(BF16)
            act[t, i, :, C3 : 2 * C3] = v.astype(BF16)
            act[t, i, :, 2 * C3 :] = raised(v).astype(BF16)
    value = None
    for b in range(3):
        left = jnp.concatenate([act[t, i + b] for t in range(FRAMES) for i in range(2)], axis=0)
        part = mm(left, table[b * 3 * C3 : (b + 1) * 3 * C3, :])
        value = part if value is None else value + part
    tap = lambda t, a: value[2 * Q * max(t, 0) : 2 * Q * (max(t, 0) + 1), a * OUT : (a + 1) * OUT]
    for t in range(FRAMES):
        out = tap(t - 2, 0) + tap(t - 1, 1) + tap(t, 2)
        for i in range(2):
            result[t, i] = out[i * Q + PAD : i * Q + PAD + OWN].astype(BF16)


def last_level(flags, level, gathered, gain, shift, table, devices):
    return pl.pallas_call(
        functools.partial(last_kernel, members=float(devices * FRAMES * 2 * OWN * (C3 // GROUPS))),
        out_shape=shape((FRAMES, 2, OWN, OUT), BF16),
        in_specs=[SMEM] + [VMEM] * 5,
        out_specs=VMEM,
        scratch_shapes=[pltpu.VMEM((FRAMES, 4, Q, 3 * C3), BF16)],
        compiler_params=params(32),
        cost_estimate=cost(1e9, 4e6),
        name="last",
    )(flags, level, gathered, gain.reshape(1, C3), shift.reshape(1, C3), table)


def forward(axis):
    return [(i, i + 1) for i in range(lax.axis_size(axis) - 1)]


def backward(axis):
    return [(i + 1, i) for i in range(lax.axis_size(axis) - 1)]


def from_both(last, first, axis):
    return lax.ppermute(last, axis, forward(axis)), lax.ppermute(first, axis, backward(axis))


def everywhere(share):
    return lax.all_to_all(share, AXES, 0, 0, tiled=True)


def shards(
    features, conv_first, first_reduce_kernel, conv_second, second_reduce_kernel, conv_last,
    gain_first, shift_first, gain_second, shift_second, gain_third, shift_third,
):
    rows, cols = lax.axis_size("rows"), lax.axis_size("cols")
    devices = rows * cols
    row, col = lax.axis_index("rows"), lax.axis_index("cols")
    flags = jnp.stack([row == 0, row == rows - 1, col == 0, col == cols - 1]).astype(jnp.int32)

    left, right = from_both(features[:, :, COLS - LEFT :], features[:, :, :RIGHT], "cols")
    table_one, table_two, table_three = weights(conv_first, conv_second, conv_last)
    planes, top, bottom = planes_of(left, features, right)
    above, below = from_both(bottom, top, "rows")
    inner, stats = middle(planes, table_one)
    outer, share, up, down = edges(planes, above, below, table_one, inner, stats, devices)
    above, below = from_both(down, up, "rows")
    hidden, share, up, down = second_level(
        flags, inner, outer, above, below, everywhere(share), gain_first, shift_first,
        first_reduce_kernel, conv_second, table_two, devices,
    )
    above, below = from_both(down, up, "rows")
    level, share = third_level(
        flags, hidden, above, below, everywhere(share), gain_second, shift_second,
        second_reduce_kernel, devices,
    )
    return last_level(flags, level, everywhere(share), gain_third, shift_third, table_three, devices)


def solution(mesh):
    return jax.shard_map(
        shards,
        mesh=mesh,
        in_specs=(P(None, "rows", "cols", None),) + (P(),) * 11,
        out_specs=P(None, "rows", "cols", None),
        check_vma=False,
    )
```

time: 260 us -> 139 us (0.53); the launches traced: 256 us -> 138 us
  blocking collectives: 113 us -> 38.4 us
  Pallas kernels: 0 us -> 35.2 us
  matrix products: 24.1 us -> 0 us
  local copies, waits for them, and re-layouts: 35.3 us -> 12.9 us
  other arithmetic: 19.6 us -> 0.08 us
  waiting for transfers between devices: 30.5 us -> 12.7 us
  starting transfers between devices: 32.6 us -> 38.5 us
    psum x12 -> x0, blocking collectives: 113 us -> none  [one_axis_at_a_time(): array = lax.psum(array, axis)]
    all_to_all x0 -> x2, blocking collectives: none -> 38.4 us  [everywhere(): return lax.all_to_all(share, AXES, 0, 0, tiled=True)]
    pallas_call x0 -> x7, Pallas kernels: none -> 35.2 us  [the longest x1 10.3 us: second_level(): pl.pallas_call(functools.partial(second_kernel, members=float(devices * F...]
    ppermute x12 -> x8, waiting for transfers between devices: 30.5 us -> 0.02 us  [the longest x4 0.01 us: from_both(): lax.ppermute(first, axis, backward(axis))]
    conv_general_dilated x5 -> x0, matrix products: 24.1 us -> none  [dilated(): lax.conv_general_dilated(input_video[None], weight_tables, strides, 'VALI...]
    all_to_all x0 -> x1, starting transfers between devices: none -> 15.9 us  [everywhere(): return lax.all_to_all(share, AXES, 0, 0, tiled=True)]
    all_to_all x0 -> x1, waiting for transfers between devices: none -> 12.7 us  [everywhere(): return lax.all_to_all(share, AXES, 0, 0, tiled=True)]
    conv_general_dilated x13 -> x0, local copies, waits for them, and re-layouts: 11.9 us -> none  [dilated(): lax.conv_general_dilated(input_video[None], weight_tables, strides, 'VALI...]
  transfers between devices with their start and end apart: 12 -> 9, of which waited for: 9 -> 1; matrix products, arithmetic and copies ran while one was open for 1% -> 3% of each run, Pallas kernels for 0% -> 8%
where the time goes in v1:
time: 139 us; the launch traced here: 138 us
  starting transfers between devices  38.5 us (28%)
  blocking collectives  38.4 us (28%)
  Pallas kernels  35.2 us (25%)
  local copies, waits for them, and re-layouts  12.9 us (9%)
  waiting for transfers between devices  12.7 us (9%)
    all_to_all x2, blocking collectives, everywhere(): return lax.all_to_all(share, AXES, 0, 0, tiled=True)  38.4 us
    all_to_all x1, starting transfers between devices, everywhere(): return lax.all_to_all(share, AXES, 0, 0, tiled=True)  15.9 us
    ppermute x4, starting transfers between devices, from_both(): lax.ppermute(last, axis, forward(axis))  13.6 us
    all_to_all x1, waiting for transfers between devices, everywhere(): return lax.all_to_all(share, AXES, 0, 0, tiled=True)  12.7 us
    pallas_call x1, Pallas kernels, second_level(): pl.pallas_call(functools.partial(second_kernel, members=float(devices * F...  10.3 us
    unnamed x31, local copies, waits for them, and re-layouts  9.13 us
    ppermute x4, starting transfers between devices, from_both(): lax.ppermute(first, axis, backward(axis))  9 us
    pallas_call x1, Pallas kernels, middle(): pl.pallas_call(middle_kernel, out_shape=(shape((FRAMES, ROWS - 2, 2 * Q,...  6.42 us
  transfers between devices with their start and end apart: 9, of which 1 were waited for; matrix products, arithmetic and copies ran while one was open for 3% of the time, Pallas kernels for 8%

profile of v1, /device:TPU:1, one launch (start us, length us, event | category | flops | bytes accessed | tf_op | source)
XLA Modules:
  0.0 138.1 jit_solution(6312352762275521172)
XLA Ops:
  0.0 1.6 %slice.7 = bf16[4,8,16,128]{3,2,1,0:T(8,128)(2,1)} slice(bf16[4,8,160,128]{3,2,1,0:T(8,128)(2,1)} %param.12), slice={[0:4], [0:8], [0:16], [0:128]} | slice | bytes 262144 | tf_op jit(solution)/shard_map/slice | solution.py:546
  1.6 5.1 %collective-permute-start.1 = (bf16[4,8,16,128]{3,2,1,0:T(8,128)(2,1)}, bf16[4,8,16,128]{3,2,1,0:T(8,128)(2,1)}, u32[]{:S(2)}, u32[]{:S(2)}) collective-permute-start(bf16[4,8,16,128]{3,2,1,0:T(8,128)(2,1)} %slice.7), channel_id=1, source_target_pairs={{1,0},{2,1},{3,2},{4,3},{5,4},{6,5},{7,6},{9,8},{10,9},{11,10},{12... | collective-permute-start | bytes 393224 | tf_op jit(solution)/shard_map/ppermute | solution.py:530
  6.7 1.5 %slice.6 = bf16[4,8,8,128]{3,2,1,0:T(8,128)(2,1)} slice(bf16[4,8,160,128]{3,2,1,0:T(8,128)(2,1)} %param.12), slice={[0:4], [0:8], [152:160], [0:128]} | slice | bytes 131072 | tf_op jit(solution)/shard_map/slice | solution.py:546
  8.2 1.9 %collective-permute-start = (bf16[4,8,8,128]{3,2,1,0:T(8,128)(2,1)}, bf16[4,8,8,128]{3,2,1,0:T(8,128)(2,1)}, u32[]{:S(2)}, u32[]{:S(2)}) collective-permute-start(bf16[4,8,8,128]{3,2,1,0:T(8,128)(2,1)} %slice.6), channel_id=1, source_target_pairs={{0,1},{1,2},{2,3},{3,4},{4,5},{5,6},{6,7},{8,9},{9,10},{10,11},{11... | collective-permute-start | bytes 196616 | tf_op jit(solution)/shard_map/ppermute | solution.py:530
  10.1 3.0 %copy.15 = bf16[3,3,3,512,32]{4,3,2,1,0:T(8,128)(2,1)S(1)} copy(bf16[3,3,3,512,32]{3,4,2,1,0:T(8,128)(2,1)} %param.17) | data formatting | bytes 1769472 | tf_op args[5]
  13.1 2.0 %copy-done = bf16[3,3,3,256,256]{4,3,2,1,0:T(8,128)(2,1)S(1)} copy-done((bf16[3,3,3,256,256]{4,3,2,1,0:T(8,128)(2,1)S(1)}, bf16[3,3,3,256,256]{4,3,2,1,0:T(8,128)(2,1)}, u32[]{:S(2)}) %copy-start) | copy-done | bytes 3538968
  16.3 4.0 %weights.1 = (bf16[7680,256]{1,0:T(8,128)(2,1)}, bf16[2,2304,256]{2,1,0:T(8,128)(2,1)S(1)}, bf16[4608,128]{1,0:T(8,128)(2,1)S(1)}) custom-call(bf16[3456,128]{1,0:T(8,128)(2,1)S(1)} %bitcast.34, bf16[3,2304,256]{2,1,0:T(8,128)(2,1)S(1)} %bitcast.32, bf16[3,4608,32]{2,1,0:T(8,128)(2,1)S(1)} %bitcast.30), custom_call_target="tpu_custom_call" | custom-call | bytes 12000000 | tf_op jit(solution)/shard_map/weights/pallas_call | solution.py:83
  20.3 1.4 %copy-done.5 = bf16[2,2304,256]{2,1,0:T(8,128)(2,1)} copy-done((bf16[2,2304,256]{2,1,0:T(8,128)(2,1)}, bf16[2,2304,256]{2,1,0:T(8,128)(2,1)S(1)}, u32[]{:S(2)}) %copy-start.5) | copy-done | bytes 2359320
  21.8 2.0 %planes.1 = (bf16[32,48,768]{2,1,0:T(8,128)(2,1)S(1)}, bf16[4,48,512]{2,1,0:T(8,128)(2,1)S(1)}, bf16[4,48,512]{2,1,0:T(8,128)(2,1)S(1)}) custom-call(bf16[32,8,128]{2,1,0:T(8,128)(2,1)} %bitcast.4.left, bf16[32,160,128]{2,1,0:T(8,128)(2,1)S(1)} %bitcast.33, bf16[32,16,128]{2,1,0:T(8,128)(2,1)} %bitcast.6.right), custom_call_target="tpu_custom_call" | custom-call | bytes 4000000 | tf_op jit(solution)/shard_map/planes/pallas_call | solution.py:117
  23.8 2.9 %collective-permute-start.2 = (bf16[4,48,512]{2,1,0:T(8,128)(2,1)S(1)}, bf16[4,48,512]{2,1,0:T(8,128)(2,1)S(1)}, u32[]{:S(2)}, u32[]{:S(2)}) collective-permute-start(bf16[4,48,512]{2,1,0:T(8,128)(2,1)S(1)} %get-tuple-element.26), channel_id=1, source_target_pairs={{0,8},{8,16},{16,24},{24,32},{32,40},{40,48},{48,56},{56,64},{64,7... | collective-permute-start | bytes 589832 | tf_op jit(solution)/shard_map/ppermute | solution.py:530
  26.7 1.3 collective-permute-start.3
  28.0 6.4 %middle.1 = (f32[4,6,96,256]{3,2,1,0:T(8,128)S(1)}, f32[8,256]{1,0:T(8,128)S(1)}) custom-call(bf16[32,48,768]{2,1,0:T(8,128)(2,1)S(1)} %get-tuple-element.23.planes, bf16[7680,256]{1,0:T(8,128)(2,1)} %get-tuple-element.24.table), custom_call_target="tpu_custom_call" | custom-call | flops 6000000000 | bytes 10000000 | tf_op jit(solution)/shard_map/middle/pallas_call | solution.py:182
  34.5 1.5 %copy-done.1 = f32[4,6,96,256]{3,2,1,0:T(8,128)} copy-done((f32[4,6,96,256]{3,2,1,0:T(8,128)}, f32[4,6,96,256]{3,2,1,0:T(8,128)S(1)}, u32[]{:S(2)}) %copy-start.1) | copy-done | bytes 2359320
  36.0 5.6 %edges.1 = (f32[4,2,96,256]{3,2,1,0:T(8,128)S(1)}, f32[256,128]{1,0:T(8,128)}, bf16[4,3,96,256]{3,2,1,0:T(8,128)(2,1)S(1)}, bf16[4,2,96,256]{3,2,1,0:T(8,128)(2,1)S(1)}) custom-call(bf16[32,48,768]{2,1,0:T(8,128)(2,1)S(1)} %get-tuple-element.23.planes, bf16[4,48,512]{2,1,0:T(8,128)(2,1)S(1)} %collective-permute-done.2.above, ...), custom_call_target="tpu_custom_call" | custom-call | flops 2000000000 | bytes 10000000 | tf_op jit(solution)/shard_map/edges/pallas_call | solution.py:274
  42.9 4.8 %collective-permute-start.4 = (bf16[4,2,96,256]{3,2,1,0:T(8,128)(2,1)S(1)}, bf16[4,2,96,256]{3,2,1,0:T(8,128)(2,1)S(1)}, u32[]{:S(2)}, u32[]{:S(2)}) collective-permute-start(bf16[4,2,96,256]{3,2,1,0:T(8,128)(2,1)S(1)} %get-tuple-element.30), channel_id=1, source_target_pairs={{0,8},{8,16},{16,24},{24,32},{32,40},{40,48},{48,56},{56,64},{64,7... | collective-permute-start | bytes 1179656 | tf_op jit(solution)/shard_map/ppermute | solution.py:530
  47.7 15.9 %all-to-all-start = ((f32[256,1,128]{2,1,0:T(1,128)}), f32[256,1,128]{2,1,0:T(1,128)S(1)}, u32[]{:S(2)}, u32[]{:S(2)}) async-start(f32[256,1,128]{2,1,0:T(1,128)} %bitcast.11), calls=%async_computation | async-start | bytes 262144 | tf_op jit(solution)/shard_map/all_to_all | solution.py:534
  63.7 12.7 %all-to-all-done = f32[256,1,128]{2,1,0:T(1,128)S(1)} async-done(((f32[256,1,128]{2,1,0:T(1,128)}), f32[256,1,128]{2,1,0:T(1,128)S(1)}, u32[]{:S(2)}, u32[]{:S(2)}) %all-to-all-start) | async-done | bytes 131104 | tf_op jit(solution)/shard_map/all_to_all | solution.py:534
  76.4 10.3 %second.1 = (f32[4,4,96,256]{3,2,1,0:T(8,128)S(1)}, f32[256,128]{1,0:T(8,128)S(1)}, bf16[4,3,96,256]{3,2,1,0:T(8,128)(2,1)S(1)}, bf16[4,2,96,256]{3,2,1,0:T(8,128)(2,1)S(1)}) custom-call(s32[4]{0:T(128)S(1)} %add_convert_fusion.flags, f32[4,6,96,256]{3,2,1,0:T(8,128)} %copy-done.1, f32[4,2,96,256]{3,2,1,0:T(8,128)S(1)} %get-tuple-element.29.outer, ...), custom_call_target="tpu_custom_call" | custom-call | flops 6000000000 | bytes 12000000 | tf_op jit(solution)/shard_map/second/pallas_call | solution.py:395
  86.7 1.3 collective-permute-start.7
  88.0 4.0 %collective-permute-start.6 = (bf16[4,2,96,256]{3,2,1,0:T(8,128)(2,1)S(1)}, bf16[4,2,96,256]{3,2,1,0:T(8,128)(2,1)S(1)}, u32[]{:S(2)}, u32[]{:S(2)}) collective-permute-start(bf16[4,2,96,256]{3,2,1,0:T(8,128)(2,1)S(1)} %get-tuple-element.35), channel_id=1, source_target_pairs={{0,8},{8,16},{16,24},{24,32},{32,40},{40,48},{48,56},{56,64},{64,7... | collective-permute-start | bytes 1179656 | tf_op jit(solution)/shard_map/ppermute | solution.py:530
  92.0 20.0 %all_to_all.33 = f32[256,1,128]{2,1,0:T(1,128)S(1)} all-to-all(f32[256,1,128]{2,1,0:T(1,128)S(1)} %bitcast.36), channel_id=1, replica_groups=mesh['rows'=32,'cols'=8] {'rows','cols'}, dimensions={0} | all-to-all | bytes 262144 | tf_op jit(solution)/shard_map/all_to_all | solution.py:534
  112.1 4.5 %third.1 = (bf16[4,4,48,512]{3,2,1,0:T(8,128)(2,1)S(1)}, f32[256,128]{1,0:T(8,128)S(1)}) custom-call(s32[4]{0:T(128)S(1)} %add_convert_fusion.flags, f32[4,4,96,256]{3,2,1,0:T(8,128)S(1)} %get-tuple-element.34.inner, bf16[4,2,96,256]{3,2,1,0:T(8,128)(2,1)S(1)} %collective-permute-done.6.above, bf16[4,3,96,256]{3,2,1,0:T(8,128)(2,1)S(1)} %collective-permute-done.7.below, ...), custom_call_target="tpu_custom_call" | custom-call | flops 2000000000 | bytes 8000000 | tf_op jit(solution)/shard_map/third/pallas_call | solution.py:465
  116.6 18.4 %all_to_all.34 = f32[256,1,128]{2,1,0:T(1,128)S(1)} all-to-all(f32[256,1,128]{2,1,0:T(1,128)S(1)} %bitcast.38), channel_id=1, replica_groups=mesh['rows'=32,'cols'=8] {'rows','cols'}, dimensions={0} | all-to-all | bytes 262144 | tf_op jit(solution)/shard_map/all_to_all | solution.py:534
  135.0 2.4 %last.1 = bf16[4,2,40,32]{3,2,1,0:T(8,128)(2,1)S(1)} custom-call(s32[4]{0:T(128)S(1)} %add_convert_fusion.flags, bf16[4,4,48,512]{3,2,1,0:T(8,128)(2,1)S(1)} %get-tuple-element.38.level, f32[256,128]{1,0:T(8,128)S(1)} %bitcast.39, f32[1,512]{1,0:T(1,128)S(1)} %bitcast.42, f32[1,512]{1,0:T(1,128)S(1)} %bitcast.43, bf16[4608,128]{1,0:T(8,128)(2,1)S(1)} %copy-done.7), custom_call_target="tpu_custom_call" | custom-call | flops 1000000000 | bytes 4000000 | tf_op jit(solution)/shard_map/last/pallas_call | solution.py:509
  (38 shorter events, 3.3 us)
Async XLA Ops:
  1.6 20.2 %collective-permute-start.1 = (bf16[4,8,16,128]{3,2,1,0:T(8,128)(2,1)}, bf16[4,8,16,128]{3,2,1,0:T(8,128)(2,1)}, u32[]{:S(2)}, u32[]{:S(2)}) collective-permute-start(bf16[4,8,16,128]{3,2,1,0:T(8,128)(2,1)} %slice.7), channel_id=1, source_target_pairs={{1,0},{2,1},{3,2},{4,3},{5,4},{6,5},{7,6},{9,8},{10,9},{11,10},{12... | collective-permute-start | bytes 393224 | tf_op jit(solution)/shard_map/ppermute | solution.py:530
  8.2 13.6 %collective-permute-start = (bf16[4,8,8,128]{3,2,1,0:T(8,128)(2,1)}, bf16[4,8,8,128]{3,2,1,0:T(8,128)(2,1)}, u32[]{:S(2)}, u32[]{:S(2)}) collective-permute-start(bf16[4,8,8,128]{3,2,1,0:T(8,128)(2,1)} %slice.6), channel_id=1, source_target_pairs={{0,1},{1,2},{2,3},{3,4},{4,5},{5,6},{6,7},{8,9},{9,10},{10,11},{11... | collective-permute-start | bytes 196616 | tf_op jit(solution)/shard_map/ppermute | solution.py:530
  13.1 2.0 %copy-start = (bf16[3,3,3,256,256]{4,3,2,1,0:T(8,128)(2,1)S(1)}, bf16[3,3,3,256,256]{4,3,2,1,0:T(8,128)(2,1)}, u32[]{:S(2)}) copy-start(bf16[3,3,3,256,256]{4,3,2,1,0:T(8,128)(2,1)} %param.15) | copy-start | bytes 10616836
  15.1 1.2 copy-start.3
  16.3 5.5 %copy-start.2 = (bf16[4,8,160,128]{3,2,1,0:T(8,128)(2,1)S(1)}, bf16[4,8,160,128]{3,2,1,0:T(8,128)(2,1)}, u32[]{:S(2)}) copy-start(bf16[4,8,160,128]{3,2,1,0:T(8,128)(2,1)} %param.12) | copy-start | bytes 3932164
  20.3 1.4 %copy-start.5 = (bf16[2,2304,256]{2,1,0:T(8,128)(2,1)}, bf16[2,2304,256]{2,1,0:T(8,128)(2,1)S(1)}, u32[]{:S(2)}) copy-start(bf16[2,2304,256]{2,1,0:T(8,128)(2,1)S(1)} %get-tuple-element.33.sums2) | copy-start | bytes 7077892
  21.8 6.2 %copy-start.6 = (bf16[4608,128]{1,0:T(8,128)(2,1)}, bf16[4608,128]{1,0:T(8,128)(2,1)S(1)}, u32[]{:S(2)}) copy-start(bf16[4608,128]{1,0:T(8,128)(2,1)S(1)} %get-tuple-element.40.table) | copy-start | bytes 3538948
  23.8 12.1 %collective-permute-start.2 = (bf16[4,48,512]{2,1,0:T(8,128)(2,1)S(1)}, bf16[4,48,512]{2,1,0:T(8,128)(2,1)S(1)}, u32[]{:S(2)}, u32[]{:S(2)}) collective-permute-start(bf16[4,48,512]{2,1,0:T(8,128)(2,1)S(1)} %get-tuple-element.26), channel_id=1, source_target_pairs={{0,8},{8,16},{16,24},{24,32},{32,40},{40,48},{48,56},{56,64},{64,7... | collective-permute-start | bytes 589832 | tf_op jit(solution)/shard_map/ppermute | solution.py:530
  26.7 9.2 %collective-permute-start.3 = (bf16[4,48,512]{2,1,0:T(8,128)(2,1)S(1)}, bf16[4,48,512]{2,1,0:T(8,128)(2,1)S(1)}, u32[]{:S(2)}, u32[]{:S(2)}) collective-permute-start(bf16[4,48,512]{2,1,0:T(8,128)(2,1)S(1)} %get-tuple-element.27), channel_id=1, source_target_pairs={{8,0},{16,8},{24,16},{32,24},{40,32},{48,40},{56,48},{64,56},{72,6... | collective-permute-start | bytes 589832 | tf_op jit(solution)/shard_map/ppermute | solution.py:530
  34.5 1.5 %copy-start.1 = (f32[4,6,96,256]{3,2,1,0:T(8,128)}, f32[4,6,96,256]{3,2,1,0:T(8,128)S(1)}, u32[]{:S(2)}) copy-start(f32[4,6,96,256]{3,2,1,0:T(8,128)S(1)} %get-tuple-element.25.inner) | copy-start | bytes 7077892
  35.9 40.4 %copy-start.8 = (bf16[3,3,128,256]{3,2,1,0:T(8,128)(2,1)S(1)}, bf16[3,3,128,256]{3,2,1,0:T(8,128)(2,1)}, u32[]{:S(2)}) copy-start(bf16[3,3,128,256]{3,2,1,0:T(8,128)(2,1)} %param.14) | copy-start | bytes 1769476
  35.9 40.4 %copy-start.13 = (f32[128]{0:T(128)S(1)}, f32[128]{0:T(128)}, u32[]{:S(2)}) copy-start(f32[128]{0:T(128)} %param.18) | copy-start | bytes 1540
  36.0 40.4 %copy-start.14 = (f32[128]{0:T(128)S(1)}, f32[128]{0:T(128)}, u32[]{:S(2)}) copy-start(f32[128]{0:T(128)} %param.19) | copy-start | bytes 1540
  41.6 34.8 %collective-permute-start.5 = (bf16[4,3,96,256]{3,2,1,0:T(8,128)(2,1)S(1)}, bf16[4,3,96,256]{3,2,1,0:T(8,128)(2,1)S(1)}, u32[]{:S(2)}, u32[]{:S(2)}) collective-permute-start(bf16[4,3,96,256]{3,2,1,0:T(8,128)(2,1)S(1)} %get-tuple-element.31), channel_id=1, source_target_pairs={{8,0},{16,8},{24,16},{32,24},{40,32},{48,40},{56,48},{64,56},{72,6... | collective-permute-start | bytes 1769480 | tf_op jit(solution)/shard_map/ppermute | solution.py:530
  42.9 33.5 %collective-permute-start.4 = (bf16[4,2,96,256]{3,2,1,0:T(8,128)(2,1)S(1)}, bf16[4,2,96,256]{3,2,1,0:T(8,128)(2,1)S(1)}, u32[]{:S(2)}, u32[]{:S(2)}) collective-permute-start(bf16[4,2,96,256]{3,2,1,0:T(8,128)(2,1)S(1)} %get-tuple-element.30), channel_id=1, source_target_pairs={{0,8},{8,16},{16,24},{24,32},{32,40},{40,48},{48,56},{56,64},{64,7... | collective-permute-start | bytes 1179656 | tf_op jit(solution)/shard_map/ppermute | solution.py:530
  47.7 28.7 %all-to-all-start = ((f32[256,1,128]{2,1,0:T(1,128)}), f32[256,1,128]{2,1,0:T(1,128)S(1)}, u32[]{:S(2)}, u32[]{:S(2)}) async-start(f32[256,1,128]{2,1,0:T(1,128)} %bitcast.11), calls=%async_computation | async-start | bytes 262144 | tf_op jit(solution)/shard_map/all_to_all | solution.py:534
  76.4 35.7 %copy-start.4 = (bf16[3,3,256,512]{3,2,1,0:T(8,128)(2,1)S(1)}, bf16[3,3,256,512]{3,2,1,0:T(8,128)(2,1)}, u32[]{:S(2)}) copy-start(bf16[3,3,256,512]{3,2,1,0:T(8,128)(2,1)} %param.16) | copy-start | bytes 7077892
  76.4 35.6 %copy-start.11 = (f32[256]{0:T(256)S(1)}, f32[256]{0:T(256)}, u32[]{:S(2)}) copy-start(f32[256]{0:T(256)} %param.20) | copy-start | bytes 3076
  76.4 35.6 %copy-start.12 = (f32[256]{0:T(256)S(1)}, f32[256]{0:T(256)}, u32[]{:S(2)}) copy-start(f32[256]{0:T(256)} %param.21) | copy-start | bytes 3076
  86.7 25.3 %collective-permute-start.7 = (bf16[4,3,96,256]{3,2,1,0:T(8,128)(2,1)S(1)}, bf16[4,3,96,256]{3,2,1,0:T(8,128)(2,1)S(1)}, u32[]{:S(2)}, u32[]{:S(2)}) collective-permute-start(bf16[4,3,96,256]{3,2,1,0:T(8,128)(2,1)S(1)} %get-tuple-element.36), channel_id=1, source_target_pairs={{8,0},{16,8},{24,16},{32,24},{40,32},{48,40},{56,48},{64,56},{72,6... | collective-permute-start | bytes 1769480 | tf_op jit(solution)/shard_map/ppermute | solution.py:530
  88.0 24.0 %collective-permute-start.6 = (bf16[4,2,96,256]{3,2,1,0:T(8,128)(2,1)S(1)}, bf16[4,2,96,256]{3,2,1,0:T(8,128)(2,1)S(1)}, u32[]{:S(2)}, u32[]{:S(2)}) collective-permute-start(bf16[4,2,96,256]{3,2,1,0:T(8,128)(2,1)S(1)} %get-tuple-element.35), channel_id=1, source_target_pairs={{0,8},{8,16},{16,24},{24,32},{32,40},{40,48},{48,56},{56,64},{64,7... | collective-permute-start | bytes 1179656 | tf_op jit(solution)/shard_map/ppermute | solution.py:530
  112.1 22.9 %copy-start.7 = (bf16[4608,128]{1,0:T(8,128)(2,1)S(1)}, bf16[4608,128]{1,0:T(8,128)(2,1)}, u32[]{:S(2)}) copy-start(bf16[4608,128]{1,0:T(8,128)(2,1)} %copy-done.6) | copy-start | bytes 3538948
  112.1 22.9 %copy-start.9 = (f32[512]{0:T(512)S(1)}, f32[512]{0:T(512)}, u32[]{:S(2)}) copy-start(f32[512]{0:T(512)} %param.22) | copy-start | bytes 6148
  112.1 22.9 %copy-start.10 = (f32[512]{0:T(512)S(1)}, f32[512]{0:T(512)}, u32[]{:S(2)}) copy-start(f32[512]{0:T(512)} %param.23) | copy-start | bytes 6148

commit v2 on v1

v2 whole, which is shorter than its diff:
```python
import functools

import jax
import jax.numpy as jnp
from jax import lax
from jax.experimental import pallas as pl
from jax.experimental.pallas import tpu as pltpu
from jax.sharding import PartitionSpec as P

GROUPS = 32
EPSILON = 1e-6
FRAMES = 4
ROWS = 8
COLS = 160
C1, C2, C3, OUT = 128, 256, 512, 32
Q = 48
PAD = 2
OWN = COLS // 4
EDGE = 16
LINE = 208
AXES = ("rows", "cols")
F32, BF16 = jnp.float32, jnp.bfloat16
VMEM = pl.BlockSpec(memory_space=pltpu.VMEM)
HBM = pl.BlockSpec(memory_space=pltpu.HBM)


def params(mib):
    return pltpu.CompilerParams(vmem_limit_bytes=mib * 1024 * 1024)


def cost(flops, read):
    return pl.CostEstimate(flops=int(flops), bytes_accessed=int(read), transcendentals=0)


def shape(dims, dtype):
    return jax.ShapeDtypeStruct(dims, dtype)


def mm(left, right):
    return jnp.dot(left, right, preferred_element_type=F32)


def exact(left, right):
    return jnp.dot(left, right, preferred_element_type=F32, precision=lax.Precision.HIGHEST)


def weights_kernel(first, one):
    zero = jnp.zeros((C1, C1), BF16)
    for b in range(3):
        for e in range(3):
            taps = [first[((a * 3 + b) * 3 + e) * C1 : ((a * 3 + b) * 3 + e + 1) * C1, :] for a in range(3)]
            wide = [k.astype(F32) for k in taps]
            pair = wide[0] + wide[1]
            for s, k in enumerate(taps + [pair.astype(BF16), (pair + wide[2]).astype(BF16)]):
                base = s * 12 * C1 + b * 4 * C1
                one[base + e * C1 : base + (e + 1) * C1, 0:C1] = k
                one[base + (e + 1) * C1 : base + (e + 2) * C1, C1 : 2 * C1] = k
        for s in range(5):
            base = s * 12 * C1 + b * 4 * C1
            one[base + 3 * C1 : base + 4 * C1, 0:C1] = zero
            one[base : base + C1, C1 : 2 * C1] = zero


def weights(first):
    return pl.pallas_call(
        weights_kernel,
        out_shape=shape((5 * 12 * C1, 2 * C1), BF16),
        in_specs=[VMEM],
        out_specs=VMEM,
        compiler_params=params(8),
        cost_estimate=cost(0, 5e6),
        name="weights",
    )(first.reshape(27 * C1, C1))


def cut_kernel(features, last, first, sem):
    copies = [
        pltpu.make_async_copy(features.at[:, pl.ds(COLS - EDGE, EDGE)], last, sem.at[0]),
        pltpu.make_async_copy(features.at[:, pl.ds(0, EDGE)], first, sem.at[1]),
    ]
    for c in copies:
        c.start()
    for c in copies:
        c.wait()


def cut(features):
    edge = shape((FRAMES * ROWS, EDGE, C1), BF16)
    return pl.pallas_call(
        cut_kernel,
        out_shape=(edge, edge),
        in_specs=[HBM],
        out_specs=(VMEM,) * 2,
        scratch_shapes=[pltpu.SemaphoreType.DMA((2,))],
        compiler_params=params(4),
        cost_estimate=cost(0, 4e5),
        name="cut",
    )(features.reshape(FRAMES * ROWS, COLS, C1))


def planes_kernel(left, own, right, planes, top, bottom, line):
    for t in range(FRAMES):
        planes[t, 0] = jnp.zeros((Q, 6 * C1), BF16)
        planes[t, ROWS + 1] = jnp.zeros((Q, 6 * C1), BF16)

        def step(r, carry, t=t):
            i = t * ROWS + r
            line[i, 0:EDGE, :] = left[i].astype(F32)
            line[i, EDGE : EDGE + COLS, :] = own[i].astype(F32)
            line[i, EDGE + COLS : 2 * EDGE + COLS, :] = right[i].astype(F32)
            line[i, 2 * EDGE + COLS : LINE, :] = jnp.zeros((LINE - 2 * EDGE - COLS, C1), F32)
            for k in range(6):
                planes[t, 1 + r, :, k * C1 : (k + 1) * C1] = line[i, pl.ds(7 + k, Q, stride=4), :].astype(BF16)
            return carry

        lax.fori_loop(0, ROWS, step, 0, unroll=True)
        top[t] = planes[t, 1, :, C1 : 5 * C1]
        bottom[t] = planes[t, ROWS, :, C1 : 5 * C1]


def planes_of(left, own, right):
    lines = FRAMES * ROWS
    return pl.pallas_call(
        planes_kernel,
        out_shape=(
            shape((FRAMES, ROWS + 2, Q, 6 * C1), BF16),
            shape((FRAMES, Q, 4 * C1), BF16),
            shape((FRAMES, Q, 4 * C1), BF16),
        ),
        in_specs=[VMEM] * 3,
        out_specs=(VMEM,) * 3,
        scratch_shapes=[pltpu.VMEM((lines, LINE, C1), F32)],
        compiler_params=params(12),
        cost_estimate=cost(0, 4e6),
        name="planes",
    )(left, own.reshape(lines, COLS, C1), right)


def own_entries(rows, lanes):
    at = lax.rem(lax.broadcasted_iota(jnp.int32, (rows, lanes), 0), Q)
    return (at >= PAD) & (at < PAD + OWN)


def sums(values, mask):
    kept = jnp.where(mask, values, 0.0)
    return jnp.sum(kept, axis=0, keepdims=True), jnp.sum(kept * kept, axis=0, keepdims=True)


def frames_conv(frame, weight, store):
    store(0, mm(frame(0), weight(4)))
    store(1, mm(frame(0), weight(3)) + mm(frame(1), weight(2)))
    for t in range(2, FRAMES):
        store(t, mm(frame(t - 2), weight(0)) + mm(frame(t - 1), weight(1)) + mm(frame(t), weight(2)))


def table_of(ref, rows):
    return lambda s: ref[s * rows : (s + 1) * rows, :]


def middle_kernel(planes, table, hidden, stats):
    rows = ROWS * Q
    mask = own_entries(2 * (rows - 2 * Q), 2 * C1)
    stats[...] = jnp.zeros(stats.shape, F32)

    def frame(t):
        parts = []
        for b in range(3):
            block = planes[t, b : b + ROWS].reshape(rows, 6 * C1)
            parts.append(jnp.concatenate([block[:, : 4 * C1], block[:, 2 * C1 :]], axis=0))
        return jnp.concatenate(parts, axis=1)

    def store(t, value):
        hidden[t, :, 0:Q, :] = value[:rows].reshape(ROWS, Q, 2 * C1)
        hidden[t, :, Q : 2 * Q, :] = value[rows:].reshape(ROWS, Q, 2 * C1)
        inside = jnp.concatenate([value[Q : rows - Q], value[rows + Q : 2 * rows - Q]], axis=0)
        one, two = sums(inside, mask)
        stats[0:1, :] += one
        stats[1:2, :] += two

    frames_conv(frame, table_of(table, 12 * C1), store)


def middle(planes, table):
    return pl.pallas_call(
        middle_kernel,
        out_shape=(
            shape((FRAMES, ROWS, 2 * Q, 2 * C1), F32),
            shape((8, 2 * C1), F32),
        ),
        in_specs=[VMEM] * 2,
        out_specs=(VMEM,) * 2,
        compiler_params=params(12),
        cost_estimate=cost(6e9, 10e6),
        name="middle",
    )(planes, table)


def group_matrix(channels, shift):
    per = channels // GROUPS
    c = lax.broadcasted_iota(jnp.int32, (channels, 128), 0)
    g = lax.broadcasted_iota(jnp.int32, (channels, 128), 1)
    low = (g - shift) * per
    return jnp.where((c >= low) & (c < low + per), 1.0, 0.0).astype(F32)


def spread_matrix(channels, shift):
    per = channels // GROUPS
    g = lax.broadcasted_iota(jnp.int32, (128, channels), 0)
    c = lax.broadcasted_iota(jnp.int32, (128, channels), 1)
    low = (g - shift) * per
    return jnp.where((c >= low) & (c < low + per), 1.0, 0.0).astype(F32)


def grouped(one, two):
    channels = one.shape[1]
    wide = lambda v: jnp.broadcast_to(v, (8, channels))
    row = exact(wide(one), group_matrix(channels, 0)) + exact(wide(two), group_matrix(channels, GROUPS))
    return row[0:1]


def norm_terms(gathered, gain, shift, members):
    channels = gain.shape[1]
    total = jnp.broadcast_to(jnp.sum(gathered[...], axis=0, keepdims=True), (8, 128))
    mean = exact(total, spread_matrix(channels, 0))[0:1] / members
    square = exact(total, spread_matrix(channels, GROUPS))[0:1] / members
    variance = jnp.maximum(square - mean * mean, 0.0)
    factor = gain[...] / jnp.sqrt(variance + EPSILON)
    return 0.5 * factor, 0.5 * (shift[...] - mean * factor)


def edges_kernel(above, below, table, inner, stats, hidden, share, up, down):
    mask = own_entries(2 * Q, 2 * C1)
    total = [stats[0:1, :], stats[1:2, :]]
    for side, (ref, b) in enumerate(((above, 0), (below, 2))):
        lines = []
        for t in range(FRAMES):
            whole = ref[t]
            first = pltpu.roll(whole[:, 3 * C1 :].astype(F32), 1, 0).astype(BF16)
            last = pltpu.roll(whole[:, :C1].astype(F32), Q - 1, 0).astype(BF16)
            even = jnp.concatenate([first, whole[:, : 3 * C1]], axis=1)
            odd = jnp.concatenate([whole[:, C1:], last], axis=1)
            lines.append(jnp.concatenate([even, odd], axis=0))

        def part(s, frames):
            base = s * 12 * C1 + b * 4 * C1
            value = mm(jnp.concatenate([lines[t] for t in frames], axis=0), table[base : base + 4 * C1, :])
            return [value[i * 2 * Q : (i + 1) * 2 * Q] for i in range(len(frames))]

        zero, one, two = part(0, (0, 1)), part(1, (1, 2)), part(2, (1, 2, 3))
        pair, all_three = part(3, (0,)), part(4, (0,))
        extra = [all_three[0], pair[0] + two[0], zero[0] + one[0] + two[1], zero[1] + one[1] + two[2]]
        for t in range(FRAMES):
            value = inner[t, side * (ROWS - 1)] + extra[t]
            hidden[t, side] = value
            if side == 0:
                up[t, 0] = value.astype(BF16)
            else:
                down[t, 1] = value.astype(BF16)
            first, second = sums(value, mask)
            total[0] += first
            total[1] += second
    for t in range(FRAMES):
        up[t, 1] = inner[t, 1].astype(BF16)
        up[t, 2] = inner[t, 2].astype(BF16)
        down[t, 0] = inner[t, ROWS - 2].astype(BF16)
    one, two = (v[:, :C1] + v[:, C1:] for v in total)
    share[...] = jnp.broadcast_to(grouped(one, two), share.shape)


def edges(above, below, table, inner, stats, devices):
    return pl.pallas_call(
        edges_kernel,
        out_shape=(
            shape((FRAMES, 2, 2 * Q, 2 * C1), F32),
            shape((devices, 128), F32),
            shape((FRAMES, 3, 2 * Q, 2 * C1), BF16),
            shape((FRAMES, 2, 2 * Q, 2 * C1), BF16),
        ),
        in_specs=[VMEM] * 5,
        out_specs=(VMEM,) * 4,
        compiler_params=params(12),
        cost_estimate=cost(2e9, 10e6),
        name="edges",
    )(above, below, table, inner, stats)


def position():
    row, col = lax.axis_index("rows"), lax.axis_index("cols")
    return row == 0, row == lax.axis_size("rows") - 1, col == 0, col == lax.axis_size("cols") - 1


def kept(entry_out, edge):
    return 1.0 - jnp.where(entry_out, edge.astype(F32), 0.0)


def activate(values, terms):
    half = values * terms[0] + terms[1]
    return half + half * jnp.tanh(half)


def twice(terms):
    return tuple(jnp.concatenate([v, v], axis=1) for v in terms)


def raised(values):
    return pltpu.roll(values, Q - 1, 0)


def lowered(values):
    return pltpu.roll(values, 1, 0)


def second_kernel(
    inner, outer, above, below, gathered, gain, shift, reduce, second,
    hidden, share, up, down, act, lev, summed, *, members,
):
    first_row, last_row, first_col, last_col = position()
    terms = twice(norm_terms(gathered, gain, shift, members))
    entry = lax.broadcasted_iota(jnp.int32, (Q, 1), 0)
    right = kept(entry >= PAD + OWN, last_col)
    outside = right * kept(entry < PAD, first_col)
    below_in = 1.0 - last_row.astype(F32)
    above_in = 1.0 - first_row.astype(F32)

    def line(t, k, value):
        keep = right * below_in if k >= 10 else right
        a = activate(value[:Q].astype(F32), terms) * keep
        b = activate(value[Q:].astype(F32), terms) * keep
        act[t, k, 0:Q, 0 : 2 * C1] = a.astype(BF16)
        act[t, k, 0:Q, 2 * C1 :] = b[:, :C1].astype(BF16)
        act[t, k, Q:, 0 : 2 * C1] = b.astype(BF16)
        act[t, k, Q:, 2 * C1 :] = raised(a[:, :C1]).astype(BF16)

    def lines(t, carry):
        line(t, 0, above[t, 0])
        line(t, 1, above[t, 1])
        line(t, 2, outer[t, 0])
        for r in range(1, ROWS - 1):
            line(t, 2 + r, inner[t, r])
        line(t, 9, outer[t, 1])
        for r in range(3):
            line(t, 10 + r, below[t, r])
        value = None
        for b in range(3):
            left = jnp.concatenate([act[t, 2 * i + b] for i in range(6)], axis=0)
            part = mm(left, reduce[b * 3 * C1 : (b + 1) * 3 * C1, :])
            value = part if value is None else value + part
        for i in range(6):
            keep = outside
            if i == 0:
                keep = keep * above_in
            if i == 5:
                keep = keep * below_in
            even = value[i * 2 * Q : i * 2 * Q + Q] * keep
            odd = value[i * 2 * Q + Q : (i + 1) * 2 * Q] * keep
            e, o = even.astype(BF16), odd.astype(BF16)
            lev[t, i, 0:Q, 0:C2] = lowered(odd).astype(BF16)
            lev[t, i, 0:Q, C2 : 2 * C2] = e
            lev[t, i, 0:Q, 2 * C2 :] = o
            lev[t, i, Q:, 0:C2] = e
            lev[t, i, Q:, C2 : 2 * C2] = o
            lev[t, i, Q:, 2 * C2 :] = raised(even).astype(BF16)
        return carry

    lax.fori_loop(0, FRAMES, lines, 0)

    def add(i, carry):
        at = pl.ds(pl.multiple_of(i * C2, C2), C2)
        pair = second[0, at, :].astype(F32) + second[1, at, :].astype(F32)
        summed[0, at, :] = pair.astype(BF16)
        summed[1, at, :] = (pair + second[2, at, :].astype(F32)).astype(BF16)
        return carry

    lax.fori_loop(0, 9, add, 0)
    rows = 4 * 2 * Q
    mask = own_entries(rows, C2)
    total = [jnp.zeros((1, C2), F32), jnp.zeros((1, C2), F32)]

    def frame(t):
        return jnp.concatenate([lev[t, b : b + 4].reshape(rows, 3 * C2) for b in range(3)], axis=1)

    def store(t, value):
        full = value.reshape(4, 2 * Q, C2)
        hidden[t] = full
        up[t] = full[0:3].astype(BF16)
        down[t] = full[2:4].astype(BF16)
        one, two = sums(value, mask)
        total[0] += one
        total[1] += two

    frames_conv(frame, lambda s: second[s] if s < 3 else summed[s - 3], store)
    share[...] = jnp.broadcast_to(grouped(*total), share.shape)


def second_level(inner, outer, above, below, gathered, gain, shift, reduce, second, devices):
    return pl.pallas_call(
        functools.partial(second_kernel, members=float(devices * FRAMES * ROWS * COLS * (C1 // GROUPS))),
        out_shape=(
            shape((FRAMES, 4, 2 * Q, C2), F32),
            shape((devices, 128), F32),
            shape((FRAMES, 3, 2 * Q, C2), BF16),
            shape((FRAMES, 2, 2 * Q, C2), BF16),
        ),
        in_specs=[VMEM] * 9,
        out_specs=(VMEM,) * 4,
        scratch_shapes=[
            pltpu.VMEM((FRAMES, 14, 2 * Q, 3 * C1), BF16),
            pltpu.VMEM((FRAMES, 6, 2 * Q, 3 * C2), BF16),
            pltpu.VMEM((2, 9 * C2, C2), BF16),
        ],
        compiler_params=params(20),
        cost_estimate=cost(6e9, 12e6),
        name="second",
    )(
        inner, outer, above, below, gathered,
        gain.reshape(1, C1), shift.reshape(1, C1),
        reduce.reshape(9 * C1, C2), second.reshape(3, 9 * C2, C2),
    )


def third_kernel(inner, above, below, gathered, gain, shift, reduce, level, share, act, *, members):
    _, last_row, _, last_col = position()
    terms = norm_terms(gathered, gain, shift, members)
    entry = lax.broadcasted_iota(jnp.int32, (Q, 1), 0)
    right = kept(entry >= PAD + OWN, last_col)
    below_in = 1.0 - last_row.astype(F32)

    def line(t, k, value):
        keep = right * below_in if k >= 6 else right
        even = activate(value[:Q].astype(F32), terms) * keep
        odd = activate(value[Q:].astype(F32), terms) * keep
        act[t, k, :, 0:C2] = even.astype(BF16)
        act[t, k, :, C2 : 2 * C2] = odd.astype(BF16)
        act[t, k, :, 2 * C2 :] = raised(even).astype(BF16)

    def lines(t, carry):
        for r in range(2):
            line(t, r, above[t, r])
        for r in range(4):
            line(t, 2 + r, inner[t, r])
        for r in range(3):
            line(t, 6 + r, below[t, r])
        return carry

    lax.fori_loop(0, FRAMES, lines, 0)
    mask = own_entries(2 * Q, C3)
    total = [jnp.zeros((1, C3), F32), jnp.zeros((1, C3), F32)]
    value = None
    for b in range(3):
        left = jnp.concatenate([act[t, 2 * i + b] for t in range(FRAMES) for i in range(4)], axis=0)
        part = mm(left, reduce[b * 3 * C2 : (b + 1) * 3 * C2, :])
        value = part if value is None else value + part
    rounded = value.astype(BF16)
    level[...] = rounded.reshape(FRAMES, 4, Q, C3)
    wide = rounded.astype(F32)
    for t in range(FRAMES):
        one, two = sums(wide[(4 * t + 1) * Q : (4 * t + 3) * Q], mask)
        total[0] += one
        total[1] += two
    share[...] = jnp.broadcast_to(grouped(*total), share.shape)


def third_level(inner, above, below, gathered, gain, shift, reduce, devices):
    return pl.pallas_call(
        functools.partial(third_kernel, members=float(devices * FRAMES * 4 * 2 * OWN * (C2 // GROUPS))),
        out_shape=(shape((FRAMES, 4, Q, C3), BF16), shape((devices, 128), F32)),
        in_specs=[VMEM] * 7,
        out_specs=(VMEM,) * 2,
        scratch_shapes=[pltpu.VMEM((FRAMES, 10, Q, 3 * C2), BF16)],
        compiler_params=params(12),
        cost_estimate=cost(2e9, 8e6),
        name="third",
    )(inner, above, below, gathered, gain.reshape(1, C2), shift.reshape(1, C2), reduce.reshape(9 * C2, C3))


def last_kernel(level, gathered, gain, shift, table, result, act, *, members):
    first_row, last_row, first_col, last_col = position()
    terms = norm_terms(gathered, gain, shift, members)
    entry = lax.broadcasted_iota(jnp.int32, (Q, 1), 0)
    outside = kept(entry >= PAD + OWN, last_col) * kept(entry < PAD, first_col)
    below_in = 1.0 - last_row.astype(F32)
    above_in = 1.0 - first_row.astype(F32)
    for t in range(FRAMES):
        for i in range(4):
            keep = outside
            if i == 0:
                keep = keep * above_in
            if i == 3:
                keep = keep * below_in
            v = activate(level[t, i].astype(F32), terms) * keep
            act[t, i, :, 0:C3] = lowered(v).astype(BF16)
            act[t, i, :, C3 : 2 * C3] = v.astype(BF16)
            act[t, i, :, 2 * C3 :] = raised(v).astype(BF16)
    value = None
    for b in range(3):
        for e in range(3):
            lanes = slice(e * C3, (e + 1) * C3)
            left = jnp.concatenate([act[t, i + b, :, lanes] for t in range(FRAMES) for i in range(2)], axis=0)
            right = jnp.concatenate([table[a, 3 * b + e] for a in range(3)], axis=0)
            part = lax.dot_general(left, right, (((1,), (1,)), ((), ())), preferred_element_type=F32)
            value = part if value is None else value + part

    def tap(t, a):
        at = 2 * Q * max(t, 0)
        return value[at : at + 2 * Q, a * OUT : (a + 1) * OUT]

    side = jnp.concatenate([tap(t - 2, 0) + tap(t - 1, 1) + tap(t, 2) for t in range(FRAMES)], axis=1).T
    for t in range(FRAMES):
        for i in range(2):
            at = i * Q + PAD
            result[t, i] = side[t * OUT : (t + 1) * OUT, at : at + OWN].astype(BF16)


def last_level(level, gathered, gain, shift, table, devices):
    swapped = jnp.swapaxes(table, 3, 4).reshape(3, 9, OUT, C3)
    out = pl.pallas_call(
        functools.partial(last_kernel, members=float(devices * FRAMES * 2 * OWN * (C3 // GROUPS))),
        out_shape=shape((FRAMES, 2, OUT, OWN), BF16),
        in_specs=[VMEM] * 5,
        out_specs=VMEM,
        scratch_shapes=[pltpu.VMEM((FRAMES, 4, Q, 3 * C3), BF16)],
        compiler_params=params(10),
        cost_estimate=cost(1e9, 4e6),
        name="last",
    )(level, gathered, gain.reshape(1, C3), shift.reshape(1, C3), swapped)
    return jnp.swapaxes(out, 2, 3)


def forward(axis):
    return [(i, i + 1) for i in range(lax.axis_size(axis) - 1)]


def backward(axis):
    return [(i + 1, i) for i in range(lax.axis_size(axis) - 1)]


def from_both(last, first, axis):
    return lax.ppermute(last, axis, forward(axis)), lax.ppermute(first, axis, backward(axis))


def everywhere(share):
    return lax.all_to_all(share, AXES, 0, 0, tiled=True)


def shards(
    features, conv_first, first_reduce_kernel, conv_second, second_reduce_kernel, conv_last,
    gain_first, shift_first, gain_second, shift_second, gain_third, shift_third,
):
    devices = lax.axis_size("rows") * lax.axis_size("cols")
    left, right = from_both(*cut(features), "cols")
    table = weights(conv_first)
    planes, top, bottom = planes_of(left, features, right)
    above, below = from_both(bottom, top, "rows")
    inner, stats = middle(planes, table)
    outer, share, up, down = edges(above, below, table, inner, stats, devices)
    above, below = from_both(down, up, "rows")
    hidden, share, up, down = second_level(
        inner, outer, above, below, everywhere(share), gain_first, shift_first,
        first_reduce_kernel, conv_second, devices,
    )
    above, below = from_both(down, up, "rows")
    level, share = third_level(
        hidden, above, below, everywhere(share), gain_second, shift_second,
        second_reduce_kernel, devices,
    )
    return last_level(level, everywhere(share), gain_third, shift_third, conv_last, devices)


def solution(mesh):
    return jax.shard_map(
        shards,
        mesh=mesh,
        in_specs=(P(None, "rows", "cols", None),) + (P(),) * 11,
        out_specs=P(None, "rows", "cols", None),
        check_vma=False,
    )
```

time: 139 us -> 119 us (0.86)
  blocking collectives: 38.4 us -> 67.4 us
  starting transfers between devices: 38.5 us -> 23 us
  Pallas kernels: 35.2 us -> 22.6 us
  local copies, waits for them, and re-layouts: 12.9 us -> 2.55 us
  waiting for transfers between devices: 12.7 us -> 2.6 us
    all_to_all x2 -> x3, blocking collectives: 38.4 us -> 67.4 us  [everywhere(): return lax.all_to_all(share, AXES, 0, 0, tiled=True)]
    all_to_all x1 -> x0, starting transfers between devices: 15.9 us -> none  [everywhere(): return lax.all_to_all(share, AXES, 0, 0, tiled=True)]
    all_to_all x1 -> x0, waiting for transfers between devices: 12.7 us -> none  [everywhere(): return lax.all_to_all(share, AXES, 0, 0, tiled=True)]
    unnamed x31 -> x26, local copies, waits for them, and re-layouts: 9.13 us -> 2.55 us
    pallas_call x3 -> x4, Pallas kernels: 12.5 us -> 6.95 us  [the longest x1 5.67 us: middle(): pl.pallas_call(middle_kernel, out_shape=(shape((FRAMES, ROWS, 2 * Q, 2 *...]
    pallas_call x1, Pallas kernels: 5.61 us -> 1.1 us  [edges(): pl.pallas_call(edges_kernel, out_shape=(shape((FRAMES, 2, 2 * Q, 2 * C1),...]
    ppermute x4, starting transfers between devices: 13.6 us -> 17 us  [from_both(): lax.ppermute(last, axis, forward(axis))]
    ppermute x4, starting transfers between devices: 9 us -> 5.94 us  [from_both(): lax.ppermute(first, axis, backward(axis))]
  transfers between devices with their start and end apart: 9 -> 8, of which waited for: 1 -> 1; matrix products, arithmetic and copies ran while one was open for 3% -> 0% of each run, Pallas kernels for 8% -> 5%
where the time goes in v2:
time: 119 us; the launch traced here: 118 us
  blocking collectives  67.4 us (57%)
  starting transfers between devices  23 us (19%)
  Pallas kernels  22.6 us (19%)
  waiting for transfers between devices  2.6 us (2%)
  local copies, waits for them, and re-layouts  2.55 us (2%)
    all_to_all x3, blocking collectives, everywhere(): return lax.all_to_all(share, AXES, 0, 0, tiled=True)  67.4 us
    ppermute x4, starting transfers between devices, from_both(): lax.ppermute(last, axis, forward(axis))  17 us
    pallas_call x1, Pallas kernels, second_level(): pl.pallas_call(functools.partial(second_kernel, members=float(devices * F...  8.2 us
    ppermute x4, starting transfers between devices, from_both(): lax.ppermute(first, axis, backward(axis))  5.94 us
    pallas_call x1, Pallas kernels, middle(): pl.pallas_call(middle_kernel, out_shape=(shape((FRAMES, ROWS, 2 * Q, 2 *...  5.67 us
    pallas_call x1, Pallas kernels, third_level(): pl.pallas_call(functools.partial(third_kernel, members=float(devices * FR...  3.69 us
    pallas_call x1, Pallas kernels, last_level(): pl.pallas_call(functools.partial(last_kernel, members=float(devices * FRA...  2.63 us
    ppermute x4, waiting for transfers between devices, from_both(): lax.ppermute(first, axis, backward(axis))  2.59 us
  transfers between devices with their start and end apart: 8, of which 1 were waited for; matrix products, arithmetic and copies ran while one was open for 0% of the time, Pallas kernels for 5%

profile of v2, /device:TPU:1, one launch (start us, length us, event | category | flops | bytes accessed | tf_op | source)
XLA Modules:
  0.0 118.4 jit_solution(17990569549666358317)
XLA Ops:
  0.0 1.3 %copy-done = bf16[4,8,160,128]{3,2,1,0:T(8,128)(2,1)S(1)} copy-done((bf16[4,8,160,128]{3,2,1,0:T(8,128)(2,1)S(1)}, bf16[4,8,160,128]{3,2,1,0:T(8,128)(2,1)}, u32[]{:S(2)}) %copy-start) | copy-done | bytes 1310744
  1.4 4.6 %collective-permute-start = (bf16[32,16,128]{2,1,0:T(8,128)(2,1)S(1)}, bf16[32,16,128]{2,1,0:T(8,128)(2,1)S(1)}, u32[]{:S(2)}, u32[]{:S(2)}) collective-permute-start(bf16[32,16,128]{2,1,0:T(8,128)(2,1)S(1)} %get-tuple-element.22), channel_id=1, source_target_pairs={{0,1},{1,2},{2,3},{3,4},{4,5},{5,6},{6,7},{8,9},{9,10},{10,11},{11... | collective-permute-start | bytes 393224 | tf_op jit(solution)/shard_map/ppermute | solution.py:538
  6.0 1.9 %collective-permute-start.1 = (bf16[32,16,128]{2,1,0:T(8,128)(2,1)S(1)}, bf16[32,16,128]{2,1,0:T(8,128)(2,1)S(1)}, u32[]{:S(2)}, u32[]{:S(2)}) collective-permute-start(bf16[32,16,128]{2,1,0:T(8,128)(2,1)S(1)} %get-tuple-element.23), channel_id=1, source_target_pairs={{1,0},{2,1},{3,2},{4,3},{5,4},{6,5},{7,6},{9,8},{10,9},{11,10},{12... | collective-permute-start | bytes 393224 | tf_op jit(solution)/shard_map/ppermute | solution.py:538
  8.0 0.0 copy-start.2
  8.0 1.2 copy-done.2
  9.1 0.6 weights.1.table
  9.7 2.6 %collective-permute-done.1.right = bf16[32,16,128]{2,1,0:T(8,128)(2,1)S(1)} collective-permute-done((bf16[32,16,128]{2,1,0:T(8,128)(2,1)S(1)}, bf16[32,16,128]{2,1,0:T(8,128)(2,1)S(1)}, u32[]{:S(2)}, u32[]{:S(2)}) %collective-permute-start.1) | collective-permute-done | bytes 131104 | tf_op jit(solution)/shard_map/ppermute | solution.py:538
  12.3 0.7 planes.1
  13.0 3.6 %collective-permute-start.2 = (bf16[4,48,512]{2,1,0:T(8,128)(2,1)S(1)}, bf16[4,48,512]{2,1,0:T(8,128)(2,1)S(1)}, u32[]{:S(2)}, u32[]{:S(2)}) collective-permute-start(bf16[4,48,512]{2,1,0:T(8,128)(2,1)S(1)} %get-tuple-element.26), channel_id=1, source_target_pairs={{0,8},{8,16},{16,24},{24,32},{32,40},{40,48},{48,56},{56,64},{64,7... | collective-permute-start | bytes 589832 | tf_op jit(solution)/shard_map/ppermute | solution.py:538
  16.5 1.3 %collective-permute-start.3 = (bf16[4,48,512]{2,1,0:T(8,128)(2,1)S(1)}, bf16[4,48,512]{2,1,0:T(8,128)(2,1)S(1)}, u32[]{:S(2)}, u32[]{:S(2)}) collective-permute-start(bf16[4,48,512]{2,1,0:T(8,128)(2,1)S(1)} %get-tuple-element.27), channel_id=1, source_target_pairs={{8,0},{16,8},{24,16},{32,24},{40,32},{48,40},{56,48},{64,56},{72,6... | collective-permute-start | bytes 589832 | tf_op jit(solution)/shard_map/ppermute | solution.py:538
  17.8 5.7 %middle.1 = (f32[4,8,96,256]{3,2,1,0:T(8,128)S(1)}, f32[8,256]{1,0:T(8,128)S(1)}) custom-call(bf16[4,10,48,768]{3,2,1,0:T(8,128)(2,1)S(1)} %get-tuple-element.24.planes, bf16[7680,256]{1,0:T(8,128)(2,1)S(1)} %weights.1.table), custom_call_target="tpu_custom_call" | custom-call | flops 6000000000 | bytes 10000000 | tf_op jit(solution)/shard_map/middle/pallas_call | solution.py:184
  23.5 0.0 copy-start.6
  23.6 0.0 copy-start.11
  23.6 1.1 edges.1
  24.7 1.4 %collective-permute-start.5 = (bf16[4,3,96,256]{3,2,1,0:T(8,128)(2,1)S(1)}, bf16[4,3,96,256]{3,2,1,0:T(8,128)(2,1)S(1)}, u32[]{:S(2)}, u32[]{:S(2)}) collective-permute-start(bf16[4,3,96,256]{3,2,1,0:T(8,128)(2,1)S(1)} %get-tuple-element.31), channel_id=1, source_target_pairs={{8,0},{16,8},{24,16},{32,24},{40,32},{48,40},{56,48},{64,56},{72,6... | collective-permute-start | bytes 1769480 | tf_op jit(solution)/shard_map/ppermute | solution.py:538
  26.1 4.8 %collective-permute-start.4 = (bf16[4,2,96,256]{3,2,1,0:T(8,128)(2,1)S(1)}, bf16[4,2,96,256]{3,2,1,0:T(8,128)(2,1)S(1)}, u32[]{:S(2)}, u32[]{:S(2)}) collective-permute-start(bf16[4,2,96,256]{3,2,1,0:T(8,128)(2,1)S(1)} %get-tuple-element.30), channel_id=1, source_target_pairs={{0,8},{8,16},{16,24},{24,32},{32,40},{40,48},{48,56},{56,64},{64,7... | collective-permute-start | bytes 1179656 | tf_op jit(solution)/shard_map/ppermute | solution.py:538
  30.9 29.1 %all_to_all.33 = f32[256,1,128]{2,1,0:T(1,128)S(1)} all-to-all(f32[256,1,128]{2,1,0:T(1,128)S(1)} %bitcast.32), channel_id=1, replica_groups=mesh['rows'=32,'cols'=8] {'rows','cols'}, dimensions={0} | all-to-all | bytes 262144 | tf_op jit(solution)/shard_map/all_to_all | solution.py:542
  60.1 8.2 %second.1 = (f32[4,4,96,256]{3,2,1,0:T(8,128)S(1)}, f32[256,128]{1,0:T(8,128)S(1)}, bf16[4,3,96,256]{3,2,1,0:T(8,128)(2,1)S(1)}, bf16[4,2,96,256]{3,2,1,0:T(8,128)(2,1)S(1)}) custom-call(f32[4,8,96,256]{3,2,1,0:T(8,128)S(1)} %get-tuple-element.25.inner, f32[4,2,96,256]{3,2,1,0:T(8,128)S(1)} %get-tuple-element.29.outer, ...), custom_call_target="tpu_custom_call" | custom-call | flops 6000000000 | bytes 12000000 | tf_op jit(solution)/shard_map/second/pallas_call | solution.py:396
  68.3 1.3 %collective-permute-start.7 = (bf16[4,3,96,256]{3,2,1,0:T(8,128)(2,1)S(1)}, bf16[4,3,96,256]{3,2,1,0:T(8,128)(2,1)S(1)}, u32[]{:S(2)}, u32[]{:S(2)}) collective-permute-start(bf16[4,3,96,256]{3,2,1,0:T(8,128)(2,1)S(1)} %get-tuple-element.35), channel_id=1, source_target_pairs={{8,0},{16,8},{24,16},{32,24},{40,32},{48,40},{56,48},{64,56},{72,6... | collective-permute-start | bytes 1769480 | tf_op jit(solution)/shard_map/ppermute | solution.py:538
  69.6 4.0 %collective-permute-start.6 = (bf16[4,2,96,256]{3,2,1,0:T(8,128)(2,1)S(1)}, bf16[4,2,96,256]{3,2,1,0:T(8,128)(2,1)S(1)}, u32[]{:S(2)}, u32[]{:S(2)}) collective-permute-start(bf16[4,2,96,256]{3,2,1,0:T(8,128)(2,1)S(1)} %get-tuple-element.34), channel_id=1, source_target_pairs={{0,8},{8,16},{16,24},{24,32},{32,40},{40,48},{48,56},{56,64},{64,7... | collective-permute-start | bytes 1179656 | tf_op jit(solution)/shard_map/ppermute | solution.py:538
  73.6 20.0 %all_to_all.34 = f32[256,1,128]{2,1,0:T(1,128)S(1)} all-to-all(f32[256,1,128]{2,1,0:T(1,128)S(1)} %bitcast.31), channel_id=1, replica_groups=mesh['rows'=32,'cols'=8] {'rows','cols'}, dimensions={0} | all-to-all | bytes 262144 | tf_op jit(solution)/shard_map/all_to_all | solution.py:542
  93.7 3.7 %third.1 = (bf16[4,4,48,512]{3,2,1,0:T(8,128)(2,1)S(1)}, f32[256,128]{1,0:T(8,128)S(1)}) custom-call(f32[4,4,96,256]{3,2,1,0:T(8,128)S(1)} %get-tuple-element.33.inner, bf16[4,2,96,256]{3,2,1,0:T(8,128)(2,1)S(1)} %collective-permute-done.6.above, bf16[4,3,96,256]{3,2,1,0:T(8,128)(2,1)S(1)} %collective-permute-done.7.below, f32[256,128]{1,0:T(8,128)S(1)} %bitcast.33, ...), custom_call_target="tpu_custom_call" | custom-call | flops 2000000000 | bytes 8000000 | tf_op jit(solution)/shard_map/third/pallas_call | solution.py:464
  97.4 18.4 %all_to_all.35 = f32[256,1,128]{2,1,0:T(1,128)S(1)} all-to-all(f32[256,1,128]{2,1,0:T(1,128)S(1)} %bitcast.34), channel_id=1, replica_groups=mesh['rows'=32,'cols'=8] {'rows','cols'}, dimensions={0} | all-to-all | bytes 262144 | tf_op jit(solution)/shard_map/all_to_all | solution.py:542
  115.7 2.6 %last.1 = bf16[4,2,32,40]{3,2,1,0:T(8,128)(2,1)} custom-call(bf16[4,4,48,512]{3,2,1,0:T(8,128)(2,1)S(1)} %get-tuple-element.37.level, f32[256,128]{1,0:T(8,128)S(1)} %bitcast.35, f32[1,512]{1,0:T(1,128)S(1)} %bitcast.40, f32[1,512]{1,0:T(1,128)S(1)} %bitcast.41, bf16[3,9,32,512]{3,2,1,0:T(8,128)(2,1)S(1)} %bitcast.38), custom_call_target="tpu_custom_call" | custom-call | flops 1000000000 | bytes 4000000 | tf_op jit(solution)/shard_map/last/pallas_call | solution.py:516
  (29 shorter events, 0.1 us)
Async XLA Ops:
  0.0 1.3 %copy-start = (bf16[4,8,160,128]{3,2,1,0:T(8,128)(2,1)S(1)}, bf16[4,8,160,128]{3,2,1,0:T(8,128)(2,1)}, u32[]{:S(2)}) copy-start(bf16[4,8,160,128]{3,2,1,0:T(8,128)(2,1)} %param.12) | copy-start | bytes 3932164
  1.3 11.0 %copy-start.1 = (bf16[4,8,160,128]{3,2,1,0:T(8,128)(2,1)S(1)}, bf16[4,8,160,128]{3,2,1,0:T(8,128)(2,1)}, u32[]{:S(2)}) copy-start(bf16[4,8,160,128]{3,2,1,0:T(8,128)(2,1)} %param.12) | copy-start | bytes 3932164
  1.4 8.3 %collective-permute-start = (bf16[32,16,128]{2,1,0:T(8,128)(2,1)S(1)}, bf16[32,16,128]{2,1,0:T(8,128)(2,1)S(1)}, u32[]{:S(2)}, u32[]{:S(2)}) collective-permute-start(bf16[32,16,128]{2,1,0:T(8,128)(2,1)S(1)} %get-tuple-element.22), channel_id=1, source_target_pairs={{0,1},{1,2},{2,3},{3,4},{4,5},{5,6},{6,7},{8,9},{9,10},{10,11},{11... | collective-permute-start | bytes 393224 | tf_op jit(solution)/shard_map/ppermute | solution.py:538
  6.0 6.3 %collective-permute-start.1 = (bf16[32,16,128]{2,1,0:T(8,128)(2,1)S(1)}, bf16[32,16,128]{2,1,0:T(8,128)(2,1)S(1)}, u32[]{:S(2)}, u32[]{:S(2)}) collective-permute-start(bf16[32,16,128]{2,1,0:T(8,128)(2,1)S(1)} %get-tuple-element.23), channel_id=1, source_target_pairs={{1,0},{2,1},{3,2},{4,3},{5,4},{6,5},{7,6},{9,8},{10,9},{11,10},{12... | collective-permute-start | bytes 393224 | tf_op jit(solution)/shard_map/ppermute | solution.py:538
  8.0 1.2 copy-start.2
  13.0 10.5 %collective-permute-start.2 = (bf16[4,48,512]{2,1,0:T(8,128)(2,1)S(1)}, bf16[4,48,512]{2,1,0:T(8,128)(2,1)S(1)}, u32[]{:S(2)}, u32[]{:S(2)}) collective-permute-start(bf16[4,48,512]{2,1,0:T(8,128)(2,1)S(1)} %get-tuple-element.26), channel_id=1, source_target_pairs={{0,8},{8,16},{16,24},{24,32},{32,40},{40,48},{48,56},{56,64},{64,7... | collective-permute-start | bytes 589832 | tf_op jit(solution)/shard_map/ppermute | solution.py:538
  16.5 7.0 %collective-permute-start.3 = (bf16[4,48,512]{2,1,0:T(8,128)(2,1)S(1)}, bf16[4,48,512]{2,1,0:T(8,128)(2,1)S(1)}, u32[]{:S(2)}, u32[]{:S(2)}) collective-permute-start(bf16[4,48,512]{2,1,0:T(8,128)(2,1)S(1)} %get-tuple-element.27), channel_id=1, source_target_pairs={{8,0},{16,8},{24,16},{32,24},{40,32},{48,40},{56,48},{64,56},{72,6... | collective-permute-start | bytes 589832 | tf_op jit(solution)/shard_map/ppermute | solution.py:538
  23.5 36.5 %copy-start.3 = (bf16[3,3,3,256,256]{4,3,2,1,0:T(8,128)(2,1)S(1)}, bf16[3,3,3,256,256]{4,3,2,1,0:T(8,128)(2,1)}, u32[]{:S(2)}) copy-start(bf16[3,3,3,256,256]{4,3,2,1,0:T(8,128)(2,1)} %param.15) | copy-start | bytes 10616836
  23.5 36.5 %copy-start.6 = (bf16[3,3,128,256]{3,2,1,0:T(8,128)(2,1)S(1)}, bf16[3,3,128,256]{3,2,1,0:T(8,128)(2,1)}, u32[]{:S(2)}) copy-start(bf16[3,3,128,256]{3,2,1,0:T(8,128)(2,1)} %param.14) | copy-start | bytes 1769476
  23.6 36.5 %copy-start.11 = (f32[128]{0:T(128)S(1)}, f32[128]{0:T(128)}, u32[]{:S(2)}) copy-start(f32[128]{0:T(128)} %param.18) | copy-start | bytes 1540
  23.6 36.5 %copy-start.12 = (f32[128]{0:T(128)S(1)}, f32[128]{0:T(128)}, u32[]{:S(2)}) copy-start(f32[128]{0:T(128)} %param.19) | copy-start | bytes 1540
  24.7 35.3 %collective-permute-start.5 = (bf16[4,3,96,256]{3,2,1,0:T(8,128)(2,1)S(1)}, bf16[4,3,96,256]{3,2,1,0:T(8,128)(2,1)S(1)}, u32[]{:S(2)}, u32[]{:S(2)}) collective-permute-start(bf16[4,3,96,256]{3,2,1,0:T(8,128)(2,1)S(1)} %get-tuple-element.31), channel_id=1, source_target_pairs={{8,0},{16,8},{24,16},{32,24},{40,32},{48,40},{56,48},{64,56},{72,6... | collective-permute-start | bytes 1769480 | tf_op jit(solution)/shard_map/ppermute | solution.py:538
  26.1 33.9 %collective-permute-start.4 = (bf16[4,2,96,256]{3,2,1,0:T(8,128)(2,1)S(1)}, bf16[4,2,96,256]{3,2,1,0:T(8,128)(2,1)S(1)}, u32[]{:S(2)}, u32[]{:S(2)}) collective-permute-start(bf16[4,2,96,256]{3,2,1,0:T(8,128)(2,1)S(1)} %get-tuple-element.30), channel_id=1, source_target_pairs={{0,8},{8,16},{16,24},{24,32},{32,40},{40,48},{48,56},{56,64},{64,7... | collective-permute-start | bytes 1179656 | tf_op jit(solution)/shard_map/ppermute | solution.py:538
  60.1 33.6 %copy-start.4 = (bf16[3,3,256,512]{3,2,1,0:T(8,128)(2,1)S(1)}, bf16[3,3,256,512]{3,2,1,0:T(8,128)(2,1)}, u32[]{:S(2)}) copy-start(bf16[3,3,256,512]{3,2,1,0:T(8,128)(2,1)} %param.16) | copy-start | bytes 7077892
  60.1 33.6 %copy-start.9 = (f32[256]{0:T(256)S(1)}, f32[256]{0:T(256)}, u32[]{:S(2)}) copy-start(f32[256]{0:T(256)} %param.20) | copy-start | bytes 3076
  60.1 33.6 %copy-start.10 = (f32[256]{0:T(256)S(1)}, f32[256]{0:T(256)}, u32[]{:S(2)}) copy-start(f32[256]{0:T(256)} %param.21) | copy-start | bytes 3076
  68.3 25.3 %collective-permute-start.7 = (bf16[4,3,96,256]{3,2,1,0:T(8,128)(2,1)S(1)}, bf16[4,3,96,256]{3,2,1,0:T(8,128)(2,1)S(1)}, u32[]{:S(2)}, u32[]{:S(2)}) collective-permute-start(bf16[4,3,96,256]{3,2,1,0:T(8,128)(2,1)S(1)} %get-tuple-element.35), channel_id=1, source_target_pairs={{8,0},{16,8},{24,16},{32,24},{40,32},{48,40},{56,48},{64,56},{72,6... | collective-permute-start | bytes 1769480 | tf_op jit(solution)/shard_map/ppermute | solution.py:538
  69.6 24.0 %collective-permute-start.6 = (bf16[4,2,96,256]{3,2,1,0:T(8,128)(2,1)S(1)}, bf16[4,2,96,256]{3,2,1,0:T(8,128)(2,1)S(1)}, u32[]{:S(2)}, u32[]{:S(2)}) collective-permute-start(bf16[4,2,96,256]{3,2,1,0:T(8,128)(2,1)S(1)} %get-tuple-element.34), channel_id=1, source_target_pairs={{0,8},{8,16},{16,24},{24,32},{32,40},{40,48},{48,56},{56,64},{64,7... | collective-permute-start | bytes 1179656 | tf_op jit(solution)/shard_map/ppermute | solution.py:538
  93.6 22.1 %copy-start.5 = (bf16[3,3,3,512,32]{3,4,2,1,0:T(8,128)(2,1)S(1)}, bf16[3,3,3,512,32]{3,4,2,1,0:T(8,128)(2,1)}, u32[]{:S(2)}) copy-start(bf16[3,3,3,512,32]{3,4,2,1,0:T(8,128)(2,1)} %param.17) | copy-start | bytes 2654212
  93.7 22.1 %copy-start.7 = (f32[512]{0:T(512)S(1)}, f32[512]{0:T(512)}, u32[]{:S(2)}) copy-start(f32[512]{0:T(512)} %param.22) | copy-start | bytes 6148
  93.7 22.1 %copy-start.8 = (f32[512]{0:T(512)S(1)}, f32[512]{0:T(512)}, u32[]{:S(2)}) copy-start(f32[512]{0:T(512)} %param.23) | copy-start | bytes 6148

commit v3 on v2

--- a/solution.py
+++ b/solution.py
@@ -40,8 +40,9 @@
     return jnp.dot(left, right, preferred_element_type=F32)
 
 
-def exact(left, right):
-    return jnp.dot(left, right, preferred_element_type=F32, precision=lax.Precision.HIGHEST)
+def position():
+    row, col = lax.axis_index("rows"), lax.axis_index("cols")
+    return row == 0, row == lax.axis_size("rows") - 1, col == 0, col == lax.axis_size("cols") - 1
 
 
 def weights_kernel(first, one):
@@ -99,15 +100,18 @@
 
 
 def planes_kernel(left, own, right, planes, top, bottom, line):
+    _, _, first_col, last_col = position()
+    left_in = 1.0 - first_col.astype(F32)
+    right_in = 1.0 - last_col.astype(F32)
     for t in range(FRAMES):
         planes[t, 0] = jnp.zeros((Q, 6 * C1), BF16)
         planes[t, ROWS + 1] = jnp.zeros((Q, 6 * C1), BF16)
 
         def step(r, carry, t=t):
             i = t * ROWS + r
-            line[i, 0:EDGE, :] = left[i].astype(F32)
+            line[i, 0:EDGE, :] = left[i].astype(F32) * left_in
             line[i, EDGE : EDGE + COLS, :] = own[i].astype(F32)
-            line[i, EDGE + COLS : 2 * EDGE + COLS, :] = right[i].astype(F32)
+            line[i, EDGE + COLS : 2 * EDGE + COLS, :] = right[i].astype(F32) * right_in
             line[i, 2 * EDGE + COLS : LINE, :] = jnp.zeros((LINE - 2 * EDGE - COLS, C1), F32)
             for k in range(6):
                 planes[t, 1 + r, :, k * C1 : (k + 1) * C1] = line[i, pl.ds(7 + k, Q, stride=4), :].astype(BF16)
@@ -195,34 +199,42 @@
     )(planes, table)
 
 
-def group_matrix(channels, shift):
-    per = channels // GROUPS
-    c = lax.broadcasted_iota(jnp.int32, (channels, 128), 0)
-    g = lax.broadcasted_iota(jnp.int32, (channels, 128), 1)
-    low = (g - shift) * per
-    return jnp.where((c >= low) & (c < low + per), 1.0, 0.0).astype(F32)
-
-
-def spread_matrix(channels, shift):
-    per = channels // GROUPS
-    g = lax.broadcasted_iota(jnp.int32, (128, channels), 0)
-    c = lax.broadcasted_iota(jnp.int32, (128, channels), 1)
-    low = (g - shift) * per
-    return jnp.where((c >= low) & (c < low + per), 1.0, 0.0).astype(F32)
+def group_totals(values, per):
+    lane = lax.broadcasted_iota(jnp.int32, (8, 128), 1)
+    step = 1
+    while step < per:
+        other = jnp.where((lane & step) == 0, pltpu.roll(values, 128 - step, 1), pltpu.roll(values, step, 1))
+        values = values + other
+        step *= 2
+    return values
+
+
+def slots(per):
+    lane = lax.broadcasted_iota(jnp.int32, (8, 128), 1)
+    return (lane & (per - 1)) == lax.broadcasted_iota(jnp.int32, (8, 128), 0)
 
 
 def grouped(one, two):
     channels = one.shape[1]
-    wide = lambda v: jnp.broadcast_to(v, (8, channels))
-    row = exact(wide(one), group_matrix(channels, 0)) + exact(wide(two), group_matrix(channels, GROUPS))
-    return row[0:1]
+    per = channels // GROUPS
+    lines = []
+    for low in range(0, channels, 128):
+        lines += [one[:, low : low + 128], two[:, low : low + 128]]
+    lines += [jnp.zeros((1, 128), F32)] * (8 - len(lines))
+    totals = group_totals(jnp.concatenate(lines, axis=0), per)
+    return jnp.sum(jnp.where(slots(per), totals, 0.0), axis=0, keepdims=True)
 
 
 def norm_terms(gathered, gain, shift, members):
     channels = gain.shape[1]
+    per = channels // GROUPS
     total = jnp.broadcast_to(jnp.sum(gathered[...], axis=0, keepdims=True), (8, 128))
-    mean = exact(total, spread_matrix(channels, 0))[0:1] / members
-    square = exact(total, spread_matrix(channels, GROUPS))[0:1] / members
+    lane = lax.broadcasted_iota(jnp.int32, (8, 128), 1)
+    source = lane - (lane & (per - 1)) + (lax.broadcasted_iota(jnp.int32, (8, 128), 0) & (per - 1))
+    lines = jnp.take_along_axis(total, source, axis=1) / members
+    count = channels // 128
+    mean = jnp.concatenate([lines[2 * i : 2 * i + 1] for i in range(count)], axis=1)
+    square = jnp.concatenate([lines[2 * i + 1 : 2 * i + 2] for i in range(count)], axis=1)
     variance = jnp.maximum(square - mean * mean, 0.0)
     factor = gain[...] / jnp.sqrt(variance + EPSILON)
     return 0.5 * factor, 0.5 * (shift[...] - mean * factor)
@@ -231,12 +243,15 @@
 def edges_kernel(above, below, table, inner, stats, hidden, share, up, down):
     mask = own_entries(2 * Q, 2 * C1)
     total = [stats[0:1, :], stats[1:2, :]]
-    for side, (ref, b) in enumerate(((above, 0), (below, 2))):
+    first_row, last_row, _, _ = position()
+    for side, (ref, b, end) in enumerate(((above, 0, first_row), (below, 2, last_row))):
+        inside = 1.0 - end.astype(F32)
         lines = []
         for t in range(FRAMES):
-            whole = ref[t]
-            first = pltpu.roll(whole[:, 3 * C1 :].astype(F32), 1, 0).astype(BF16)
-            last = pltpu.roll(whole[:, :C1].astype(F32), Q - 1, 0).astype(BF16)
+            wide = ref[t].astype(F32) * inside
+            whole = wide.astype(BF16)
+            first = pltpu.roll(wide[:, 3 * C1 :], 1, 0).astype(BF16)
+            last = pltpu.roll(wide[:, :C1], Q - 1, 0).astype(BF16)
             even = jnp.concatenate([first, whole[:, : 3 * C1]], axis=1)
             odd = jnp.concatenate([whole[:, C1:], last], axis=1)
             lines.append(jnp.concatenate([even, odd], axis=0))
@@ -282,11 +297,6 @@
         cost_estimate=cost(2e9, 10e6),
         name="edges",
     )(above, below, table, inner, stats)
-
-
-def position():
-    row, col = lax.axis_index("rows"), lax.axis_index("cols")
-    return row == 0, row == lax.axis_size("rows") - 1, col == 0, col == lax.axis_size("cols") - 1
 
 
 def kept(entry_out, edge):
@@ -362,7 +372,7 @@
             lev[t, i, Q:, 2 * C2 :] = raised(even).astype(BF16)
         return carry
 
-    lax.fori_loop(0, FRAMES, lines, 0)
+    lax.fori_loop(0, FRAMES, lines, 0, unroll=True)
 
     def add(i, carry):
         at = pl.ds(pl.multiple_of(i * C2, C2), C2)
@@ -371,7 +381,7 @@
         summed[1, at, :] = (pair + second[2, at, :].astype(F32)).astype(BF16)
         return carry
 
-    lax.fori_loop(0, 9, add, 0)
+    lax.fori_loop(0, 9, add, 0, unroll=True)
     rows = 4 * 2 * Q
     mask = own_entries(rows, C2)
     total = [jnp.zeros((1, C2), F32), jnp.zeros((1, C2), F32)]
@@ -442,7 +452,7 @@
             line(t, 6 + r, below[t, r])
         return carry
 
-    lax.fori_loop(0, FRAMES, lines, 0)
+    lax.fori_loop(0, FRAMES, lines, 0, unroll=True)
     mask = own_entries(2 * Q, C3)
     total = [jnp.zeros((1, C3), F32), jnp.zeros((1, C3), F32)]
     value = None
@@ -527,11 +537,11 @@
 
 
 def forward(axis):
-    return [(i, i + 1) for i in range(lax.axis_size(axis) - 1)]
+    return [(i, (i + 1) % lax.axis_size(axis)) for i in range(lax.axis_size(axis))]
 
 
 def backward(axis):
-    return [(i + 1, i) for i in range(lax.axis_size(axis) - 1)]
+    return [((i + 1) % lax.axis_size(axis), i) for i in range(lax.axis_size(axis))]
 
 
 def from_both(last, first, axis):

time: 119 us -> 104 us (0.87)
  starting transfers between devices: 23 us -> 16.7 us
  blocking collectives: 67.4 us -> 62.8 us
  Pallas kernels: 22.6 us -> 19.5 us
    ppermute x4, starting transfers between devices: 17 us -> 4.51 us  [from_both(): lax.ppermute(last, axis, forward(axis))]
    ppermute x4, starting transfers between devices: 5.94 us -> 12.2 us  [from_both(): lax.ppermute(first, axis, backward(axis))]
    all_to_all x3, blocking collectives: 67.4 us -> 62.8 us  [everywhere(): return lax.all_to_all(share, AXES, 0, 0, tiled=True)]
    pallas_call x1, Pallas kernels: 8.2 us -> 6.84 us  [second_level(): pl.pallas_call(functools.partial(second_kernel, members=float(devices * F...]
  transfers between devices with their start and end apart: 8 -> 8, of which waited for: 1 -> 1; matrix products, arithmetic and copies ran while one was open for 0% -> 0% of each run, Pallas kernels for 5% -> 6%
where the time goes in v3:
time: 104 us
  blocking collectives  62.8 us (60%)
  Pallas kernels  19.5 us (19%)
  starting transfers between devices  16.7 us (16%)
  local copies, waits for them, and re-layouts  2.55 us (2%)
  waiting for transfers between devices  2.28 us (2%)
    all_to_all x3, blocking collectives, everywhere(): return lax.all_to_all(share, AXES, 0, 0, tiled=True)  62.8 us
    ppermute x4, starting transfers between devices, from_both(): lax.ppermute(first, axis, backward(axis))  12.2 us
    pallas_call x1, Pallas kernels, second_level(): pl.pallas_call(functools.partial(second_kernel, members=float(devices * F...  6.84 us
    pallas_call x1, Pallas kernels, middle(): pl.pallas_call(middle_kernel, out_shape=(shape((FRAMES, ROWS, 2 * Q, 2 *...  5.66 us
    ppermute x4, starting transfers between devices, from_both(): lax.ppermute(last, axis, forward(axis))  4.51 us
    pallas_call x1, Pallas kernels, third_level(): pl.pallas_call(functools.partial(third_kernel, members=float(devices * FR...  2.59 us
    unnamed x26, local copies, waits for them, and re-layouts  2.55 us
    ppermute x4, waiting for transfers between devices, from_both(): lax.ppermute(first, axis, backward(axis))  2.27 us
  transfers between devices with their start and end apart: 8, of which 1 were waited for; matrix products, arithmetic and copies ran while one was open for 0% of the time, Pallas kernels for 6%

profile of v3, /device:TPU:1, one launch (start us, length us, event | category | flops | bytes accessed | tf_op | source)
XLA Modules:
  0.0 104.1 jit_solution(11477616787792540197)
XLA Ops:
  0.0 1.3 %copy-done = bf16[4,8,160,128]{3,2,1,0:T(8,128)(2,1)S(1)} copy-done((bf16[4,8,160,128]{3,2,1,0:T(8,128)(2,1)S(1)}, bf16[4,8,160,128]{3,2,1,0:T(8,128)(2,1)}, u32[]{:S(2)}) %copy-start) | copy-done | bytes 1310744
  1.4 2.6 %collective-permute-start = (bf16[32,16,128]{2,1,0:T(8,128)(2,1)S(1)}, bf16[32,16,128]{2,1,0:T(8,128)(2,1)S(1)}, u32[]{:S(2)}, u32[]{:S(2)}) collective-permute-start(bf16[32,16,128]{2,1,0:T(8,128)(2,1)S(1)} %get-tuple-element.22), channel_id=1, source_target_pairs={{0,1},{1,2},{2,3},{3,4},{4,5},{5,6},{6,7},{7,0},{8,9},{9,10},{10,1... | collective-permute-start | bytes 393224 | tf_op jit(solution)/shard_map/ppermute | solution.py:548
  4.0 0.7 collective-permute-start.1
  4.6 1.2 %copy-done.2 = bf16[3,3,3,128,128]{4,3,2,1,0:T(8,128)(2,1)S(1)} copy-done((bf16[3,3,3,128,128]{4,3,2,1,0:T(8,128)(2,1)S(1)}, bf16[3,3,3,128,128]{4,3,2,1,0:T(8,128)(2,1)}, u32[]{:S(2)}) %copy-start.2) | copy-done | bytes 884760
  5.8 0.6 weights.1.table
  6.4 2.3 %collective-permute-done.1.right = bf16[32,16,128]{2,1,0:T(8,128)(2,1)S(1)} collective-permute-done((bf16[32,16,128]{2,1,0:T(8,128)(2,1)S(1)}, bf16[32,16,128]{2,1,0:T(8,128)(2,1)S(1)}, u32[]{:S(2)}, u32[]{:S(2)}) %collective-permute-start.1) | collective-permute-done | bytes 131104 | tf_op jit(solution)/shard_map/ppermute | solution.py:548
  8.7 0.7 planes.1
  9.4 1.4 %collective-permute-start.2 = (bf16[4,48,512]{2,1,0:T(8,128)(2,1)S(1)}, bf16[4,48,512]{2,1,0:T(8,128)(2,1)S(1)}, u32[]{:S(2)}, u32[]{:S(2)}) collective-permute-start(bf16[4,48,512]{2,1,0:T(8,128)(2,1)S(1)} %get-tuple-element.26), channel_id=1, source_target_pairs={{0,8},{8,16},{16,24},{24,32},{32,40},{40,48},{48,56},{56,64},{64,7... | collective-permute-start | bytes 589832 | tf_op jit(solution)/shard_map/ppermute | solution.py:548
  10.8 6.5 %collective-permute-start.3 = (bf16[4,48,512]{2,1,0:T(8,128)(2,1)S(1)}, bf16[4,48,512]{2,1,0:T(8,128)(2,1)S(1)}, u32[]{:S(2)}, u32[]{:S(2)}) collective-permute-start(bf16[4,48,512]{2,1,0:T(8,128)(2,1)S(1)} %get-tuple-element.27), channel_id=1, source_target_pairs={{8,0},{16,8},{24,16},{32,24},{40,32},{48,40},{56,48},{64,56},{72,6... | collective-permute-start | bytes 589832 | tf_op jit(solution)/shard_map/ppermute | solution.py:548
  17.3 5.7 %middle.1 = (f32[4,8,96,256]{3,2,1,0:T(8,128)S(1)}, f32[8,256]{1,0:T(8,128)S(1)}) custom-call(bf16[4,10,48,768]{3,2,1,0:T(8,128)(2,1)S(1)} %get-tuple-element.24.planes, bf16[7680,256]{1,0:T(8,128)(2,1)S(1)} %weights.1.table), custom_call_target="tpu_custom_call" | custom-call | flops 6000000000 | bytes 10000000 | tf_op jit(solution)/shard_map/middle/pallas_call | solution.py:188
  22.9 0.0 copy-start.3
  23.0 0.0 copy-start.12
  23.0 0.9 edges.1
  23.9 4.0 %collective-permute-start.5 = (bf16[4,3,96,256]{3,2,1,0:T(8,128)(2,1)S(1)}, bf16[4,3,96,256]{3,2,1,0:T(8,128)(2,1)S(1)}, u32[]{:S(2)}, u32[]{:S(2)}) collective-permute-start(bf16[4,3,96,256]{3,2,1,0:T(8,128)(2,1)S(1)} %get-tuple-element.31), channel_id=1, source_target_pairs={{8,0},{16,8},{24,16},{32,24},{40,32},{48,40},{56,48},{64,56},{72,6... | collective-permute-start | bytes 1769480 | tf_op jit(solution)/shard_map/ppermute | solution.py:548
  27.9 22.6 %all_to_all.33 = f32[256,1,128]{2,1,0:T(1,128)S(1)} all-to-all(f32[256,1,128]{2,1,0:T(1,128)S(1)} %bitcast.32), channel_id=1, replica_groups=mesh['rows'=32,'cols'=8] {'rows','cols'}, dimensions={0} | all-to-all | bytes 262144 | tf_op jit(solution)/shard_map/all_to_all | solution.py:552
  50.5 0.0 copy-start.9
  50.5 0.0 copy-start.10
  50.6 6.8 %second.1 = (f32[4,4,96,256]{3,2,1,0:T(8,128)S(1)}, f32[256,128]{1,0:T(8,128)S(1)}, bf16[4,3,96,256]{3,2,1,0:T(8,128)(2,1)S(1)}, bf16[4,2,96,256]{3,2,1,0:T(8,128)(2,1)S(1)}) custom-call(f32[4,8,96,256]{3,2,1,0:T(8,128)S(1)} %get-tuple-element.25.inner, f32[4,2,96,256]{3,2,1,0:T(8,128)S(1)} %get-tuple-element.29.outer, ...), custom_call_target="tpu_custom_call" | custom-call | flops 6000000000 | bytes 12000000 | tf_op jit(solution)/shard_map/second/pallas_call | solution.py:406
  57.4 1.1 %collective-permute-start.7 = (bf16[4,3,96,256]{3,2,1,0:T(8,128)(2,1)S(1)}, bf16[4,3,96,256]{3,2,1,0:T(8,128)(2,1)S(1)}, u32[]{:S(2)}, u32[]{:S(2)}) collective-permute-start(bf16[4,3,96,256]{3,2,1,0:T(8,128)(2,1)S(1)} %get-tuple-element.35), channel_id=1, source_target_pairs={{8,0},{16,8},{24,16},{32,24},{40,32},{48,40},{56,48},{64,56},{72,6... | collective-permute-start | bytes 1769480 | tf_op jit(solution)/shard_map/ppermute | solution.py:548
  58.5 0.5 collective-permute-start.6
  58.9 20.3 %all_to_all.34 = f32[256,1,128]{2,1,0:T(1,128)S(1)} all-to-all(f32[256,1,128]{2,1,0:T(1,128)S(1)} %bitcast.31), channel_id=1, replica_groups=mesh['rows'=32,'cols'=8] {'rows','cols'}, dimensions={0} | all-to-all | bytes 262144 | tf_op jit(solution)/shard_map/all_to_all | solution.py:552
  79.3 2.6 %third.1 = (bf16[4,4,48,512]{3,2,1,0:T(8,128)(2,1)S(1)}, f32[256,128]{1,0:T(8,128)S(1)}) custom-call(f32[4,4,96,256]{3,2,1,0:T(8,128)S(1)} %get-tuple-element.33.inner, bf16[4,2,96,256]{3,2,1,0:T(8,128)(2,1)S(1)} %collective-permute-done.6.above, bf16[4,3,96,256]{3,2,1,0:T(8,128)(2,1)S(1)} %collective-permute-done.7.below, f32[256,128]{1,0:T(8,128)S(1)} %bitcast.33, ...), custom_call_target="tpu_custom_call" | custom-call | flops 2000000000 | bytes 8000000 | tf_op jit(solution)/shard_map/third/pallas_call | solution.py:474
  81.9 19.9 %all_to_all.35 = f32[256,1,128]{2,1,0:T(1,128)S(1)} all-to-all(f32[256,1,128]{2,1,0:T(1,128)S(1)} %bitcast.34), channel_id=1, replica_groups=mesh['rows'=32,'cols'=8] {'rows','cols'}, dimensions={0} | all-to-all | bytes 262144 | tf_op jit(solution)/shard_map/all_to_all | solution.py:552
  101.9 2.2 %last.1 = bf16[4,2,32,40]{3,2,1,0:T(8,128)(2,1)} custom-call(bf16[4,4,48,512]{3,2,1,0:T(8,128)(2,1)S(1)} %get-tuple-element.37.level, f32[256,128]{1,0:T(8,128)S(1)} %bitcast.35, f32[1,512]{1,0:T(1,128)S(1)} %bitcast.40, f32[1,512]{1,0:T(1,128)S(1)} %bitcast.41, bf16[3,9,32,512]{3,2,1,0:T(8,128)(2,1)S(1)} %bitcast.38), custom_call_target="tpu_custom_call" | custom-call | flops 1000000000 | bytes 4000000 | tf_op jit(solution)/shard_map/last/pallas_call | solution.py:526
  (29 shorter events, 0.1 us)
Async XLA Ops:
  0.0 1.3 %copy-start = (bf16[4,8,160,128]{3,2,1,0:T(8,128)(2,1)S(1)}, bf16[4,8,160,128]{3,2,1,0:T(8,128)(2,1)}, u32[]{:S(2)}) copy-start(bf16[4,8,160,128]{3,2,1,0:T(8,128)(2,1)} %param.12) | copy-start | bytes 3932164
  1.3 7.4 %copy-start.1 = (bf16[4,8,160,128]{3,2,1,0:T(8,128)(2,1)S(1)}, bf16[4,8,160,128]{3,2,1,0:T(8,128)(2,1)}, u32[]{:S(2)}) copy-start(bf16[4,8,160,128]{3,2,1,0:T(8,128)(2,1)} %param.12) | copy-start | bytes 3932164
  1.4 5.0 %collective-permute-start = (bf16[32,16,128]{2,1,0:T(8,128)(2,1)S(1)}, bf16[32,16,128]{2,1,0:T(8,128)(2,1)S(1)}, u32[]{:S(2)}, u32[]{:S(2)}) collective-permute-start(bf16[32,16,128]{2,1,0:T(8,128)(2,1)S(1)} %get-tuple-element.22), channel_id=1, source_target_pairs={{0,1},{1,2},{2,3},{3,4},{4,5},{5,6},{6,7},{7,0},{8,9},{9,10},{10,1... | collective-permute-start | bytes 393224 | tf_op jit(solution)/shard_map/ppermute | solution.py:548
  4.0 4.7 %collective-permute-start.1 = (bf16[32,16,128]{2,1,0:T(8,128)(2,1)S(1)}, bf16[32,16,128]{2,1,0:T(8,128)(2,1)S(1)}, u32[]{:S(2)}, u32[]{:S(2)}) collective-permute-start(bf16[32,16,128]{2,1,0:T(8,128)(2,1)S(1)} %get-tuple-element.23), channel_id=1, source_target_pairs={{1,0},{2,1},{3,2},{4,3},{5,4},{6,5},{7,6},{0,7},{9,8},{10,9},{11,1... | collective-permute-start | bytes 393224 | tf_op jit(solution)/shard_map/ppermute | solution.py:548
  4.6 1.2 %copy-start.2 = (bf16[3,3,3,128,128]{4,3,2,1,0:T(8,128)(2,1)S(1)}, bf16[3,3,3,128,128]{4,3,2,1,0:T(8,128)(2,1)}, u32[]{:S(2)}) copy-start(bf16[3,3,3,128,128]{4,3,2,1,0:T(8,128)(2,1)} %param.13) | copy-start | bytes 2654212
  9.4 13.6 %collective-permute-start.2 = (bf16[4,48,512]{2,1,0:T(8,128)(2,1)S(1)}, bf16[4,48,512]{2,1,0:T(8,128)(2,1)S(1)}, u32[]{:S(2)}, u32[]{:S(2)}) collective-permute-start(bf16[4,48,512]{2,1,0:T(8,128)(2,1)S(1)} %get-tuple-element.26), channel_id=1, source_target_pairs={{0,8},{8,16},{16,24},{24,32},{32,40},{40,48},{48,56},{56,64},{64,7... | collective-permute-start | bytes 589832 | tf_op jit(solution)/shard_map/ppermute | solution.py:548
  10.8 12.2 %collective-permute-start.3 = (bf16[4,48,512]{2,1,0:T(8,128)(2,1)S(1)}, bf16[4,48,512]{2,1,0:T(8,128)(2,1)S(1)}, u32[]{:S(2)}, u32[]{:S(2)}) collective-permute-start(bf16[4,48,512]{2,1,0:T(8,128)(2,1)S(1)} %get-tuple-element.27), channel_id=1, source_target_pairs={{8,0},{16,8},{24,16},{32,24},{40,32},{48,40},{56,48},{64,56},{72,6... | collective-permute-start | bytes 589832 | tf_op jit(solution)/shard_map/ppermute | solution.py:548
  22.9 27.5 %copy-start.3 = (bf16[3,3,3,256,256]{4,3,2,1,0:T(8,128)(2,1)S(1)}, bf16[3,3,3,256,256]{4,3,2,1,0:T(8,128)(2,1)}, u32[]{:S(2)}) copy-start(bf16[3,3,3,256,256]{4,3,2,1,0:T(8,128)(2,1)} %param.15) | copy-start | bytes 10616836
  23.0 27.5 %copy-start.6 = (bf16[3,3,128,256]{3,2,1,0:T(8,128)(2,1)S(1)}, bf16[3,3,128,256]{3,2,1,0:T(8,128)(2,1)}, u32[]{:S(2)}) copy-start(bf16[3,3,128,256]{3,2,1,0:T(8,128)(2,1)} %param.14) | copy-start | bytes 1769476
  23.0 27.5 %copy-start.11 = (f32[128]{0:T(128)S(1)}, f32[128]{0:T(128)}, u32[]{:S(2)}) copy-start(f32[128]{0:T(128)} %param.18) | copy-start | bytes 1540
  23.0 27.5 %copy-start.12 = (f32[128]{0:T(128)S(1)}, f32[128]{0:T(128)}, u32[]{:S(2)}) copy-start(f32[128]{0:T(128)} %param.19) | copy-start | bytes 1540
  23.9 26.6 %collective-permute-start.5 = (bf16[4,3,96,256]{3,2,1,0:T(8,128)(2,1)S(1)}, bf16[4,3,96,256]{3,2,1,0:T(8,128)(2,1)S(1)}, u32[]{:S(2)}, u32[]{:S(2)}) collective-permute-start(bf16[4,3,96,256]{3,2,1,0:T(8,128)(2,1)S(1)} %get-tuple-element.31), channel_id=1, source_target_pairs={{8,0},{16,8},{24,16},{32,24},{40,32},{48,40},{56,48},{64,56},{72,6... | collective-permute-start | bytes 1769480 | tf_op jit(solution)/shard_map/ppermute | solution.py:548
  27.9 22.6 %collective-permute-start.4 = (bf16[4,2,96,256]{3,2,1,0:T(8,128)(2,1)S(1)}, bf16[4,2,96,256]{3,2,1,0:T(8,128)(2,1)S(1)}, u32[]{:S(2)}, u32[]{:S(2)}) collective-permute-start(bf16[4,2,96,256]{3,2,1,0:T(8,128)(2,1)S(1)} %get-tuple-element.30), channel_id=1, source_target_pairs={{0,8},{8,16},{16,24},{24,32},{32,40},{40,48},{48,56},{56,64},{64,7... | collective-permute-start | bytes 1179656 | tf_op jit(solution)/shard_map/ppermute | solution.py:548
  50.5 28.8 %copy-start.4 = (bf16[3,3,256,512]{3,2,1,0:T(8,128)(2,1)S(1)}, bf16[3,3,256,512]{3,2,1,0:T(8,128)(2,1)}, u32[]{:S(2)}) copy-start(bf16[3,3,256,512]{3,2,1,0:T(8,128)(2,1)} %param.16) | copy-start | bytes 7077892
  50.5 28.7 %copy-start.9 = (f32[256]{0:T(256)S(1)}, f32[256]{0:T(256)}, u32[]{:S(2)}) copy-start(f32[256]{0:T(256)} %param.20) | copy-start | bytes 3076
  50.5 28.7 %copy-start.10 = (f32[256]{0:T(256)S(1)}, f32[256]{0:T(256)}, u32[]{:S(2)}) copy-start(f32[256]{0:T(256)} %param.21) | copy-start | bytes 3076
  57.4 21.9 %collective-permute-start.7 = (bf16[4,3,96,256]{3,2,1,0:T(8,128)(2,1)S(1)}, bf16[4,3,96,256]{3,2,1,0:T(8,128)(2,1)S(1)}, u32[]{:S(2)}, u32[]{:S(2)}) collective-permute-start(bf16[4,3,96,256]{3,2,1,0:T(8,128)(2,1)S(1)} %get-tuple-element.35), channel_id=1, source_target_pairs={{8,0},{16,8},{24,16},{32,24},{40,32},{48,40},{56,48},{64,56},{72,6... | collective-permute-start | bytes 1769480 | tf_op jit(solution)/shard_map/ppermute | solution.py:548
  58.5 20.8 %collective-permute-start.6 = (bf16[4,2,96,256]{3,2,1,0:T(8,128)(2,1)S(1)}, bf16[4,2,96,256]{3,2,1,0:T(8,128)(2,1)S(1)}, u32[]{:S(2)}, u32[]{:S(2)}) collective-permute-start(bf16[4,2,96,256]{3,2,1,0:T(8,128)(2,1)S(1)} %get-tuple-element.34), channel_id=1, source_target_pairs={{0,8},{8,16},{16,24},{24,32},{32,40},{40,48},{48,56},{56,64},{64,7... | collective-permute-start | bytes 1179656 | tf_op jit(solution)/shard_map/ppermute | solution.py:548
  79.3 22.6 %copy-start.5 = (bf16[3,3,3,512,32]{3,4,2,1,0:T(8,128)(2,1)S(1)}, bf16[3,3,3,512,32]{3,4,2,1,0:T(8,128)(2,1)}, u32[]{:S(2)}) copy-start(bf16[3,3,3,512,32]{3,4,2,1,0:T(8,128)(2,1)} %param.17) | copy-start | bytes 2654212
  79.3 22.5 %copy-start.7 = (f32[512]{0:T(512)S(1)}, f32[512]{0:T(512)}, u32[]{:S(2)}) copy-start(f32[512]{0:T(512)} %param.22) | copy-start | bytes 6148
  79.3 22.5 %copy-start.8 = (f32[512]{0:T(512)S(1)}, f32[512]{0:T(512)}, u32[]{:S(2)}) copy-start(f32[512]{0:T(512)} %param.23) | copy-start | bytes 6148

commit v4 on v3

--- a/solution.py
+++ b/solution.py
@@ -104,8 +104,6 @@
     left_in = 1.0 - first_col.astype(F32)
     right_in = 1.0 - last_col.astype(F32)
     for t in range(FRAMES):
-        planes[t, 0] = jnp.zeros((Q, 6 * C1), BF16)
-        planes[t, ROWS + 1] = jnp.zeros((Q, 6 * C1), BF16)
 
         def step(r, carry, t=t):
             i = t * ROWS + r
@@ -114,12 +112,12 @@
             line[i, EDGE + COLS : 2 * EDGE + COLS, :] = right[i].astype(F32) * right_in
             line[i, 2 * EDGE + COLS : LINE, :] = jnp.zeros((LINE - 2 * EDGE - COLS, C1), F32)
             for k in range(6):
-                planes[t, 1 + r, :, k * C1 : (k + 1) * C1] = line[i, pl.ds(7 + k, Q, stride=4), :].astype(BF16)
+                planes[t, r, :, k * C1 : (k + 1) * C1] = line[i, pl.ds(7 + k, Q, stride=4), :].astype(BF16)
             return carry
 
         lax.fori_loop(0, ROWS, step, 0, unroll=True)
-        top[t] = planes[t, 1, :, C1 : 5 * C1]
-        bottom[t] = planes[t, ROWS, :, C1 : 5 * C1]
+        top[t] = planes[t, 0, :, C1 : 5 * C1]
+        bottom[t] = planes[t, ROWS - 1, :, C1 : 5 * C1]
 
 
 def planes_of(left, own, right):
@@ -127,7 +125,7 @@
     return pl.pallas_call(
         planes_kernel,
         out_shape=(
-            shape((FRAMES, ROWS + 2, Q, 6 * C1), BF16),
+            shape((FRAMES, ROWS, Q, 6 * C1), BF16),
             shape((FRAMES, Q, 4 * C1), BF16),
             shape((FRAMES, Q, 4 * C1), BF16),
         ),
@@ -150,38 +148,37 @@
     return jnp.sum(kept, axis=0, keepdims=True), jnp.sum(kept * kept, axis=0, keepdims=True)
 
 
-def frames_conv(frame, weight, store):
-    store(0, mm(frame(0), weight(4)))
-    store(1, mm(frame(0), weight(3)) + mm(frame(1), weight(2)))
-    for t in range(2, FRAMES):
-        store(t, mm(frame(t - 2), weight(0)) + mm(frame(t - 1), weight(1)) + mm(frame(t), weight(2)))
-
-
-def table_of(ref, rows):
-    return lambda s: ref[s * rows : (s + 1) * rows, :]
+FRAME_TERMS = [[(0, 4)], [(0, 3), (1, 2)], [(0, 0), (1, 1), (2, 2)], [(1, 0), (2, 1), (3, 2)]]
 
 
 def middle_kernel(planes, table, hidden, stats):
-    rows = ROWS * Q
-    mask = own_entries(2 * (rows - 2 * Q), 2 * C1)
+    mask = own_entries((ROWS - 2) * Q, 2 * C1)
     stats[...] = jnp.zeros(stats.shape, F32)
-
-    def frame(t):
-        parts = []
-        for b in range(3):
-            block = planes[t, b : b + ROWS].reshape(rows, 6 * C1)
-            parts.append(jnp.concatenate([block[:, : 4 * C1], block[:, 2 * C1 :]], axis=0))
-        return jnp.concatenate(parts, axis=1)
-
-    def store(t, value):
-        hidden[t, :, 0:Q, :] = value[:rows].reshape(ROWS, Q, 2 * C1)
-        hidden[t, :, Q : 2 * Q, :] = value[rows:].reshape(ROWS, Q, 2 * C1)
-        inside = jnp.concatenate([value[Q : rows - Q], value[rows + Q : 2 * rows - Q]], axis=0)
-        one, two = sums(inside, mask)
-        stats[0:1, :] += one
-        stats[1:2, :] += two
-
-    frames_conv(frame, table_of(table, 12 * C1), store)
+    for t, terms in enumerate(FRAME_TERMS):
+        for odd in range(2):
+            lanes = slice(2 * C1 * odd, 2 * C1 * odd + 4 * C1)
+
+            def tap(b):
+                low, high = max(b - 1, 0), ROWS + min(b - 1, 0)
+                value = None
+                for f, s in terms:
+                    left = planes[f, low:high, :, lanes].reshape((high - low) * Q, 4 * C1)
+                    base = (3 * s + b) * 4 * C1
+                    part = mm(left, table[base : base + 4 * C1, :])
+                    value = part if value is None else value + part
+                return value
+
+            up, here, down = tap(0), tap(1), tap(2)
+            first = here[:Q] + down[:Q]
+            last = here[-Q:] + up[-Q:]
+            inside = here[Q:-Q] + up[:-Q] + down[Q:]
+            at = slice(odd * Q, (odd + 1) * Q)
+            hidden[t, 0, at, :] = first
+            hidden[t, 1 : ROWS - 1, at, :] = inside.reshape(ROWS - 2, Q, 2 * C1)
+            hidden[t, ROWS - 1, at, :] = last
+            one, two = sums(inside, mask)
+            stats[0:1, :] += one
+            stats[1:2, :] += two
 
 
 def middle(planes, table):
@@ -322,7 +319,7 @@
 
 def second_kernel(
     inner, outer, above, below, gathered, gain, shift, reduce, second,
-    hidden, share, up, down, act, lev, summed, *, members,
+    hidden, share, up, act, lev, summed, *, members,
 ):
     first_row, last_row, first_col, last_col = position()
     terms = twice(norm_terms(gathered, gain, shift, members))
@@ -392,13 +389,17 @@
     def store(t, value):
         full = value.reshape(4, 2 * Q, C2)
         hidden[t] = full
-        up[t] = full[0:3].astype(BF16)
-        down[t] = full[2:4].astype(BF16)
+        up[t] = full[0].astype(BF16)
         one, two = sums(value, mask)
         total[0] += one
         total[1] += two
 
-    frames_conv(frame, lambda s: second[s] if s < 3 else summed[s - 3], store)
+    for t, terms in enumerate(FRAME_TERMS):
+        value = None
+        for f, s in terms:
+            part = mm(frame(f), second[s] if s < 3 else summed[s - 3])
+            value = part if value is None else value + part
+        store(t, value)
     share[...] = jnp.broadcast_to(grouped(*total), share.shape)
 
 
@@ -408,11 +409,10 @@
         out_shape=(
             shape((FRAMES, 4, 2 * Q, C2), F32),
             shape((devices, 128), F32),
-            shape((FRAMES, 3, 2 * Q, C2), BF16),
-            shape((FRAMES, 2, 2 * Q, C2), BF16),
+            shape((FRAMES, 2 * Q, C2), BF16),
         ),
         in_specs=[VMEM] * 9,
-        out_specs=(VMEM,) * 4,
+        out_specs=(VMEM,) * 3,
         scratch_shapes=[
             pltpu.VMEM((FRAMES, 14, 2 * Q, 3 * C1), BF16),
             pltpu.VMEM((FRAMES, 6, 2 * Q, 3 * C2), BF16),
@@ -428,7 +428,7 @@
     )
 
 
-def third_kernel(inner, above, below, gathered, gain, shift, reduce, level, share, act, *, members):
+def third_kernel(inner, below, gathered, gain, shift, reduce, level, share, top, bottom, act, *, members):
     _, last_row, _, last_col = position()
     terms = norm_terms(gathered, gain, shift, members)
     entry = lax.broadcasted_iota(jnp.int32, (Q, 1), 0)
@@ -436,54 +436,50 @@
     below_in = 1.0 - last_row.astype(F32)
 
     def line(t, k, value):
-        keep = right * below_in if k >= 6 else right
+        keep = right * below_in if k == 4 else right
         even = activate(value[:Q].astype(F32), terms) * keep
         odd = activate(value[Q:].astype(F32), terms) * keep
         act[t, k, :, 0:C2] = even.astype(BF16)
         act[t, k, :, C2 : 2 * C2] = odd.astype(BF16)
         act[t, k, :, 2 * C2 :] = raised(even).astype(BF16)
 
-    def lines(t, carry):
-        for r in range(2):
-            line(t, r, above[t, r])
+    for t in range(FRAMES):
         for r in range(4):
-            line(t, 2 + r, inner[t, r])
-        for r in range(3):
-            line(t, 6 + r, below[t, r])
-        return carry
-
-    lax.fori_loop(0, FRAMES, lines, 0, unroll=True)
-    mask = own_entries(2 * Q, C3)
-    total = [jnp.zeros((1, C3), F32), jnp.zeros((1, C3), F32)]
+            line(t, r, inner[t, r])
+        line(t, 4, below[t])
     value = None
     for b in range(3):
-        left = jnp.concatenate([act[t, 2 * i + b] for t in range(FRAMES) for i in range(4)], axis=0)
+        left = jnp.concatenate([act[t, 2 * i + b] for t in range(FRAMES) for i in range(2)], axis=0)
         part = mm(left, reduce[b * 3 * C2 : (b + 1) * 3 * C2, :])
         value = part if value is None else value + part
     rounded = value.astype(BF16)
-    level[...] = rounded.reshape(FRAMES, 4, Q, C3)
-    wide = rounded.astype(F32)
+    level[...] = rounded.reshape(FRAMES, 2, Q, C3)
     for t in range(FRAMES):
-        one, two = sums(wide[(4 * t + 1) * Q : (4 * t + 3) * Q], mask)
-        total[0] += one
-        total[1] += two
-    share[...] = jnp.broadcast_to(grouped(*total), share.shape)
-
-
-def third_level(inner, above, below, gathered, gain, shift, reduce, devices):
+        top[t] = rounded[2 * t * Q : (2 * t + 1) * Q]
+        bottom[t] = rounded[(2 * t + 1) * Q : (2 * t + 2) * Q]
+    one, two = sums(rounded.astype(F32), own_entries(FRAMES * 2 * Q, C3))
+    share[...] = jnp.broadcast_to(grouped(one, two), share.shape)
+
+
+def third_level(inner, below, gathered, gain, shift, reduce, devices):
     return pl.pallas_call(
         functools.partial(third_kernel, members=float(devices * FRAMES * 4 * 2 * OWN * (C2 // GROUPS))),
-        out_shape=(shape((FRAMES, 4, Q, C3), BF16), shape((devices, 128), F32)),
-        in_specs=[VMEM] * 7,
-        out_specs=(VMEM,) * 2,
-        scratch_shapes=[pltpu.VMEM((FRAMES, 10, Q, 3 * C2), BF16)],
+        out_shape=(
+            shape((FRAMES, 2, Q, C3), BF16),
+            shape((devices, 128), F32),
+            shape((FRAMES, Q, C3), BF16),
+            shape((FRAMES, Q, C3), BF16),
+        ),
+        in_specs=[VMEM] * 6,
+        out_specs=(VMEM,) * 4,
+        scratch_shapes=[pltpu.VMEM((FRAMES, 5, Q, 3 * C2), BF16)],
         compiler_params=params(12),
-        cost_estimate=cost(2e9, 8e6),
+        cost_estimate=cost(1e9, 8e6),
         name="third",
-    )(inner, above, below, gathered, gain.reshape(1, C2), shift.reshape(1, C2), reduce.reshape(9 * C2, C3))
-
-
-def last_kernel(level, gathered, gain, shift, table, result, act, *, members):
+    )(inner, below, gathered, gain.reshape(1, C2), shift.reshape(1, C2), reduce.reshape(9 * C2, C3))
+
+
+def last_kernel(level, above, below, gathered, gain, shift, table, result, act, *, members):
     first_row, last_row, first_col, last_col = position()
     terms = norm_terms(gathered, gain, shift, members)
     entry = lax.broadcasted_iota(jnp.int32, (Q, 1), 0)
@@ -497,7 +493,8 @@
                 keep = keep * above_in
             if i == 3:
                 keep = keep * below_in
-            v = activate(level[t, i].astype(F32), terms) * keep
+            value = above[t] if i == 0 else below[t] if i == 3 else level[t, i - 1]
+            v = activate(value.astype(F32), terms) * keep
             act[t, i, :, 0:C3] = lowered(v).astype(BF16)
             act[t, i, :, C3 : 2 * C3] = v.astype(BF16)
             act[t, i, :, 2 * C3 :] = raised(v).astype(BF16)
@@ -521,18 +518,18 @@
             result[t, i] = side[t * OUT : (t + 1) * OUT, at : at + OWN].astype(BF16)
 
 
-def last_level(level, gathered, gain, shift, table, devices):
+def last_level(level, above, below, gathered, gain, shift, table, devices):
     swapped = jnp.swapaxes(table, 3, 4).reshape(3, 9, OUT, C3)
     out = pl.pallas_call(
         functools.partial(last_kernel, members=float(devices * FRAMES * 2 * OWN * (C3 // GROUPS))),
         out_shape=shape((FRAMES, 2, OUT, OWN), BF16),
-        in_specs=[VMEM] * 5,
+        in_specs=[VMEM] * 7,
         out_specs=VMEM,
         scratch_shapes=[pltpu.VMEM((FRAMES, 4, Q, 3 * C3), BF16)],
         compiler_params=params(10),
         cost_estimate=cost(1e9, 4e6),
         name="last",
-    )(level, gathered, gain.reshape(1, C3), shift.reshape(1, C3), swapped)
+    )(level, above, below, gathered, gain.reshape(1, C3), shift.reshape(1, C3), swapped)
     return jnp.swapaxes(out, 2, 3)
 
 
@@ -564,16 +561,16 @@
     inner, stats = middle(planes, table)
     outer, share, up, down = edges(above, below, table, inner, stats, devices)
     above, below = from_both(down, up, "rows")
-    hidden, share, up, down = second_level(
+    hidden, share, up = second_level(
         inner, outer, above, below, everywhere(share), gain_first, shift_first,
         first_reduce_kernel, conv_second, devices,
     )
-    above, below = from_both(down, up, "rows")
-    level, share = third_level(
-        hidden, above, below, everywhere(share), gain_second, shift_second,
-        second_reduce_kernel, devices,
+    below = lax.ppermute(up, "rows", backward("rows"))
+    level, share, top, bottom = third_level(
+        hidden, below, everywhere(share), gain_second, shift_second, second_reduce_kernel, devices
     )
-    return last_level(level, everywhere(share), gain_third, shift_third, conv_last, devices)
+    above, below = from_both(bottom, top, "rows")
+    return last_level(level, above, below, everywhere(share), gain_third, shift_third, conv_last, devices)
 
 
 def solution(mesh):

time: 104 us -> 108 us (1.038)
  blocking collectives: 62.8 us -> 22.5 us
  starting transfers between devices: 16.7 us -> 44.2 us
  waiting for transfers between devices: 2.28 us -> 15.1 us
  local copies, waits for them, and re-layouts: 2.55 us -> 6.29 us
    all_to_all x3 -> x1, blocking collectives: 62.8 us -> 22.5 us  [everywhere(): return lax.all_to_all(share, AXES, 0, 0, tiled=True)]
    all_to_all x0 -> x2, starting transfers between devices: none -> 15 us  [everywhere(): return lax.all_to_all(share, AXES, 0, 0, tiled=True)]
    ppermute x4, waiting for transfers between devices: 0.01 us -> 6.76 us  [from_both(): lax.ppermute(last, axis, forward(axis))]
    ppermute x0 -> x1, starting transfers between devices: none -> 6.72 us  [shards(): below = lax.ppermute(up, 'rows', backward('rows'))]
    ppermute x4, starting transfers between devices: 12.2 us -> 16.8 us  [from_both(): lax.ppermute(first, axis, backward(axis))]
    ppermute x0 -> x1, waiting for transfers between devices: none -> 3.93 us  [shards(): below = lax.ppermute(up, 'rows', backward('rows'))]
    unnamed x26 -> x30, local copies, waits for them, and re-layouts: 2.55 us -> 6.29 us
    all_to_all x0 -> x2, waiting for transfers between devices: none -> 2.15 us  [everywhere(): return lax.all_to_all(share, AXES, 0, 0, tiled=True)]
  transfers between devices with their start and end apart: 8 -> 11, of which waited for: 1 -> 4; matrix products, arithmetic and copies ran while one was open for 0% -> 0% of each run, Pallas kernels for 6% -> 5%
where the time goes in v4:
time: 108 us
  starting transfers between devices  44.2 us (41%)
  blocking collectives  22.5 us (21%)
  Pallas kernels  19.5 us (18%)
  waiting for transfers between devices  15.1 us (14%)
  local copies, waits for them, and re-layouts  6.29 us (6%)
    all_to_all x1, blocking collectives, everywhere(): return lax.all_to_all(share, AXES, 0, 0, tiled=True)  22.5 us
    ppermute x4, starting transfers between devices, from_both(): lax.ppermute(first, axis, backward(axis))  16.8 us
    all_to_all x2, starting transfers between devices, everywhere(): return lax.all_to_all(share, AXES, 0, 0, tiled=True)  15 us
    pallas_call x1, Pallas kernels, second_level(): pl.pallas_call(functools.partial(second_kernel, members=float(devices * F...  7.49 us
    ppermute x4, waiting for transfers between devices, from_both(): lax.ppermute(last, axis, forward(axis))  6.76 us
    ppermute x1, starting transfers between devices, shards(): below = lax.ppermute(up, 'rows', backward('rows'))  6.72 us
    unnamed x30, local copies, waits for them, and re-layouts  6.29 us
    ppermute x4, starting transfers between devices, from_both(): lax.ppermute(last, axis, forward(axis))  5.62 us
  transfers between devices with their start and end apart: 11, of which 4 were waited for; matrix products, arithmetic and copies ran while one was open for 0% of the time, Pallas kernels for 5%

profile of v4, /device:TPU:1, one launch (start us, length us, event | category | flops | bytes accessed | tf_op | source)
XLA Modules:
  0.0 107.8 jit_solution(1402603972893969557)
XLA Ops:
  0.0 1.3 %copy-done = bf16[4,8,160,128]{3,2,1,0:T(8,128)(2,1)S(1)} copy-done((bf16[4,8,160,128]{3,2,1,0:T(8,128)(2,1)S(1)}, bf16[4,8,160,128]{3,2,1,0:T(8,128)(2,1)}, u32[]{:S(2)}) %copy-start) | copy-done | bytes 1310744
  1.4 2.6 %collective-permute-start = (bf16[32,16,128]{2,1,0:T(8,128)(2,1)S(1)}, bf16[32,16,128]{2,1,0:T(8,128)(2,1)S(1)}, u32[]{:S(2)}, u32[]{:S(2)}) collective-permute-start(bf16[32,16,128]{2,1,0:T(8,128)(2,1)S(1)} %get-tuple-element.23), channel_id=1, source_target_pairs={{0,1},{1,2},{2,3},{3,4},{4,5},{5,6},{6,7},{7,0},{8,9},{9,10},{10,1... | collective-permute-start | bytes 393224 | tf_op jit(solution)/shard_map/ppermute | solution.py:545
  4.6 1.2 %copy-done.5 = bf16[3,3,3,128,128]{4,3,2,1,0:T(8,128)(2,1)S(1)} copy-done((bf16[3,3,3,128,128]{4,3,2,1,0:T(8,128)(2,1)S(1)}, bf16[3,3,3,128,128]{4,3,2,1,0:T(8,128)(2,1)}, u32[]{:S(2)}) %copy-start.5) | copy-done | bytes 884760
  6.4 2.3 %collective-permute-done.1.right = bf16[32,16,128]{2,1,0:T(8,128)(2,1)S(1)} collective-permute-done((bf16[32,16,128]{2,1,0:T(8,128)(2,1)S(1)}, bf16[32,16,128]{2,1,0:T(8,128)(2,1)S(1)}, u32[]{:S(2)}, u32[]{:S(2)}) %collective-permute-start.1) | collective-permute-done | bytes 131104 | tf_op jit(solution)/shard_map/ppermute | solution.py:545
  9.3 1.4 %collective-permute-start.2 = (bf16[4,48,512]{2,1,0:T(8,128)(2,1)S(1)}, bf16[4,48,512]{2,1,0:T(8,128)(2,1)S(1)}, u32[]{:S(2)}, u32[]{:S(2)}) collective-permute-start(bf16[4,48,512]{2,1,0:T(8,128)(2,1)S(1)} %get-tuple-element.27), channel_id=1, source_target_pairs={{0,8},{8,16},{16,24},{24,32},{32,40},{40,48},{48,56},{56,64},{64,7... | collective-permute-start | bytes 589832 | tf_op jit(solution)/shard_map/ppermute | solution.py:545
  10.7 6.5 %collective-permute-start.3 = (bf16[4,48,512]{2,1,0:T(8,128)(2,1)S(1)}, bf16[4,48,512]{2,1,0:T(8,128)(2,1)S(1)}, u32[]{:S(2)}, u32[]{:S(2)}) collective-permute-start(bf16[4,48,512]{2,1,0:T(8,128)(2,1)S(1)} %get-tuple-element.28), channel_id=1, source_target_pairs={{8,0},{16,8},{24,16},{32,24},{40,32},{48,40},{56,48},{64,56},{72,6... | collective-permute-start | bytes 589832 | tf_op jit(solution)/shard_map/ppermute | solution.py:545
  17.2 5.3 %middle.1 = (f32[4,8,96,256]{3,2,1,0:T(8,128)S(1)}, f32[8,256]{1,0:T(8,128)S(1)}) custom-call(bf16[4,8,48,768]{3,2,1,0:T(8,128)(2,1)S(1)} %get-tuple-element.25.planes, bf16[7680,256]{1,0:T(8,128)(2,1)S(1)} %weights.1.table), custom_call_target="tpu_custom_call" | custom-call | flops 6000000000 | bytes 10000000 | tf_op jit(solution)/shard_map/middle/pallas_call | solution.py:185
  22.5 0.9 edges.1
  23.4 4.5 %collective-permute-start.5 = (bf16[4,3,96,256]{3,2,1,0:T(8,128)(2,1)S(1)}, bf16[4,3,96,256]{3,2,1,0:T(8,128)(2,1)S(1)}, u32[]{:S(2)}, u32[]{:S(2)}) collective-permute-start(bf16[4,3,96,256]{3,2,1,0:T(8,128)(2,1)S(1)} %get-tuple-element.32), channel_id=1, source_target_pairs={{8,0},{16,8},{24,16},{32,24},{40,32},{48,40},{56,48},{64,56},{72,6... | collective-permute-start | bytes 1769480 | tf_op jit(solution)/shard_map/ppermute | solution.py:545
  27.9 22.5 %all_to_all.33 = f32[256,1,128]{2,1,0:T(1,128)S(1)} all-to-all(f32[256,1,128]{2,1,0:T(1,128)S(1)} %bitcast.34), channel_id=1, replica_groups=mesh['rows'=32,'cols'=8] {'rows','cols'}, dimensions={0} | all-to-all | bytes 262144 | tf_op jit(solution)/shard_map/all_to_all | solution.py:549
  50.5 7.5 %second.1 = (f32[4,4,96,256]{3,2,1,0:T(8,128)S(1)}, f32[256,128]{1,0:T(8,128)}, bf16[4,96,256]{2,1,0:T(8,128)(2,1)S(1)}) custom-call(f32[4,8,96,256]{3,2,1,0:T(8,128)S(1)} %get-tuple-element.26.inner, f32[4,2,96,256]{3,2,1,0:T(8,128)S(1)} %get-tuple-element.30.outer, bf16[4,2,96,256]{3,2,1,0:T(8,128)(2,1)S(1)} %collective-permute-done.4.above, ...), custom_call_target="tpu_custom_call" | custom-call | flops 6000000000 | bytes 12000000 | tf_op jit(solution)/shard_map/second/pallas_call | solution.py:407
  58.0 1.2 %copy-done.3 = f32[4,4,96,256]{3,2,1,0:T(8,128)} copy-done((f32[4,4,96,256]{3,2,1,0:T(8,128)}, f32[4,4,96,256]{3,2,1,0:T(8,128)S(1)}, u32[]{:S(2)}) %copy-start.3) | copy-done | bytes 1572888
  59.2 5.8 %all-to-all-start.1 = ((f32[256,1,128]{2,1,0:T(1,128)}), f32[256,1,128]{2,1,0:T(1,128)S(1)}, u32[]{:S(2)}, u32[]{:S(2)}) async-start(f32[256,1,128]{2,1,0:T(1,128)} %bitcast.10), calls=%async_computation.1 | async-start | bytes 262144 | tf_op jit(solution)/shard_map/all_to_all | solution.py:549
  65.0 6.7 %collective-permute-start.6 = (bf16[4,96,256]{2,1,0:T(8,128)(2,1)S(1)}, bf16[4,96,256]{2,1,0:T(8,128)(2,1)S(1)}, u32[]{:S(2)}, u32[]{:S(2)}) collective-permute-start(bf16[4,96,256]{2,1,0:T(8,128)(2,1)S(1)} %get-tuple-element.35), channel_id=1, source_target_pairs={{8,0},{16,8},{24,16},{32,24},{40,32},{48,40},{56,48},{64,56},{72,6... | collective-permute-start | bytes 589832 | tf_op jit(solution)/shard_map/ppermute | solution.py:568
  71.7 3.9 %collective-permute-done.6.below = bf16[4,96,256]{2,1,0:T(8,128)(2,1)S(1)} collective-permute-done((bf16[4,96,256]{2,1,0:T(8,128)(2,1)S(1)}, bf16[4,96,256]{2,1,0:T(8,128)(2,1)S(1)}, u32[]{:S(2)}, u32[]{:S(2)}) %collective-permute-start.6) | collective-permute-done | bytes 196640 | tf_op jit(solution)/shard_map/ppermute | solution.py:568
  75.7 2.1 %all-to-all-done.1 = f32[256,1,128]{2,1,0:T(1,128)S(1)} async-done(((f32[256,1,128]{2,1,0:T(1,128)}), f32[256,1,128]{2,1,0:T(1,128)S(1)}, u32[]{:S(2)}, u32[]{:S(2)}) %all-to-all-start.1) | async-done | bytes 131104 | tf_op jit(solution)/shard_map/all_to_all | solution.py:549
  77.8 1.4 %copy-done.4 = f32[4,4,96,256]{3,2,1,0:T(8,128)S(1)} copy-done((f32[4,4,96,256]{3,2,1,0:T(8,128)S(1)}, f32[4,4,96,256]{3,2,1,0:T(8,128)}, u32[]{:S(2)}) %copy-start.4) | copy-done | bytes 1572888
  79.2 2.3 %third.1 = (bf16[4,2,48,512]{3,2,1,0:T(8,128)(2,1)S(1)}, f32[256,128]{1,0:T(8,128)}, bf16[4,48,512]{2,1,0:T(8,128)(2,1)S(1)}, bf16[4,48,512]{2,1,0:T(8,128)(2,1)S(1)}) custom-call(f32[4,4,96,256]{3,2,1,0:T(8,128)S(1)} %copy-done.4, bf16[4,96,256]{2,1,0:T(8,128)(2,1)S(1)} %collective-permute-done.6.below, f32[256,128]{1,0:T(8,128)S(1)} %bitcast.31, ...), custom_call_target="tpu_custom_call" | custom-call | flops 1000000000 | bytes 8000000 | tf_op jit(solution)/shard_map/third/pallas_call | solution.py:465
  81.6 9.2 %all-to-all-start.2 = ((f32[256,1,128]{2,1,0:T(1,128)}), f32[256,1,128]{2,1,0:T(1,128)S(1)}, u32[]{:S(2)}, u32[]{:S(2)}) async-start(f32[256,1,128]{2,1,0:T(1,128)} %bitcast.16), calls=%async_computation.2 | async-start | bytes 262144 | tf_op jit(solution)/shard_map/all_to_all | solution.py:549
  90.8 1.6 %collective-permute-start.7 = (bf16[4,48,512]{2,1,0:T(8,128)(2,1)S(1)}, bf16[4,48,512]{2,1,0:T(8,128)(2,1)S(1)}, u32[]{:S(2)}, u32[]{:S(2)}) collective-permute-start(bf16[4,48,512]{2,1,0:T(8,128)(2,1)S(1)} %get-tuple-element.38), channel_id=1, source_target_pairs={{0,8},{8,16},{16,24},{24,32},{32,40},{40,48},{48,56},{56,64},{64,7... | collective-permute-start | bytes 589832 | tf_op jit(solution)/shard_map/ppermute | solution.py:545
  92.3 5.2 %collective-permute-start.8 = (bf16[4,48,512]{2,1,0:T(8,128)(2,1)S(1)}, bf16[4,48,512]{2,1,0:T(8,128)(2,1)S(1)}, u32[]{:S(2)}, u32[]{:S(2)}) collective-permute-start(bf16[4,48,512]{2,1,0:T(8,128)(2,1)S(1)} %get-tuple-element.39), channel_id=1, source_target_pairs={{8,0},{16,8},{24,16},{32,24},{40,32},{48,40},{56,48},{64,56},{72,6... | collective-permute-start | bytes 589832 | tf_op jit(solution)/shard_map/ppermute | solution.py:545
  97.6 6.7 %collective-permute-done.7.above = bf16[4,48,512]{2,1,0:T(8,128)(2,1)S(1)} collective-permute-done((bf16[4,48,512]{2,1,0:T(8,128)(2,1)S(1)}, bf16[4,48,512]{2,1,0:T(8,128)(2,1)S(1)}, u32[]{:S(2)}, u32[]{:S(2)}) %collective-permute-start.7) | collective-permute-done | bytes 196640 | tf_op jit(solution)/shard_map/ppermute | solution.py:545
  104.4 1.2 %copy-done.9 = bf16[3,3,3,512,32]{3,4,2,1,0:T(8,128)(2,1)S(1)} copy-done((bf16[3,3,3,512,32]{3,4,2,1,0:T(8,128)(2,1)S(1)}, bf16[3,3,3,512,32]{3,4,2,1,0:T(8,128)(2,1)}, u32[]{:S(2)}) %copy-start.9) | copy-done | bytes 884760
  105.5 2.2 %last.1 = bf16[4,2,32,40]{3,2,1,0:T(8,128)(2,1)} custom-call(bf16[4,2,48,512]{3,2,1,0:T(8,128)(2,1)S(1)} %get-tuple-element.37.level, bf16[4,48,512]{2,1,0:T(8,128)(2,1)S(1)} %collective-permute-done.7.above, bf16[4,48,512]{2,1,0:T(8,128)(2,1)S(1)} %collective-permute-done.8.below, f32[256,128]{1,0:T(8,128)S(1)} %bitcast.32, f32[1,512]{1,0:T(1,128)S(1)} %bitcast.40, ...), custom_call_target="tpu_custom_call" | custom-call | flops 1000000000 | bytes 4000000 | tf_op jit(solution)/shard_map/last/pallas_call | solution.py:523
  (37 shorter events, 2.0 us)
Async XLA Ops:
  0.0 1.3 %copy-start = (bf16[4,8,160,128]{3,2,1,0:T(8,128)(2,1)S(1)}, bf16[4,8,160,128]{3,2,1,0:T(8,128)(2,1)}, u32[]{:S(2)}) copy-start(bf16[4,8,160,128]{3,2,1,0:T(8,128)(2,1)} %param.12) | copy-start | bytes 3932164
  1.4 5.0 %collective-permute-start = (bf16[32,16,128]{2,1,0:T(8,128)(2,1)S(1)}, bf16[32,16,128]{2,1,0:T(8,128)(2,1)S(1)}, u32[]{:S(2)}, u32[]{:S(2)}) collective-permute-start(bf16[32,16,128]{2,1,0:T(8,128)(2,1)S(1)} %get-tuple-element.23), channel_id=1, source_target_pairs={{0,1},{1,2},{2,3},{3,4},{4,5},{5,6},{6,7},{7,0},{8,9},{9,10},{10,1... | collective-permute-start | bytes 393224 | tf_op jit(solution)/shard_map/ppermute | solution.py:545
  4.0 4.7 %collective-permute-start.1 = (bf16[32,16,128]{2,1,0:T(8,128)(2,1)S(1)}, bf16[32,16,128]{2,1,0:T(8,128)(2,1)S(1)}, u32[]{:S(2)}, u32[]{:S(2)}) collective-permute-start(bf16[32,16,128]{2,1,0:T(8,128)(2,1)S(1)} %get-tuple-element.24), channel_id=1, source_target_pairs={{1,0},{2,1},{3,2},{4,3},{5,4},{6,5},{7,6},{0,7},{9,8},{10,9},{11,1... | collective-permute-start | bytes 393224 | tf_op jit(solution)/shard_map/ppermute | solution.py:545
  5.8 2.9 %copy-start.1 = (bf16[4,8,160,128]{3,2,1,0:T(8,128)(2,1)S(1)}, bf16[4,8,160,128]{3,2,1,0:T(8,128)(2,1)}, u32[]{:S(2)}) copy-start(bf16[4,8,160,128]{3,2,1,0:T(8,128)(2,1)} %param.12) | copy-start | bytes 3932164
  9.3 13.2 %collective-permute-start.2 = (bf16[4,48,512]{2,1,0:T(8,128)(2,1)S(1)}, bf16[4,48,512]{2,1,0:T(8,128)(2,1)S(1)}, u32[]{:S(2)}, u32[]{:S(2)}) collective-permute-start(bf16[4,48,512]{2,1,0:T(8,128)(2,1)S(1)} %get-tuple-element.27), channel_id=1, source_target_pairs={{0,8},{8,16},{16,24},{24,32},{32,40},{40,48},{48,56},{56,64},{64,7... | collective-permute-start | bytes 589832 | tf_op jit(solution)/shard_map/ppermute | solution.py:545
  10.7 11.7 %collective-permute-start.3 = (bf16[4,48,512]{2,1,0:T(8,128)(2,1)S(1)}, bf16[4,48,512]{2,1,0:T(8,128)(2,1)S(1)}, u32[]{:S(2)}, u32[]{:S(2)}) collective-permute-start(bf16[4,48,512]{2,1,0:T(8,128)(2,1)S(1)} %get-tuple-element.28), channel_id=1, source_target_pairs={{8,0},{16,8},{24,16},{32,24},{40,32},{48,40},{56,48},{64,56},{72,6... | collective-permute-start | bytes 589832 | tf_op jit(solution)/shard_map/ppermute | solution.py:545
  22.5 27.9 %copy-start.8 = (bf16[3,3,3,256,256]{4,3,2,1,0:T(8,128)(2,1)S(1)}, bf16[3,3,3,256,256]{4,3,2,1,0:T(8,128)(2,1)}, u32[]{:S(2)}) copy-start(bf16[3,3,3,256,256]{4,3,2,1,0:T(8,128)(2,1)} %param.15) | copy-start | bytes 10616836
  22.5 27.9 %copy-start.10 = (bf16[3,3,128,256]{3,2,1,0:T(8,128)(2,1)S(1)}, bf16[3,3,128,256]{3,2,1,0:T(8,128)(2,1)}, u32[]{:S(2)}) copy-start(bf16[3,3,128,256]{3,2,1,0:T(8,128)(2,1)} %param.14) | copy-start | bytes 1769476
  22.5 27.9 %copy-start.13 = (f32[128]{0:T(128)S(1)}, f32[128]{0:T(128)}, u32[]{:S(2)}) copy-start(f32[128]{0:T(128)} %param.18) | copy-start | bytes 1540
  22.5 27.9 %copy-start.14 = (f32[128]{0:T(128)S(1)}, f32[128]{0:T(128)}, u32[]{:S(2)}) copy-start(f32[128]{0:T(128)} %param.19) | copy-start | bytes 1540
  23.4 27.0 %collective-permute-start.5 = (bf16[4,3,96,256]{3,2,1,0:T(8,128)(2,1)S(1)}, bf16[4,3,96,256]{3,2,1,0:T(8,128)(2,1)S(1)}, u32[]{:S(2)}, u32[]{:S(2)}) collective-permute-start(bf16[4,3,96,256]{3,2,1,0:T(8,128)(2,1)S(1)} %get-tuple-element.32), channel_id=1, source_target_pairs={{8,0},{16,8},{24,16},{32,24},{40,32},{48,40},{56,48},{64,56},{72,6... | collective-permute-start | bytes 1769480 | tf_op jit(solution)/shard_map/ppermute | solution.py:545
  27.9 22.5 %collective-permute-start.4 = (bf16[4,2,96,256]{3,2,1,0:T(8,128)(2,1)S(1)}, bf16[4,2,96,256]{3,2,1,0:T(8,128)(2,1)S(1)}, u32[]{:S(2)}, u32[]{:S(2)}) collective-permute-start(bf16[4,2,96,256]{3,2,1,0:T(8,128)(2,1)S(1)} %get-tuple-element.31), channel_id=1, source_target_pairs={{0,8},{8,16},{16,24},{24,32},{32,40},{40,48},{48,56},{56,64},{64,7... | collective-permute-start | bytes 1179656 | tf_op jit(solution)/shard_map/ppermute | solution.py:545
  50.5 27.4 %copy-start.2 = (bf16[3,3,256,512]{3,2,1,0:T(8,128)(2,1)S(1)}, bf16[3,3,256,512]{3,2,1,0:T(8,128)(2,1)}, u32[]{:S(2)}) copy-start(bf16[3,3,256,512]{3,2,1,0:T(8,128)(2,1)} %param.16) | copy-start | bytes 7077892
  50.5 27.4 %copy-start.6 = (f32[256]{0:T(256)S(1)}, f32[256]{0:T(256)}, u32[]{:S(2)}) copy-start(f32[256]{0:T(256)} %param.20) | copy-start | bytes 3076
  50.5 27.4 %copy-start.7 = (f32[256]{0:T(256)S(1)}, f32[256]{0:T(256)}, u32[]{:S(2)}) copy-start(f32[256]{0:T(256)} %param.21) | copy-start | bytes 3076
  58.0 1.2 %copy-start.3 = (f32[4,4,96,256]{3,2,1,0:T(8,128)}, f32[4,4,96,256]{3,2,1,0:T(8,128)S(1)}, u32[]{:S(2)}) copy-start(f32[4,4,96,256]{3,2,1,0:T(8,128)S(1)} %get-tuple-element.34.inner) | copy-start | bytes 4718596
  59.2 45.2 %copy-start.11 = (f32[512]{0:T(512)S(1)}, f32[512]{0:T(512)}, u32[]{:S(2)}) copy-start(f32[512]{0:T(512)} %param.22) | copy-start | bytes 6148
  59.2 45.2 %copy-start.12 = (f32[512]{0:T(512)S(1)}, f32[512]{0:T(512)}, u32[]{:S(2)}) copy-start(f32[512]{0:T(512)} %param.23) | copy-start | bytes 6148
  59.2 18.7 %all-to-all-start.1 = ((f32[256,1,128]{2,1,0:T(1,128)}), f32[256,1,128]{2,1,0:T(1,128)S(1)}, u32[]{:S(2)}, u32[]{:S(2)}) async-start(f32[256,1,128]{2,1,0:T(1,128)} %bitcast.10), calls=%async_computation.1 | async-start | bytes 262144 | tf_op jit(solution)/shard_map/all_to_all | solution.py:549
  65.0 10.7 %collective-permute-start.6 = (bf16[4,96,256]{2,1,0:T(8,128)(2,1)S(1)}, bf16[4,96,256]{2,1,0:T(8,128)(2,1)S(1)}, u32[]{:S(2)}, u32[]{:S(2)}) collective-permute-start(bf16[4,96,256]{2,1,0:T(8,128)(2,1)S(1)} %get-tuple-element.35), channel_id=1, source_target_pairs={{8,0},{16,8},{24,16},{32,24},{40,32},{48,40},{56,48},{64,56},{72,6... | collective-permute-start | bytes 589832 | tf_op jit(solution)/shard_map/ppermute | solution.py:568
  77.8 1.4 %copy-start.4 = (f32[4,4,96,256]{3,2,1,0:T(8,128)S(1)}, f32[4,4,96,256]{3,2,1,0:T(8,128)}, u32[]{:S(2)}) copy-start(f32[4,4,96,256]{3,2,1,0:T(8,128)} %copy-done.3) | copy-start | bytes 4718596
  81.6 22.7 %all-to-all-start.2 = ((f32[256,1,128]{2,1,0:T(1,128)}), f32[256,1,128]{2,1,0:T(1,128)S(1)}, u32[]{:S(2)}, u32[]{:S(2)}) async-start(f32[256,1,128]{2,1,0:T(1,128)} %bitcast.16), calls=%async_computation.2 | async-start | bytes 262144 | tf_op jit(solution)/shard_map/all_to_all | solution.py:549
  90.8 13.6 %collective-permute-start.7 = (bf16[4,48,512]{2,1,0:T(8,128)(2,1)S(1)}, bf16[4,48,512]{2,1,0:T(8,128)(2,1)S(1)}, u32[]{:S(2)}, u32[]{:S(2)}) collective-permute-start(bf16[4,48,512]{2,1,0:T(8,128)(2,1)S(1)} %get-tuple-element.38), channel_id=1, source_target_pairs={{0,8},{8,16},{16,24},{24,32},{32,40},{40,48},{48,56},{56,64},{64,7... | collective-permute-start | bytes 589832 | tf_op jit(solution)/shard_map/ppermute | solution.py:545
  92.3 12.0 %collective-permute-start.8 = (bf16[4,48,512]{2,1,0:T(8,128)(2,1)S(1)}, bf16[4,48,512]{2,1,0:T(8,128)(2,1)S(1)}, u32[]{:S(2)}, u32[]{:S(2)}) collective-permute-start(bf16[4,48,512]{2,1,0:T(8,128)(2,1)S(1)} %get-tuple-element.39), channel_id=1, source_target_pairs={{8,0},{16,8},{24,16},{32,24},{40,32},{48,40},{56,48},{64,56},{72,6... | collective-permute-start | bytes 589832 | tf_op jit(solution)/shard_map/ppermute | solution.py:545
  (2 other events, 2.3 us)

commit v5 on v3

--- a/solution.py
+++ b/solution.py
@@ -18,6 +18,7 @@
 OWN = COLS // 4
 EDGE = 16
 LINE = 208
+K0, MINUS, K2, PAIR, ALL = range(5)
 AXES = ("rows", "cols")
 F32, BF16 = jnp.float32, jnp.bfloat16
 VMEM = pl.BlockSpec(memory_space=pltpu.VMEM)
@@ -51,8 +52,9 @@
         for e in range(3):
             taps = [first[((a * 3 + b) * 3 + e) * C1 : ((a * 3 + b) * 3 + e + 1) * C1, :] for a in range(3)]
             wide = [k.astype(F32) for k in taps]
-            pair = wide[0] + wide[1]
-            for s, k in enumerate(taps + [pair.astype(BF16), (pair + wide[2]).astype(BF16)]):
+            pair, ends = wide[0] + wide[1], wide[0] + wide[2]
+            made = [v.astype(BF16) for v in (ends - wide[1], pair, pair + wide[2])]
+            for s, k in enumerate([taps[0], made[0], taps[2], made[1], made[2]]):
                 base = s * 12 * C1 + b * 4 * C1
                 one[base + e * C1 : base + (e + 1) * C1, 0:C1] = k
                 one[base + (e + 1) * C1 : base + (e + 2) * C1, C1 : 2 * C1] = k
@@ -104,8 +106,6 @@
     left_in = 1.0 - first_col.astype(F32)
     right_in = 1.0 - last_col.astype(F32)
     for t in range(FRAMES):
-        planes[t, 0] = jnp.zeros((Q, 6 * C1), BF16)
-        planes[t, ROWS + 1] = jnp.zeros((Q, 6 * C1), BF16)
 
         def step(r, carry, t=t):
             i = t * ROWS + r
@@ -114,12 +114,12 @@
             line[i, EDGE + COLS : 2 * EDGE + COLS, :] = right[i].astype(F32) * right_in
             line[i, 2 * EDGE + COLS : LINE, :] = jnp.zeros((LINE - 2 * EDGE - COLS, C1), F32)
             for k in range(6):
-                planes[t, 1 + r, :, k * C1 : (k + 1) * C1] = line[i, pl.ds(7 + k, Q, stride=4), :].astype(BF16)
+                planes[t, r, :, k * C1 : (k + 1) * C1] = line[i, pl.ds(7 + k, Q, stride=4), :].astype(BF16)
             return carry
 
         lax.fori_loop(0, ROWS, step, 0, unroll=True)
-        top[t] = planes[t, 1, :, C1 : 5 * C1]
-        bottom[t] = planes[t, ROWS, :, C1 : 5 * C1]
+        top[t] = planes[t, 0, :, C1 : 5 * C1]
+        bottom[t] = planes[t, ROWS - 1, :, C1 : 5 * C1]
 
 
 def planes_of(left, own, right):
@@ -127,7 +127,7 @@
     return pl.pallas_call(
         planes_kernel,
         out_shape=(
-            shape((FRAMES, ROWS + 2, Q, 6 * C1), BF16),
+            shape((FRAMES, ROWS, Q, 6 * C1), BF16),
             shape((FRAMES, Q, 4 * C1), BF16),
             shape((FRAMES, Q, 4 * C1), BF16),
         ),
@@ -150,38 +150,42 @@
     return jnp.sum(kept, axis=0, keepdims=True), jnp.sum(kept * kept, axis=0, keepdims=True)
 
 
-def frames_conv(frame, weight, store):
-    store(0, mm(frame(0), weight(4)))
-    store(1, mm(frame(0), weight(3)) + mm(frame(1), weight(2)))
-    for t in range(2, FRAMES):
-        store(t, mm(frame(t - 2), weight(0)) + mm(frame(t - 1), weight(1)) + mm(frame(t), weight(2)))
-
-
-def table_of(ref, rows):
-    return lambda s: ref[s * rows : (s + 1) * rows, :]
-
-
-def middle_kernel(planes, table, hidden, stats):
-    rows = ROWS * Q
-    mask = own_entries(2 * (rows - 2 * Q), 2 * C1)
+def mixed(one):
+    return one[0] - one[2], one[1] + one[2], one[2] - one[1], one[1] - one[3]
+
+
+def causal(product, frames, mix):
+    yield product(frames[0], ALL)
+    yield product(frames[0], PAIR) + product(frames[1], K2)
+    plus, minus = product(mix[1], ALL), product(mix[2], MINUS)
+    yield product(mix[0], K0) + 0.5 * (plus + minus)
+    yield 0.5 * (plus - minus) - product(mix[3], K2)
+
+
+def middle_kernel(planes, table, hidden, stats, mix):
+    mask = own_entries((ROWS - 2) * Q, 2 * C1)
     stats[...] = jnp.zeros(stats.shape, F32)
-
-    def frame(t):
-        parts = []
-        for b in range(3):
-            block = planes[t, b : b + ROWS].reshape(rows, 6 * C1)
-            parts.append(jnp.concatenate([block[:, : 4 * C1], block[:, 2 * C1 :]], axis=0))
-        return jnp.concatenate(parts, axis=1)
-
-    def store(t, value):
-        hidden[t, :, 0:Q, :] = value[:rows].reshape(ROWS, Q, 2 * C1)
-        hidden[t, :, Q : 2 * Q, :] = value[rows:].reshape(ROWS, Q, 2 * C1)
-        inside = jnp.concatenate([value[Q : rows - Q], value[rows + Q : 2 * rows - Q]], axis=0)
-        one, two = sums(inside, mask)
-        stats[0:1, :] += one
-        stats[1:2, :] += two
-
-    frames_conv(frame, table_of(table, 12 * C1), store)
+    for i, value in enumerate(mixed([planes[t] for t in range(FRAMES)])):
+        mix[i] = value
+    for odd in range(2):
+        lanes = slice(2 * C1 * odd, 2 * C1 * odd + 4 * C1)
+        at = slice(odd * Q, (odd + 1) * Q)
+
+        def product(v, s):
+            def tap(b):
+                low, high = max(b - 1, 0), ROWS + min(b - 1, 0)
+                left = v[0][v[1], low:high, :, lanes].reshape((high - low) * Q, 4 * C1)
+                base = (3 * s + b) * 4 * C1
+                return mm(left, table[base : base + 4 * C1, :])
+
+            up, here, down = tap(0), tap(1), tap(2)
+            return jnp.concatenate([here[:Q] + down[:Q], here[Q:-Q] + up[:-Q] + down[Q:], here[-Q:] + up[-Q:]], axis=0)
+
+        for t, value in enumerate(causal(product, [(planes, t) for t in range(FRAMES)], [(mix, i) for i in range(4)])):
+            hidden[t, :, at, :] = value.reshape(ROWS, Q, 2 * C1)
+            one, two = sums(value[Q:-Q], mask)
+            stats[0:1, :] += one
+            stats[1:2, :] += two
 
 
 def middle(planes, table):
@@ -193,6 +197,7 @@
         ),
         in_specs=[VMEM] * 2,
         out_specs=(VMEM,) * 2,
+        scratch_shapes=[pltpu.VMEM((4, ROWS, Q, 6 * C1), BF16)],
         compiler_params=params(12),
         cost_estimate=cost(6e9, 10e6),
         name="middle",
@@ -256,14 +261,11 @@
             odd = jnp.concatenate([whole[:, C1:], last], axis=1)
             lines.append(jnp.concatenate([even, odd], axis=0))
 
-        def part(s, frames):
+        def product(v, s):
             base = s * 12 * C1 + b * 4 * C1
-            value = mm(jnp.concatenate([lines[t] for t in frames], axis=0), table[base : base + 4 * C1, :])
-            return [value[i * 2 * Q : (i + 1) * 2 * Q] for i in range(len(frames))]
-
-        zero, one, two = part(0, (0, 1)), part(1, (1, 2)), part(2, (1, 2, 3))
-        pair, all_three = part(3, (0,)), part(4, (0,))
-        extra = [all_three[0], pair[0] + two[0], zero[0] + one[0] + two[1], zero[1] + one[1] + two[2]]
+            return mm(v, table[base : base + 4 * C1, :])
+
+        extra = list(causal(product, lines, mixed(lines)))
         for t in range(FRAMES):
             value = inner[t, side * (ROWS - 1)] + extra[t]
             hidden[t, side] = value
@@ -322,7 +324,7 @@
 
 def second_kernel(
     inner, outer, above, below, gathered, gain, shift, reduce, second,
-    hidden, share, up, down, act, lev, summed, *, members,
+    hidden, share, up, down, act, lev, mix, made, *, members,
 ):
     first_row, last_row, first_col, last_col = position()
     terms = twice(norm_terms(gathered, gain, shift, members))
@@ -376,9 +378,10 @@
 
     def add(i, carry):
         at = pl.ds(pl.multiple_of(i * C2, C2), C2)
-        pair = second[0, at, :].astype(F32) + second[1, at, :].astype(F32)
-        summed[0, at, :] = pair.astype(BF16)
-        summed[1, at, :] = (pair + second[2, at, :].astype(F32)).astype(BF16)
+        k0, k1, k2 = (second[a, at, :].astype(F32) for a in range(3))
+        made[0, at, :] = (k0 - k1 + k2).astype(BF16)
+        made[1, at, :] = (k0 + k1).astype(BF16)
+        made[2, at, :] = (k0 + k1 + k2).astype(BF16)
         return carry
 
     lax.fori_loop(0, 9, add, 0, unroll=True)
@@ -386,8 +389,13 @@
     mask = own_entries(rows, C2)
     total = [jnp.zeros((1, C2), F32), jnp.zeros((1, C2), F32)]
 
-    def frame(t):
-        return jnp.concatenate([lev[t, b : b + 4].reshape(rows, 3 * C2) for b in range(3)], axis=1)
+    for i, value in enumerate(mixed([lev[t] for t in range(FRAMES)])):
+        mix[i] = value
+    tables = {K0: second.at[0], MINUS: made.at[0], K2: second.at[2], PAIR: made.at[1], ALL: made.at[2]}
+
+    def product(v, s):
+        left = jnp.concatenate([v[0][v[1], b : b + 4].reshape(rows, 3 * C2) for b in range(3)], axis=1)
+        return mm(left, tables[s][...])
 
     def store(t, value):
         full = value.reshape(4, 2 * Q, C2)
@@ -398,7 +406,8 @@
         total[0] += one
         total[1] += two
 
-    frames_conv(frame, lambda s: second[s] if s < 3 else summed[s - 3], store)
+    for t, value in enumerate(causal(product, [(lev, t) for t in range(FRAMES)], [(mix, i) for i in range(4)])):
+        store(t, value)
     share[...] = jnp.broadcast_to(grouped(*total), share.shape)
 
 
@@ -416,9 +425,10 @@
         scratch_shapes=[
             pltpu.VMEM((FRAMES, 14, 2 * Q, 3 * C1), BF16),
             pltpu.VMEM((FRAMES, 6, 2 * Q, 3 * C2), BF16),
-            pltpu.VMEM((2, 9 * C2, C2), BF16),
+            pltpu.VMEM((4, 6, 2 * Q, 3 * C2), BF16),
+            pltpu.VMEM((3, 9 * C2, C2), BF16),
         ],
-        compiler_params=params(20),
+        compiler_params=params(24),
         cost_estimate=cost(6e9, 12e6),
         name="second",
     )(

time: 104 us -> 104 us (level)
  Pallas kernels: 19.5 us -> 17.6 us
    pallas_call x1, Pallas kernels: 5.66 us -> 4.35 us  [middle(): pl.pallas_call(middle_kernel, out_shape=(shape((FRAMES, ROWS, 2 * Q, 2 *...]
  transfers between devices with their start and end apart: 8 -> 8, of which waited for: 1 -> 2; matrix products, arithmetic and copies ran while one was open for 0% -> 0% of each run, Pallas kernels for 6% -> 5%
where the time goes in v5:
time: 104 us; the launch traced here: 103 us
  blocking collectives  62.8 us (60%)
  Pallas kernels  17.6 us (17%)
  starting transfers between devices  17.4 us (17%)
  waiting for transfers between devices  2.99 us (3%)
  local copies, waits for them, and re-layouts  2.54 us (2%)
    all_to_all x3, blocking collectives, everywhere(): return lax.all_to_all(share, AXES, 0, 0, tiled=True)  62.8 us
    ppermute x4, starting transfers between devices, from_both(): lax.ppermute(first, axis, backward(axis))  12.9 us
    pallas_call x1, Pallas kernels, second_level(): pl.pallas_call(functools.partial(second_kernel, members=float(devices * F...  6.24 us
    ppermute x4, starting transfers between devices, from_both(): lax.ppermute(last, axis, forward(axis))  4.51 us
    pallas_call x1, Pallas kernels, middle(): pl.pallas_call(middle_kernel, out_shape=(shape((FRAMES, ROWS, 2 * Q, 2 *...  4.35 us
    pallas_call x1, Pallas kernels, third_level(): pl.pallas_call(functools.partial(third_kernel, members=float(devices * FR...  2.6 us
    unnamed x26, local copies, waits for them, and re-layouts  2.54 us
    ppermute x4, waiting for transfers between devices, from_both(): lax.ppermute(first, axis, backward(axis))  2.27 us
  transfers between devices with their start and end apart: 8, of which 2 were waited for; matrix products, arithmetic and copies ran while one was open for 0% of the time, Pallas kernels for 5%

profile of v5, /device:TPU:1, one launch (start us, length us, event | category | flops | bytes accessed | tf_op | source)
XLA Modules:
  0.0 103.5 jit_solution(16670052517026434582)
XLA Ops:
  0.0 1.3 %copy-done = bf16[4,8,160,128]{3,2,1,0:T(8,128)(2,1)S(1)} copy-done((bf16[4,8,160,128]{3,2,1,0:T(8,128)(2,1)S(1)}, bf16[4,8,160,128]{3,2,1,0:T(8,128)(2,1)}, u32[]{:S(2)}) %copy-start) | copy-done | bytes 1310744
  1.4 2.6 %collective-permute-start = (bf16[32,16,128]{2,1,0:T(8,128)(2,1)S(1)}, bf16[32,16,128]{2,1,0:T(8,128)(2,1)S(1)}, u32[]{:S(2)}, u32[]{:S(2)}) collective-permute-start(bf16[32,16,128]{2,1,0:T(8,128)(2,1)S(1)} %get-tuple-element.22), channel_id=1, source_target_pairs={{0,1},{1,2},{2,3},{3,4},{4,5},{5,6},{6,7},{7,0},{8,9},{9,10},{10,1... | collective-permute-start | bytes 393224 | tf_op jit(solution)/shard_map/ppermute | solution.py:558
  4.0 0.7 collective-permute-start.1
  4.6 1.2 %copy-done.2 = bf16[3,3,3,128,128]{4,3,2,1,0:T(8,128)(2,1)S(1)} copy-done((bf16[3,3,3,128,128]{4,3,2,1,0:T(8,128)(2,1)S(1)}, bf16[3,3,3,128,128]{4,3,2,1,0:T(8,128)(2,1)}, u32[]{:S(2)}) %copy-start.2) | copy-done | bytes 884760
  5.8 0.6 weights.1.table
  6.4 2.3 %collective-permute-done.1.right = bf16[32,16,128]{2,1,0:T(8,128)(2,1)S(1)} collective-permute-done((bf16[32,16,128]{2,1,0:T(8,128)(2,1)S(1)}, bf16[32,16,128]{2,1,0:T(8,128)(2,1)S(1)}, u32[]{:S(2)}, u32[]{:S(2)}) %collective-permute-start.1) | collective-permute-done | bytes 131104 | tf_op jit(solution)/shard_map/ppermute | solution.py:558
  8.7 0.6 planes.1
  9.3 1.4 %collective-permute-start.2 = (bf16[4,48,512]{2,1,0:T(8,128)(2,1)S(1)}, bf16[4,48,512]{2,1,0:T(8,128)(2,1)S(1)}, u32[]{:S(2)}, u32[]{:S(2)}) collective-permute-start(bf16[4,48,512]{2,1,0:T(8,128)(2,1)S(1)} %get-tuple-element.26), channel_id=1, source_target_pairs={{0,8},{8,16},{16,24},{24,32},{32,40},{40,48},{48,56},{56,64},{64,7... | collective-permute-start | bytes 589832 | tf_op jit(solution)/shard_map/ppermute | solution.py:558
  10.7 6.5 %collective-permute-start.3 = (bf16[4,48,512]{2,1,0:T(8,128)(2,1)S(1)}, bf16[4,48,512]{2,1,0:T(8,128)(2,1)S(1)}, u32[]{:S(2)}, u32[]{:S(2)}) collective-permute-start(bf16[4,48,512]{2,1,0:T(8,128)(2,1)S(1)} %get-tuple-element.27), channel_id=1, source_target_pairs={{8,0},{16,8},{24,16},{32,24},{40,32},{48,40},{56,48},{64,56},{72,6... | collective-permute-start | bytes 589832 | tf_op jit(solution)/shard_map/ppermute | solution.py:558
  17.2 4.3 %middle.1 = (f32[4,8,96,256]{3,2,1,0:T(8,128)S(1)}, f32[8,256]{1,0:T(8,128)S(1)}) custom-call(bf16[4,8,48,768]{3,2,1,0:T(8,128)(2,1)S(1)} %get-tuple-element.24.planes, bf16[7680,256]{1,0:T(8,128)(2,1)S(1)} %weights.1.table), custom_call_target="tpu_custom_call" | custom-call | flops 6000000000 | bytes 10000000 | tf_op jit(solution)/shard_map/middle/pallas_call | solution.py:192
  21.6 0.7 collective-permute-done.2.above
  22.3 0.0 copy-start.12
  22.3 0.9 edges.1
  23.3 4.7 %collective-permute-start.5 = (bf16[4,3,96,256]{3,2,1,0:T(8,128)(2,1)S(1)}, bf16[4,3,96,256]{3,2,1,0:T(8,128)(2,1)S(1)}, u32[]{:S(2)}, u32[]{:S(2)}) collective-permute-start(bf16[4,3,96,256]{3,2,1,0:T(8,128)(2,1)S(1)} %get-tuple-element.31), channel_id=1, source_target_pairs={{8,0},{16,8},{24,16},{32,24},{40,32},{48,40},{56,48},{64,56},{72,6... | collective-permute-start | bytes 1769480 | tf_op jit(solution)/shard_map/ppermute | solution.py:558
  27.9 22.5 %all_to_all.33 = f32[256,1,128]{2,1,0:T(1,128)S(1)} all-to-all(f32[256,1,128]{2,1,0:T(1,128)S(1)} %bitcast.32), channel_id=1, replica_groups=mesh['rows'=32,'cols'=8] {'rows','cols'}, dimensions={0} | all-to-all | bytes 262144 | tf_op jit(solution)/shard_map/all_to_all | solution.py:562
  50.5 0.0 copy-start.4
  50.6 6.2 %second.1 = (f32[4,4,96,256]{3,2,1,0:T(8,128)S(1)}, f32[256,128]{1,0:T(8,128)S(1)}, bf16[4,3,96,256]{3,2,1,0:T(8,128)(2,1)S(1)}, bf16[4,2,96,256]{3,2,1,0:T(8,128)(2,1)S(1)}) custom-call(f32[4,8,96,256]{3,2,1,0:T(8,128)S(1)} %get-tuple-element.25.inner, f32[4,2,96,256]{3,2,1,0:T(8,128)S(1)} %get-tuple-element.29.outer, ...), custom_call_target="tpu_custom_call" | custom-call | flops 6000000000 | bytes 12000000 | tf_op jit(solution)/shard_map/second/pallas_call | solution.py:415
  56.8 1.1 %collective-permute-start.7 = (bf16[4,3,96,256]{3,2,1,0:T(8,128)(2,1)S(1)}, bf16[4,3,96,256]{3,2,1,0:T(8,128)(2,1)S(1)}, u32[]{:S(2)}, u32[]{:S(2)}) collective-permute-start(bf16[4,3,96,256]{3,2,1,0:T(8,128)(2,1)S(1)} %get-tuple-element.35), channel_id=1, source_target_pairs={{8,0},{16,8},{24,16},{32,24},{40,32},{48,40},{56,48},{64,56},{72,6... | collective-permute-start | bytes 1769480 | tf_op jit(solution)/shard_map/ppermute | solution.py:558
  57.9 0.5 collective-permute-start.6
  58.3 20.3 %all_to_all.34 = f32[256,1,128]{2,1,0:T(1,128)S(1)} all-to-all(f32[256,1,128]{2,1,0:T(1,128)S(1)} %bitcast.31), channel_id=1, replica_groups=mesh['rows'=32,'cols'=8] {'rows','cols'}, dimensions={0} | all-to-all | bytes 262144 | tf_op jit(solution)/shard_map/all_to_all | solution.py:562
  78.7 0.0 copy-start.5
  78.7 2.6 %third.1 = (bf16[4,4,48,512]{3,2,1,0:T(8,128)(2,1)S(1)}, f32[256,128]{1,0:T(8,128)S(1)}) custom-call(f32[4,4,96,256]{3,2,1,0:T(8,128)S(1)} %get-tuple-element.33.inner, bf16[4,2,96,256]{3,2,1,0:T(8,128)(2,1)S(1)} %collective-permute-done.6.above, bf16[4,3,96,256]{3,2,1,0:T(8,128)(2,1)S(1)} %collective-permute-done.7.below, f32[256,128]{1,0:T(8,128)S(1)} %bitcast.33, ...), custom_call_target="tpu_custom_call" | custom-call | flops 2000000000 | bytes 8000000 | tf_op jit(solution)/shard_map/third/pallas_call | solution.py:484
  81.3 19.9 %all_to_all.35 = f32[256,1,128]{2,1,0:T(1,128)S(1)} all-to-all(f32[256,1,128]{2,1,0:T(1,128)S(1)} %bitcast.34), channel_id=1, replica_groups=mesh['rows'=32,'cols'=8] {'rows','cols'}, dimensions={0} | all-to-all | bytes 262144 | tf_op jit(solution)/shard_map/all_to_all | solution.py:562
  101.2 2.3 %last.1 = bf16[4,2,32,40]{3,2,1,0:T(8,128)(2,1)} custom-call(bf16[4,4,48,512]{3,2,1,0:T(8,128)(2,1)S(1)} %get-tuple-element.37.level, f32[256,128]{1,0:T(8,128)S(1)} %bitcast.35, f32[1,512]{1,0:T(1,128)S(1)} %bitcast.40, f32[1,512]{1,0:T(1,128)S(1)} %bitcast.41, bf16[3,9,32,512]{3,2,1,0:T(8,128)(2,1)S(1)} %bitcast.38), custom_call_target="tpu_custom_call" | custom-call | flops 1000000000 | bytes 4000000 | tf_op jit(solution)/shard_map/last/pallas_call | solution.py:536
  (29 shorter events, 0.1 us)
Async XLA Ops:
  0.0 1.3 %copy-start = (bf16[4,8,160,128]{3,2,1,0:T(8,128)(2,1)S(1)}, bf16[4,8,160,128]{3,2,1,0:T(8,128)(2,1)}, u32[]{:S(2)}) copy-start(bf16[4,8,160,128]{3,2,1,0:T(8,128)(2,1)} %param.12) | copy-start | bytes 3932164
  1.4 5.0 %collective-permute-start = (bf16[32,16,128]{2,1,0:T(8,128)(2,1)S(1)}, bf16[32,16,128]{2,1,0:T(8,128)(2,1)S(1)}, u32[]{:S(2)}, u32[]{:S(2)}) collective-permute-start(bf16[32,16,128]{2,1,0:T(8,128)(2,1)S(1)} %get-tuple-element.22), channel_id=1, source_target_pairs={{0,1},{1,2},{2,3},{3,4},{4,5},{5,6},{6,7},{7,0},{8,9},{9,10},{10,1... | collective-permute-start | bytes 393224 | tf_op jit(solution)/shard_map/ppermute | solution.py:558
  4.0 4.7 %collective-permute-start.1 = (bf16[32,16,128]{2,1,0:T(8,128)(2,1)S(1)}, bf16[32,16,128]{2,1,0:T(8,128)(2,1)S(1)}, u32[]{:S(2)}, u32[]{:S(2)}) collective-permute-start(bf16[32,16,128]{2,1,0:T(8,128)(2,1)S(1)} %get-tuple-element.23), channel_id=1, source_target_pairs={{1,0},{2,1},{3,2},{4,3},{5,4},{6,5},{7,6},{0,7},{9,8},{10,9},{11,1... | collective-permute-start | bytes 393224 | tf_op jit(solution)/shard_map/ppermute | solution.py:558
  4.6 1.2 %copy-start.2 = (bf16[3,3,3,128,128]{4,3,2,1,0:T(8,128)(2,1)S(1)}, bf16[3,3,3,128,128]{4,3,2,1,0:T(8,128)(2,1)}, u32[]{:S(2)}) copy-start(bf16[3,3,3,128,128]{4,3,2,1,0:T(8,128)(2,1)} %param.13) | copy-start | bytes 2654212
  5.8 2.9 %copy-start.1 = (bf16[4,8,160,128]{3,2,1,0:T(8,128)(2,1)S(1)}, bf16[4,8,160,128]{3,2,1,0:T(8,128)(2,1)}, u32[]{:S(2)}) copy-start(bf16[4,8,160,128]{3,2,1,0:T(8,128)(2,1)} %param.12) | copy-start | bytes 3932164
  9.3 13.0 %collective-permute-start.2 = (bf16[4,48,512]{2,1,0:T(8,128)(2,1)S(1)}, bf16[4,48,512]{2,1,0:T(8,128)(2,1)S(1)}, u32[]{:S(2)}, u32[]{:S(2)}) collective-permute-start(bf16[4,48,512]{2,1,0:T(8,128)(2,1)S(1)} %get-tuple-element.26), channel_id=1, source_target_pairs={{0,8},{8,16},{16,24},{24,32},{32,40},{40,48},{48,56},{56,64},{64,7... | collective-permute-start | bytes 589832 | tf_op jit(solution)/shard_map/ppermute | solution.py:558
  10.7 11.6 %collective-permute-start.3 = (bf16[4,48,512]{2,1,0:T(8,128)(2,1)S(1)}, bf16[4,48,512]{2,1,0:T(8,128)(2,1)S(1)}, u32[]{:S(2)}, u32[]{:S(2)}) collective-permute-start(bf16[4,48,512]{2,1,0:T(8,128)(2,1)S(1)} %get-tuple-element.27), channel_id=1, source_target_pairs={{8,0},{16,8},{24,16},{32,24},{40,32},{48,40},{56,48},{64,56},{72,6... | collective-permute-start | bytes 589832 | tf_op jit(solution)/shard_map/ppermute | solution.py:558
  22.3 28.2 %copy-start.3 = (bf16[3,3,3,256,256]{4,3,2,1,0:T(8,128)(2,1)S(1)}, bf16[3,3,3,256,256]{4,3,2,1,0:T(8,128)(2,1)}, u32[]{:S(2)}) copy-start(bf16[3,3,3,256,256]{4,3,2,1,0:T(8,128)(2,1)} %param.15) | copy-start | bytes 10616836
  22.3 28.2 %copy-start.6 = (bf16[3,3,128,256]{3,2,1,0:T(8,128)(2,1)S(1)}, bf16[3,3,128,256]{3,2,1,0:T(8,128)(2,1)}, u32[]{:S(2)}) copy-start(bf16[3,3,128,256]{3,2,1,0:T(8,128)(2,1)} %param.14) | copy-start | bytes 1769476
  22.3 28.2 %copy-start.11 = (f32[128]{0:T(128)S(1)}, f32[128]{0:T(128)}, u32[]{:S(2)}) copy-start(f32[128]{0:T(128)} %param.18) | copy-start | bytes 1540
  22.3 28.2 %copy-start.12 = (f32[128]{0:T(128)S(1)}, f32[128]{0:T(128)}, u32[]{:S(2)}) copy-start(f32[128]{0:T(128)} %param.19) | copy-start | bytes 1540
  23.3 27.2 %collective-permute-start.5 = (bf16[4,3,96,256]{3,2,1,0:T(8,128)(2,1)S(1)}, bf16[4,3,96,256]{3,2,1,0:T(8,128)(2,1)S(1)}, u32[]{:S(2)}, u32[]{:S(2)}) collective-permute-start(bf16[4,3,96,256]{3,2,1,0:T(8,128)(2,1)S(1)} %get-tuple-element.31), channel_id=1, source_target_pairs={{8,0},{16,8},{24,16},{32,24},{40,32},{48,40},{56,48},{64,56},{72,6... | collective-permute-start | bytes 1769480 | tf_op jit(solution)/shard_map/ppermute | solution.py:558
  27.9 22.5 %collective-permute-start.4 = (bf16[4,2,96,256]{3,2,1,0:T(8,128)(2,1)S(1)}, bf16[4,2,96,256]{3,2,1,0:T(8,128)(2,1)S(1)}, u32[]{:S(2)}, u32[]{:S(2)}) collective-permute-start(bf16[4,2,96,256]{3,2,1,0:T(8,128)(2,1)S(1)} %get-tuple-element.30), channel_id=1, source_target_pairs={{0,8},{8,16},{16,24},{24,32},{32,40},{40,48},{48,56},{56,64},{64,7... | collective-permute-start | bytes 1179656 | tf_op jit(solution)/shard_map/ppermute | solution.py:558
  50.5 28.1 %copy-start.4 = (bf16[3,3,256,512]{3,2,1,0:T(8,128)(2,1)S(1)}, bf16[3,3,256,512]{3,2,1,0:T(8,128)(2,1)}, u32[]{:S(2)}) copy-start(bf16[3,3,256,512]{3,2,1,0:T(8,128)(2,1)} %param.16) | copy-start | bytes 7077892
  50.5 28.1 %copy-start.9 = (f32[256]{0:T(256)S(1)}, f32[256]{0:T(256)}, u32[]{:S(2)}) copy-start(f32[256]{0:T(256)} %param.20) | copy-start | bytes 3076
  50.5 28.1 %copy-start.10 = (f32[256]{0:T(256)S(1)}, f32[256]{0:T(256)}, u32[]{:S(2)}) copy-start(f32[256]{0:T(256)} %param.21) | copy-start | bytes 3076
  56.8 21.9 %collective-permute-start.7 = (bf16[4,3,96,256]{3,2,1,0:T(8,128)(2,1)S(1)}, bf16[4,3,96,256]{3,2,1,0:T(8,128)(2,1)S(1)}, u32[]{:S(2)}, u32[]{:S(2)}) collective-permute-start(bf16[4,3,96,256]{3,2,1,0:T(8,128)(2,1)S(1)} %get-tuple-element.35), channel_id=1, source_target_pairs={{8,0},{16,8},{24,16},{32,24},{40,32},{48,40},{56,48},{64,56},{72,6... | collective-permute-start | bytes 1769480 | tf_op jit(solution)/shard_map/ppermute | solution.py:558
  57.9 20.8 %collective-permute-start.6 = (bf16[4,2,96,256]{3,2,1,0:T(8,128)(2,1)S(1)}, bf16[4,2,96,256]{3,2,1,0:T(8,128)(2,1)S(1)}, u32[]{:S(2)}, u32[]{:S(2)}) collective-permute-start(bf16[4,2,96,256]{3,2,1,0:T(8,128)(2,1)S(1)} %get-tuple-element.34), channel_id=1, source_target_pairs={{0,8},{8,16},{16,24},{24,32},{32,40},{40,48},{48,56},{56,64},{64,7... | collective-permute-start | bytes 1179656 | tf_op jit(solution)/shard_map/ppermute | solution.py:558
  78.7 22.5 %copy-start.5 = (bf16[3,3,3,512,32]{3,4,2,1,0:T(8,128)(2,1)S(1)}, bf16[3,3,3,512,32]{3,4,2,1,0:T(8,128)(2,1)}, u32[]{:S(2)}) copy-start(bf16[3,3,3,512,32]{3,4,2,1,0:T(8,128)(2,1)} %param.17) | copy-start | bytes 2654212
  78.7 22.5 %copy-start.7 = (f32[512]{0:T(512)S(1)}, f32[512]{0:T(512)}, u32[]{:S(2)}) copy-start(f32[512]{0:T(512)} %param.22) | copy-start | bytes 6148
  78.7 22.5 %copy-start.8 = (f32[512]{0:T(512)S(1)}, f32[512]{0:T(512)}, u32[]{:S(2)}) copy-start(f32[512]{0:T(512)} %param.23) | copy-start | bytes 6148

commit v6 on v5

--- a/solution.py
+++ b/solution.py
@@ -76,10 +76,15 @@
     )(first.reshape(27 * C1, C1))
 
 
-def cut_kernel(features, last, first, sem):
+def cut_kernel(features, last, first, bottom, top, sem):
+    def copy(i, source, target):
+        return pltpu.make_async_copy(source, target, sem.at[i])
+
     copies = [
-        pltpu.make_async_copy(features.at[:, pl.ds(COLS - EDGE, EDGE)], last, sem.at[0]),
-        pltpu.make_async_copy(features.at[:, pl.ds(0, EDGE)], first, sem.at[1]),
+        copy(0, features.at[:, :, pl.ds(COLS - EDGE, EDGE)], last),
+        copy(1, features.at[:, :, pl.ds(0, EDGE)], first),
+        copy(2, features.at[:, ROWS - 1], bottom),
+        copy(3, features.at[:, 0], top),
     ]
     for c in copies:
         c.start()
@@ -88,17 +93,28 @@
 
 
 def cut(features):
-    edge = shape((FRAMES * ROWS, EDGE, C1), BF16)
+    edge, line = shape((FRAMES, ROWS, EDGE, C1), BF16), shape((FRAMES, COLS, C1), BF16)
     return pl.pallas_call(
         cut_kernel,
-        out_shape=(edge, edge),
+        out_shape=(edge, edge, line, line),
         in_specs=[HBM],
-        out_specs=(VMEM,) * 2,
-        scratch_shapes=[pltpu.SemaphoreType.DMA((2,))],
+        out_specs=(VMEM,) * 4,
+        scratch_shapes=[pltpu.SemaphoreType.DMA((4,))],
         compiler_params=params(4),
         cost_estimate=cost(0, 4e5),
         name="cut",
-    )(features.reshape(FRAMES * ROWS, COLS, C1))
+    )(features)
+
+
+def lay(line, left, own, right):
+    line[0:EDGE, :] = left
+    line[EDGE : EDGE + COLS, :] = own
+    line[EDGE + COLS : 2 * EDGE + COLS, :] = right
+    line[2 * EDGE + COLS : LINE, :] = jnp.zeros((LINE - 2 * EDGE - COLS, C1), F32)
+
+
+def plane(line, k):
+    return line[pl.ds(7 + k, Q, stride=4), :].astype(BF16)
 
 
 def planes_kernel(left, own, right, planes, top, bottom, line):
@@ -106,38 +122,31 @@
     left_in = 1.0 - first_col.astype(F32)
     right_in = 1.0 - last_col.astype(F32)
     for t in range(FRAMES):
-
-        def step(r, carry, t=t):
-            i = t * ROWS + r
-            line[i, 0:EDGE, :] = left[i].astype(F32) * left_in
-            line[i, EDGE : EDGE + COLS, :] = own[i].astype(F32)
-            line[i, EDGE + COLS : 2 * EDGE + COLS, :] = right[i].astype(F32) * right_in
-            line[i, 2 * EDGE + COLS : LINE, :] = jnp.zeros((LINE - 2 * EDGE - COLS, C1), F32)
+        for r in range(ROWS):
+            before = left[t, r].astype(F32) * left_in
+            after = right[t, r].astype(F32) * right_in
+            at = line.at[t * ROWS + r]
+            lay(at, before, own[t, r].astype(F32), after)
             for k in range(6):
-                planes[t, r, :, k * C1 : (k + 1) * C1] = line[i, pl.ds(7 + k, Q, stride=4), :].astype(BF16)
-            return carry
-
-        lax.fori_loop(0, ROWS, step, 0, unroll=True)
-        top[t] = planes[t, 0, :, C1 : 5 * C1]
-        bottom[t] = planes[t, ROWS - 1, :, C1 : 5 * C1]
+                planes[t, r, :, k * C1 : (k + 1) * C1] = plane(at, k)
+            if r in (0, ROWS - 1):
+                corner = top if r == 0 else bottom
+                corner[t, 0] = before.astype(BF16)
+                corner[t, 1] = after.astype(BF16)
 
 
 def planes_of(left, own, right):
-    lines = FRAMES * ROWS
+    corner = shape((FRAMES, 2, EDGE, C1), BF16)
     return pl.pallas_call(
         planes_kernel,
-        out_shape=(
-            shape((FRAMES, ROWS, Q, 6 * C1), BF16),
-            shape((FRAMES, Q, 4 * C1), BF16),
-            shape((FRAMES, Q, 4 * C1), BF16),
-        ),
+        out_shape=(shape((FRAMES, ROWS, Q, 6 * C1), BF16), corner, corner),
         in_specs=[VMEM] * 3,
         out_specs=(VMEM,) * 3,
-        scratch_shapes=[pltpu.VMEM((lines, LINE, C1), F32)],
+        scratch_shapes=[pltpu.VMEM((FRAMES * ROWS, LINE, C1), F32)],
         compiler_params=params(12),
         cost_estimate=cost(0, 4e6),
         name="planes",
-    )(left, own.reshape(lines, COLS, C1), right)
+    )(left, own, right)
 
 
 def own_entries(rows, lanes):
@@ -245,20 +254,22 @@
     return 0.5 * factor, 0.5 * (shift[...] - mean * factor)
 
 
-def edges_kernel(above, below, table, inner, stats, hidden, share, up, down):
+def edges_kernel(
+    above, below, corners_above, corners_below, table, inner, stats, hidden, share, up, down, line
+):
     mask = own_entries(2 * Q, 2 * C1)
     total = [stats[0:1, :], stats[1:2, :]]
     first_row, last_row, _, _ = position()
-    for side, (ref, b, end) in enumerate(((above, 0, first_row), (below, 2, last_row))):
+    sides = ((above, corners_above, 0, first_row), (below, corners_below, 2, last_row))
+    for side, (ref, corner, b, end) in enumerate(sides):
         inside = 1.0 - end.astype(F32)
         lines = []
         for t in range(FRAMES):
-            wide = ref[t].astype(F32) * inside
-            whole = wide.astype(BF16)
-            first = pltpu.roll(wide[:, 3 * C1 :], 1, 0).astype(BF16)
-            last = pltpu.roll(wide[:, :C1], Q - 1, 0).astype(BF16)
-            even = jnp.concatenate([first, whole[:, : 3 * C1]], axis=1)
-            odd = jnp.concatenate([whole[:, C1:], last], axis=1)
+            at = line.at[side * FRAMES + t]
+            lay(at, *(v.astype(F32) * inside for v in (corner[t, 0], ref[t], corner[t, 1])))
+            parts = [plane(at, k) for k in range(6)]
+            even = jnp.concatenate(parts[:4], axis=1)
+            odd = jnp.concatenate(parts[2:], axis=1)
             lines.append(jnp.concatenate([even, odd], axis=0))
 
         def product(v, s):
@@ -284,7 +295,7 @@
     share[...] = jnp.broadcast_to(grouped(one, two), share.shape)
 
 
-def edges(above, below, table, inner, stats, devices):
+def edges(above, below, corners_above, corners_below, table, inner, stats, devices):
     return pl.pallas_call(
         edges_kernel,
         out_shape=(
@@ -293,12 +304,13 @@
             shape((FRAMES, 3, 2 * Q, 2 * C1), BF16),
             shape((FRAMES, 2, 2 * Q, 2 * C1), BF16),
         ),
-        in_specs=[VMEM] * 5,
+        in_specs=[VMEM] * 7,
         out_specs=(VMEM,) * 4,
+        scratch_shapes=[pltpu.VMEM((2 * FRAMES, LINE, C1), F32)],
         compiler_params=params(12),
         cost_estimate=cost(2e9, 10e6),
         name="edges",
-    )(above, below, table, inner, stats)
+    )(above, below, corners_above, corners_below, table, inner, stats)
 
 
 def kept(entry_out, edge):
@@ -567,12 +579,14 @@
     gain_first, shift_first, gain_second, shift_second, gain_third, shift_third,
 ):
     devices = lax.axis_size("rows") * lax.axis_size("cols")
-    left, right = from_both(*cut(features), "cols")
+    last, first, bottom, top = cut(features)
+    left, right = from_both(last, first, "cols")
+    above, below = from_both(bottom, top, "rows")
     table = weights(conv_first)
     planes, top, bottom = planes_of(left, features, right)
-    above, below = from_both(bottom, top, "rows")
+    corners_above, corners_below = from_both(bottom, top, "rows")
     inner, stats = middle(planes, table)
-    outer, share, up, down = edges(above, below, table, inner, stats, devices)
+    outer, share, up, down = edges(above, below, corners_above, corners_below, table, inner, stats, devices)
     above, below = from_both(down, up, "rows")
     hidden, share, up, down = second_level(
         inner, outer, above, below, everywhere(share), gain_first, shift_first,

time: 104 us -> 105 us (level)
  waiting for transfers between devices: 2.99 us -> 0.03 us
  blocking collectives: 62.8 us -> 65.2 us
  starting transfers between devices: 17.4 us -> 18.8 us
    all_to_all x3, blocking collectives: 62.8 us -> 65.2 us  [everywhere(): return lax.all_to_all(share, AXES, 0, 0, tiled=True)]
    ppermute x4 -> x5, waiting for transfers between devices: 2.27 us -> 0.01 us  [from_both(): lax.ppermute(first, axis, backward(axis))]
    ppermute x4 -> x5, starting transfers between devices: 12.9 us -> 14.6 us  [from_both(): lax.ppermute(first, axis, backward(axis))]
    ppermute x4 -> x5, starting transfers between devices: 4.51 us -> 4.15 us  [from_both(): lax.ppermute(last, axis, forward(axis))]
  transfers between devices with their start and end apart: 8 -> 10, of which waited for: 2 -> 0; matrix products, arithmetic and copies ran while one was open for 0% -> 0% of each run, Pallas kernels for 5% -> 5%
where the time goes in v6:
time: 105 us
  blocking collectives  65.2 us (62%)
  starting transfers between devices  18.8 us (18%)
  Pallas kernels  17.7 us (17%)
  local copies, waits for them, and re-layouts  3.26 us (3%)
    all_to_all x3, blocking collectives, everywhere(): return lax.all_to_all(share, AXES, 0, 0, tiled=True)  65.2 us
    ppermute x5, starting transfers between devices, from_both(): lax.ppermute(first, axis, backward(axis))  14.6 us
    pallas_call x1, Pallas kernels, second_level(): pl.pallas_call(functools.partial(second_kernel, members=float(devices * F...  6.24 us
    pallas_call x1, Pallas kernels, middle(): pl.pallas_call(middle_kernel, out_shape=(shape((FRAMES, ROWS, 2 * Q, 2 *...  4.35 us
    ppermute x5, starting transfers between devices, from_both(): lax.ppermute(last, axis, forward(axis))  4.15 us
    unnamed x26, local copies, waits for them, and re-layouts  3.26 us
    pallas_call x1, Pallas kernels, third_level(): pl.pallas_call(functools.partial(third_kernel, members=float(devices * FR...  2.6 us
    pallas_call x1, Pallas kernels, last_level(): pl.pallas_call(functools.partial(last_kernel, members=float(devices * FRA...  2.25 us
  transfers between devices with their start and end apart: 10, of which 0 were waited for; matrix products, arithmetic and copies ran while one was open for 0% of the time, Pallas kernels for 5%

profile of v6, /device:TPU:1, one launch (start us, length us, event | category | flops | bytes accessed | tf_op | source)
XLA Modules:
  0.0 105.2 jit_solution(8062262615748396586)
XLA Ops:
  0.0 1.3 %copy-done = bf16[4,8,160,128]{3,2,1,0:T(8,128)(2,1)S(1)} copy-done((bf16[4,8,160,128]{3,2,1,0:T(8,128)(2,1)S(1)}, bf16[4,8,160,128]{3,2,1,0:T(8,128)(2,1)}, u32[]{:S(2)}) %copy-start) | copy-done | bytes 1310744
  1.3 0.2 cut.1
  1.5 2.6 %collective-permute-start = (bf16[4,8,16,128]{3,2,1,0:T(8,128)(2,1)S(1)}, bf16[4,8,16,128]{3,2,1,0:T(8,128)(2,1)S(1)}, u32[]{:S(2)}, u32[]{:S(2)}) collective-permute-start(bf16[4,8,16,128]{3,2,1,0:T(8,128)(2,1)S(1)} %get-tuple-element.24), channel_id=1, source_target_pairs={{0,1},{1,2},{2,3},{3,4},{4,5},{5,6},{6,7},{7,0},{8,9},{9,10},{10,1... | collective-permute-start | bytes 393224 | tf_op jit(solution)/shard_map/ppermute | solution.py:570
  4.1 0.7 collective-permute-start.1
  4.8 1.0 collective-permute-start.2
  5.7 6.4 %collective-permute-start.3 = (bf16[4,160,128]{2,1,0:T(8,128)(2,1)S(1)}, bf16[4,160,128]{2,1,0:T(8,128)(2,1)S(1)}, u32[]{:S(2)}, u32[]{:S(2)}) collective-permute-start(bf16[4,160,128]{2,1,0:T(8,128)(2,1)S(1)} %get-tuple-element.29), channel_id=1, source_target_pairs={{8,0},{16,8},{24,16},{32,24},{40,32},{48,40},{56,48},{64,56},{72,6... | collective-permute-start | bytes 491528 | tf_op jit(solution)/shard_map/ppermute | solution.py:570
  12.1 1.2 %copy-done.2 = bf16[3,3,3,128,128]{4,3,2,1,0:T(8,128)(2,1)S(1)} copy-done((bf16[3,3,3,128,128]{4,3,2,1,0:T(8,128)(2,1)S(1)}, bf16[3,3,3,128,128]{4,3,2,1,0:T(8,128)(2,1)}, u32[]{:S(2)}) %copy-start.2) | copy-done | bytes 884760
  13.3 0.6 weights.1.table
  13.9 0.7 copy-done.1
  14.6 0.6 planes.1
  15.2 0.1 collective-permute-start.4
  15.3 4.8 %collective-permute-start.5 = (bf16[4,2,16,128]{3,2,1,0:T(8,128)(2,1)S(1)}, bf16[4,2,16,128]{3,2,1,0:T(8,128)(2,1)S(1)}, u32[]{:S(2)}, u32[]{:S(2)}) collective-permute-start(bf16[4,2,16,128]{3,2,1,0:T(8,128)(2,1)S(1)} %get-tuple-element.31), channel_id=1, source_target_pairs={{8,0},{16,8},{24,16},{32,24},{40,32},{48,40},{56,48},{64,56},{72,6... | collective-permute-start | bytes 98312 | tf_op jit(solution)/shard_map/ppermute | solution.py:570
  20.1 4.3 %middle.1 = (f32[4,8,96,256]{3,2,1,0:T(8,128)S(1)}, f32[8,256]{1,0:T(8,128)S(1)}) custom-call(bf16[4,8,48,768]{3,2,1,0:T(8,128)(2,1)S(1)} %get-tuple-element.26.planes, bf16[7680,256]{1,0:T(8,128)(2,1)S(1)} %weights.1.table), custom_call_target="tpu_custom_call" | custom-call | flops 6000000000 | bytes 10000000 | tf_op jit(solution)/shard_map/middle/pallas_call | solution.py:201
  24.5 0.0 copy-start.11
  24.5 0.9 edges.1
  25.5 1.7 %collective-permute-start.7 = (bf16[4,3,96,256]{3,2,1,0:T(8,128)(2,1)S(1)}, bf16[4,3,96,256]{3,2,1,0:T(8,128)(2,1)S(1)}, u32[]{:S(2)}, u32[]{:S(2)}) collective-permute-start(bf16[4,3,96,256]{3,2,1,0:T(8,128)(2,1)S(1)} %get-tuple-element.35), channel_id=1, source_target_pairs={{8,0},{16,8},{24,16},{32,24},{40,32},{48,40},{56,48},{64,56},{72,6... | collective-permute-start | bytes 1769480 | tf_op jit(solution)/shard_map/ppermute | solution.py:570
  27.2 24.9 %all_to_all.33 = f32[256,1,128]{2,1,0:T(1,128)S(1)} all-to-all(f32[256,1,128]{2,1,0:T(1,128)S(1)} %bitcast.27), channel_id=1, replica_groups=mesh['rows'=32,'cols'=8] {'rows','cols'}, dimensions={0} | all-to-all | bytes 262144 | tf_op jit(solution)/shard_map/all_to_all | solution.py:574
  52.2 6.2 %second.1 = (f32[4,4,96,256]{3,2,1,0:T(8,128)S(1)}, f32[256,128]{1,0:T(8,128)S(1)}, bf16[4,3,96,256]{3,2,1,0:T(8,128)(2,1)S(1)}, bf16[4,2,96,256]{3,2,1,0:T(8,128)(2,1)S(1)}) custom-call(f32[4,8,96,256]{3,2,1,0:T(8,128)S(1)} %get-tuple-element.27.inner, f32[4,2,96,256]{3,2,1,0:T(8,128)S(1)} %get-tuple-element.33.outer, ...), custom_call_target="tpu_custom_call" | custom-call | flops 6000000000 | bytes 12000000 | tf_op jit(solution)/shard_map/second/pallas_call | solution.py:427
  58.5 1.1 %collective-permute-start.9 = (bf16[4,3,96,256]{3,2,1,0:T(8,128)(2,1)S(1)}, bf16[4,3,96,256]{3,2,1,0:T(8,128)(2,1)S(1)}, u32[]{:S(2)}, u32[]{:S(2)}) collective-permute-start(bf16[4,3,96,256]{3,2,1,0:T(8,128)(2,1)S(1)} %get-tuple-element.39), channel_id=1, source_target_pairs={{8,0},{16,8},{24,16},{32,24},{40,32},{48,40},{56,48},{64,56},{72,6... | collective-permute-start | bytes 1769480 | tf_op jit(solution)/shard_map/ppermute | solution.py:570
  59.5 0.5 collective-permute-start.8
  60.0 20.3 %all_to_all.34 = f32[256,1,128]{2,1,0:T(1,128)S(1)} all-to-all(f32[256,1,128]{2,1,0:T(1,128)S(1)} %bitcast.29), channel_id=1, replica_groups=mesh['rows'=32,'cols'=8] {'rows','cols'}, dimensions={0} | all-to-all | bytes 262144 | tf_op jit(solution)/shard_map/all_to_all | solution.py:574
  80.4 2.6 %third.1 = (bf16[4,4,48,512]{3,2,1,0:T(8,128)(2,1)S(1)}, f32[256,128]{1,0:T(8,128)S(1)}) custom-call(f32[4,4,96,256]{3,2,1,0:T(8,128)S(1)} %get-tuple-element.37.inner, bf16[4,2,96,256]{3,2,1,0:T(8,128)(2,1)S(1)} %collective-permute-done.8.above, bf16[4,3,96,256]{3,2,1,0:T(8,128)(2,1)S(1)} %collective-permute-done.9.below, f32[256,128]{1,0:T(8,128)S(1)} %bitcast.30, ...), custom_call_target="tpu_custom_call" | custom-call | flops 2000000000 | bytes 8000000 | tf_op jit(solution)/shard_map/third/pallas_call | solution.py:496
  83.0 19.9 %all_to_all.35 = f32[256,1,128]{2,1,0:T(1,128)S(1)} all-to-all(f32[256,1,128]{2,1,0:T(1,128)S(1)} %bitcast.31), channel_id=1, replica_groups=mesh['rows'=32,'cols'=8] {'rows','cols'}, dimensions={0} | all-to-all | bytes 262144 | tf_op jit(solution)/shard_map/all_to_all | solution.py:574
  102.9 2.3 %last.1 = bf16[4,2,32,40]{3,2,1,0:T(8,128)(2,1)} custom-call(bf16[4,4,48,512]{3,2,1,0:T(8,128)(2,1)S(1)} %get-tuple-element.41.level, f32[256,128]{1,0:T(8,128)S(1)} %bitcast.32, f32[1,512]{1,0:T(1,128)S(1)} %bitcast.37, f32[1,512]{1,0:T(1,128)S(1)} %bitcast.38, bf16[3,9,32,512]{3,2,1,0:T(8,128)(2,1)S(1)} %bitcast.35), custom_call_target="tpu_custom_call" | custom-call | flops 1000000000 | bytes 4000000 | tf_op jit(solution)/shard_map/last/pallas_call | solution.py:548
  (33 shorter events, 0.1 us)
Async XLA Ops:
  0.0 1.3 %copy-start = (bf16[4,8,160,128]{3,2,1,0:T(8,128)(2,1)S(1)}, bf16[4,8,160,128]{3,2,1,0:T(8,128)(2,1)}, u32[]{:S(2)}) copy-start(bf16[4,8,160,128]{3,2,1,0:T(8,128)(2,1)} %own.1) | copy-start | bytes 3932164
  1.5 12.4 %collective-permute-start = (bf16[4,8,16,128]{3,2,1,0:T(8,128)(2,1)S(1)}, bf16[4,8,16,128]{3,2,1,0:T(8,128)(2,1)S(1)}, u32[]{:S(2)}, u32[]{:S(2)}) collective-permute-start(bf16[4,8,16,128]{3,2,1,0:T(8,128)(2,1)S(1)} %get-tuple-element.24), channel_id=1, source_target_pairs={{0,1},{1,2},{2,3},{3,4},{4,5},{5,6},{6,7},{7,0},{8,9},{9,10},{10,1... | collective-permute-start | bytes 393224 | tf_op jit(solution)/shard_map/ppermute | solution.py:570
  4.1 9.8 %collective-permute-start.1 = (bf16[4,8,16,128]{3,2,1,0:T(8,128)(2,1)S(1)}, bf16[4,8,16,128]{3,2,1,0:T(8,128)(2,1)S(1)}, u32[]{:S(2)}, u32[]{:S(2)}) collective-permute-start(bf16[4,8,16,128]{3,2,1,0:T(8,128)(2,1)S(1)} %get-tuple-element.25), channel_id=1, source_target_pairs={{1,0},{2,1},{3,2},{4,3},{5,4},{6,5},{7,6},{0,7},{9,8},{10,9},{11,1... | collective-permute-start | bytes 393224 | tf_op jit(solution)/shard_map/ppermute | solution.py:570
  4.8 19.7 %collective-permute-start.2 = (bf16[4,160,128]{2,1,0:T(8,128)(2,1)S(1)}, bf16[4,160,128]{2,1,0:T(8,128)(2,1)S(1)}, u32[]{:S(2)}, u32[]{:S(2)}) collective-permute-start(bf16[4,160,128]{2,1,0:T(8,128)(2,1)S(1)} %get-tuple-element.28), channel_id=1, source_target_pairs={{0,8},{8,16},{16,24},{24,32},{32,40},{40,48},{48,56},{56,64},{64,7... | collective-permute-start | bytes 491528 | tf_op jit(solution)/shard_map/ppermute | solution.py:570
  5.7 18.7 %collective-permute-start.3 = (bf16[4,160,128]{2,1,0:T(8,128)(2,1)S(1)}, bf16[4,160,128]{2,1,0:T(8,128)(2,1)S(1)}, u32[]{:S(2)}, u32[]{:S(2)}) collective-permute-start(bf16[4,160,128]{2,1,0:T(8,128)(2,1)S(1)} %get-tuple-element.29), channel_id=1, source_target_pairs={{8,0},{16,8},{24,16},{32,24},{40,32},{48,40},{56,48},{64,56},{72,6... | collective-permute-start | bytes 491528 | tf_op jit(solution)/shard_map/ppermute | solution.py:570
  12.1 1.2 %copy-start.2 = (bf16[3,3,3,128,128]{4,3,2,1,0:T(8,128)(2,1)S(1)}, bf16[3,3,3,128,128]{4,3,2,1,0:T(8,128)(2,1)}, u32[]{:S(2)}) copy-start(bf16[3,3,3,128,128]{4,3,2,1,0:T(8,128)(2,1)} %param.13) | copy-start | bytes 2654212
  13.3 1.3 %copy-start.1 = (bf16[4,8,160,128]{3,2,1,0:T(8,128)(2,1)S(1)}, bf16[4,8,160,128]{3,2,1,0:T(8,128)(2,1)}, u32[]{:S(2)}) copy-start(bf16[4,8,160,128]{3,2,1,0:T(8,128)(2,1)} %own.1) | copy-start | bytes 3932164
  15.2 9.2 %collective-permute-start.4 = (bf16[4,2,16,128]{3,2,1,0:T(8,128)(2,1)S(1)}, bf16[4,2,16,128]{3,2,1,0:T(8,128)(2,1)S(1)}, u32[]{:S(2)}, u32[]{:S(2)}) collective-permute-start(bf16[4,2,16,128]{3,2,1,0:T(8,128)(2,1)S(1)} %get-tuple-element.30), channel_id=1, source_target_pairs={{0,8},{8,16},{16,24},{24,32},{32,40},{40,48},{48,56},{56,64},{64,7... | collective-permute-start | bytes 98312 | tf_op jit(solution)/shard_map/ppermute | solution.py:570
  15.3 9.2 %collective-permute-start.5 = (bf16[4,2,16,128]{3,2,1,0:T(8,128)(2,1)S(1)}, bf16[4,2,16,128]{3,2,1,0:T(8,128)(2,1)S(1)}, u32[]{:S(2)}, u32[]{:S(2)}) collective-permute-start(bf16[4,2,16,128]{3,2,1,0:T(8,128)(2,1)S(1)} %get-tuple-element.31), channel_id=1, source_target_pairs={{8,0},{16,8},{24,16},{32,24},{40,32},{48,40},{56,48},{64,56},{72,6... | collective-permute-start | bytes 98312 | tf_op jit(solution)/shard_map/ppermute | solution.py:570
  24.5 27.7 %copy-start.3 = (bf16[3,3,3,256,256]{4,3,2,1,0:T(8,128)(2,1)S(1)}, bf16[3,3,3,256,256]{4,3,2,1,0:T(8,128)(2,1)}, u32[]{:S(2)}) copy-start(bf16[3,3,3,256,256]{4,3,2,1,0:T(8,128)(2,1)} %param.15) | copy-start | bytes 10616836
  24.5 27.7 %copy-start.6 = (bf16[3,3,128,256]{3,2,1,0:T(8,128)(2,1)S(1)}, bf16[3,3,128,256]{3,2,1,0:T(8,128)(2,1)}, u32[]{:S(2)}) copy-start(bf16[3,3,128,256]{3,2,1,0:T(8,128)(2,1)} %param.14) | copy-start | bytes 1769476
  24.5 27.7 %copy-start.11 = (f32[128]{0:T(128)S(1)}, f32[128]{0:T(128)}, u32[]{:S(2)}) copy-start(f32[128]{0:T(128)} %param.18) | copy-start | bytes 1540
  24.5 27.7 %copy-start.12 = (f32[128]{0:T(128)S(1)}, f32[128]{0:T(128)}, u32[]{:S(2)}) copy-start(f32[128]{0:T(128)} %param.19) | copy-start | bytes 1540
  25.5 26.7 %collective-permute-start.7 = (bf16[4,3,96,256]{3,2,1,0:T(8,128)(2,1)S(1)}, bf16[4,3,96,256]{3,2,1,0:T(8,128)(2,1)S(1)}, u32[]{:S(2)}, u32[]{:S(2)}) collective-permute-start(bf16[4,3,96,256]{3,2,1,0:T(8,128)(2,1)S(1)} %get-tuple-element.35), channel_id=1, source_target_pairs={{8,0},{16,8},{24,16},{32,24},{40,32},{48,40},{56,48},{64,56},{72,6... | collective-permute-start | bytes 1769480 | tf_op jit(solution)/shard_map/ppermute | solution.py:570
  27.2 24.9 %collective-permute-start.6 = (bf16[4,2,96,256]{3,2,1,0:T(8,128)(2,1)S(1)}, bf16[4,2,96,256]{3,2,1,0:T(8,128)(2,1)S(1)}, u32[]{:S(2)}, u32[]{:S(2)}) collective-permute-start(bf16[4,2,96,256]{3,2,1,0:T(8,128)(2,1)S(1)} %get-tuple-element.34), channel_id=1, source_target_pairs={{0,8},{8,16},{16,24},{24,32},{32,40},{40,48},{48,56},{56,64},{64,7... | collective-permute-start | bytes 1179656 | tf_op jit(solution)/shard_map/ppermute | solution.py:570
  52.2 28.1 %copy-start.4 = (bf16[3,3,256,512]{3,2,1,0:T(8,128)(2,1)S(1)}, bf16[3,3,256,512]{3,2,1,0:T(8,128)(2,1)}, u32[]{:S(2)}) copy-start(bf16[3,3,256,512]{3,2,1,0:T(8,128)(2,1)} %param.16) | copy-start | bytes 7077892
  52.2 28.1 %copy-start.9 = (f32[256]{0:T(256)S(1)}, f32[256]{0:T(256)}, u32[]{:S(2)}) copy-start(f32[256]{0:T(256)} %param.20) | copy-start | bytes 3076
  52.2 28.1 %copy-start.10 = (f32[256]{0:T(256)S(1)}, f32[256]{0:T(256)}, u32[]{:S(2)}) copy-start(f32[256]{0:T(256)} %param.21) | copy-start | bytes 3076
  58.5 21.9 %collective-permute-start.9 = (bf16[4,3,96,256]{3,2,1,0:T(8,128)(2,1)S(1)}, bf16[4,3,96,256]{3,2,1,0:T(8,128)(2,1)S(1)}, u32[]{:S(2)}, u32[]{:S(2)}) collective-permute-start(bf16[4,3,96,256]{3,2,1,0:T(8,128)(2,1)S(1)} %get-tuple-element.39), channel_id=1, source_target_pairs={{8,0},{16,8},{24,16},{32,24},{40,32},{48,40},{56,48},{64,56},{72,6... | collective-permute-start | bytes 1769480 | tf_op jit(solution)/shard_map/ppermute | solution.py:570
  59.5 20.8 %collective-permute-start.8 = (bf16[4,2,96,256]{3,2,1,0:T(8,128)(2,1)S(1)}, bf16[4,2,96,256]{3,2,1,0:T(8,128)(2,1)S(1)}, u32[]{:S(2)}, u32[]{:S(2)}) collective-permute-start(bf16[4,2,96,256]{3,2,1,0:T(8,128)(2,1)S(1)} %get-tuple-element.38), channel_id=1, source_target_pairs={{0,8},{8,16},{16,24},{24,32},{32,40},{40,48},{48,56},{56,64},{64,7... | collective-permute-start | bytes 1179656 | tf_op jit(solution)/shard_map/ppermute | solution.py:570
  80.3 22.6 %copy-start.5 = (bf16[3,3,3,512,32]{3,4,2,1,0:T(8,128)(2,1)S(1)}, bf16[3,3,3,512,32]{3,4,2,1,0:T(8,128)(2,1)}, u32[]{:S(2)}) copy-start(bf16[3,3,3,512,32]{3,4,2,1,0:T(8,128)(2,1)} %param.17) | copy-start | bytes 2654212
  80.4 22.6 %copy-start.7 = (f32[512]{0:T(512)S(1)}, f32[512]{0:T(512)}, u32[]{:S(2)}) copy-start(f32[512]{0:T(512)} %param.22) | copy-start | bytes 6148
  80.4 22.5 %copy-start.8 = (f32[512]{0:T(512)S(1)}, f32[512]{0:T(512)}, u32[]{:S(2)}) copy-start(f32[512]{0:T(512)} %param.23) | copy-start | bytes 6148

commit v7 on v5

--- a/solution.py
+++ b/solution.py
@@ -338,10 +338,9 @@
         keep = right * below_in if k >= 10 else right
         a = activate(value[:Q].astype(F32), terms) * keep
         b = activate(value[Q:].astype(F32), terms) * keep
-        act[t, k, 0:Q, 0 : 2 * C1] = a.astype(BF16)
-        act[t, k, 0:Q, 2 * C1 :] = b[:, :C1].astype(BF16)
-        act[t, k, Q:, 0 : 2 * C1] = b.astype(BF16)
-        act[t, k, Q:, 2 * C1 :] = raised(a[:, :C1]).astype(BF16)
+        act[t, k, :, 0 : 2 * C1] = a.astype(BF16)
+        act[t, k, :, 2 * C1 : 4 * C1] = b.astype(BF16)
+        act[t, k, :, 4 * C1 :] = raised(a[:, :C1]).astype(BF16)
 
     def lines(t, carry):
         line(t, 0, above[t, 0])
@@ -352,11 +351,11 @@
         line(t, 9, outer[t, 1])
         for r in range(3):
             line(t, 10 + r, below[t, r])
-        value = None
+        parts = []
         for b in range(3):
-            left = jnp.concatenate([act[t, 2 * i + b] for i in range(6)], axis=0)
-            part = mm(left, reduce[b * 3 * C1 : (b + 1) * 3 * C1, :])
-            value = part if value is None else value + part
+            whole = [act[t, 2 * i + b, :, low : low + 3 * C1] for i in range(6) for low in (0, 2 * C1)]
+            parts.append(jnp.concatenate(whole, axis=0))
+        value = mm(jnp.concatenate(parts, axis=1), reduce[...])
         for i in range(6):
             keep = outside
             if i == 0:
@@ -365,13 +364,10 @@
                 keep = keep * below_in
             even = value[i * 2 * Q : i * 2 * Q + Q] * keep
             odd = value[i * 2 * Q + Q : (i + 1) * 2 * Q] * keep
-            e, o = even.astype(BF16), odd.astype(BF16)
-            lev[t, i, 0:Q, 0:C2] = lowered(odd).astype(BF16)
-            lev[t, i, 0:Q, C2 : 2 * C2] = e
-            lev[t, i, 0:Q, 2 * C2 :] = o
-            lev[t, i, Q:, 0:C2] = e
-            lev[t, i, Q:, C2 : 2 * C2] = o
-            lev[t, i, Q:, 2 * C2 :] = raised(even).astype(BF16)
+            lev[t, i, :, 0:C2] = lowered(odd).astype(BF16)
+            lev[t, i, :, C2 : 2 * C2] = even.astype(BF16)
+            lev[t, i, :, 2 * C2 : 3 * C2] = odd.astype(BF16)
+            lev[t, i, :, 3 * C2 :] = raised(even).astype(BF16)
         return carry
 
     lax.fori_loop(0, FRAMES, lines, 0, unroll=True)
@@ -394,8 +390,11 @@
     tables = {K0: second.at[0], MINUS: made.at[0], K2: second.at[2], PAIR: made.at[1], ALL: made.at[2]}
 
     def product(v, s):
-        left = jnp.concatenate([v[0][v[1], b : b + 4].reshape(rows, 3 * C2) for b in range(3)], axis=1)
-        return mm(left, tables[s][...])
+        parts = []
+        for b in range(3):
+            lines = [v[0][v[1], b + i, :, low : low + 3 * C2] for i in range(4) for low in (0, C2)]
+            parts.append(jnp.concatenate(lines, axis=0))
+        return mm(jnp.concatenate(parts, axis=1), tables[s][...])
 
     def store(t, value):
         full = value.reshape(4, 2 * Q, C2)
@@ -423,9 +422,9 @@
         in_specs=[VMEM] * 9,
         out_specs=(VMEM,) * 4,
         scratch_shapes=[
-            pltpu.VMEM((FRAMES, 14, 2 * Q, 3 * C1), BF16),
-            pltpu.VMEM((FRAMES, 6, 2 * Q, 3 * C2), BF16),
-            pltpu.VMEM((4, 6, 2 * Q, 3 * C2), BF16),
+            pltpu.VMEM((FRAMES, 14, Q, 5 * C1), BF16),
+            pltpu.VMEM((FRAMES, 6, Q, 4 * C2), BF16),
+            pltpu.VMEM((4, 6, Q, 4 * C2), BF16),
             pltpu.VMEM((3, 9 * C2, C2), BF16),
         ],
         compiler_params=params(24),

time: 104 us -> 103 us (level)
  no operation moved by 1% of the time
where the time goes in v7:
time: 103 us
  blocking collectives  62.8 us (61%)
  Pallas kernels  17.4 us (17%)
  starting transfers between devices  17.4 us (17%)
  waiting for transfers between devices  2.99 us (3%)
  local copies, waits for them, and re-layouts  2.54 us (2%)
    all_to_all x3, blocking collectives, everywhere(): return lax.all_to_all(share, AXES, 0, 0, tiled=True)  62.8 us
    ppermute x4, starting transfers between devices, from_both(): lax.ppermute(first, axis, backward(axis))  12.9 us
    pallas_call x1, Pallas kernels, second_level(): pl.pallas_call(functools.partial(second_kernel, members=float(devices * F...  6 us
    ppermute x4, starting transfers between devices, from_both(): lax.ppermute(last, axis, forward(axis))  4.51 us
    pallas_call x1, Pallas kernels, middle(): pl.pallas_call(middle_kernel, out_shape=(shape((FRAMES, ROWS, 2 * Q, 2 *...  4.35 us
    pallas_call x1, Pallas kernels, third_level(): pl.pallas_call(functools.partial(third_kernel, members=float(devices * FR...  2.6 us
    unnamed x26, local copies, waits for them, and re-layouts  2.54 us
    ppermute x4, waiting for transfers between devices, from_both(): lax.ppermute(first, axis, backward(axis))  2.27 us
  transfers between devices with their start and end apart: 8, of which 2 were waited for; matrix products, arithmetic and copies ran while one was open for 0% of the time, Pallas kernels for 5%

profile of v7, /device:TPU:1, one launch (start us, length us, event | category | flops | bytes accessed | tf_op | source)
XLA Modules:
  0.0 103.3 jit_solution(2970334787771641307)
XLA Ops:
  0.0 1.3 %copy-done = bf16[4,8,160,128]{3,2,1,0:T(8,128)(2,1)S(1)} copy-done((bf16[4,8,160,128]{3,2,1,0:T(8,128)(2,1)S(1)}, bf16[4,8,160,128]{3,2,1,0:T(8,128)(2,1)}, u32[]{:S(2)}) %copy-start) | copy-done | bytes 1310744
  1.4 2.6 %collective-permute-start = (bf16[32,16,128]{2,1,0:T(8,128)(2,1)S(1)}, bf16[32,16,128]{2,1,0:T(8,128)(2,1)S(1)}, u32[]{:S(2)}, u32[]{:S(2)}) collective-permute-start(bf16[32,16,128]{2,1,0:T(8,128)(2,1)S(1)} %get-tuple-element.22), channel_id=1, source_target_pairs={{0,1},{1,2},{2,3},{3,4},{4,5},{5,6},{6,7},{7,0},{8,9},{9,10},{10,1... | collective-permute-start | bytes 393224 | tf_op jit(solution)/shard_map/ppermute | solution.py:557
  4.0 0.7 collective-permute-start.1
  4.6 1.2 %copy-done.2 = bf16[3,3,3,128,128]{4,3,2,1,0:T(8,128)(2,1)S(1)} copy-done((bf16[3,3,3,128,128]{4,3,2,1,0:T(8,128)(2,1)S(1)}, bf16[3,3,3,128,128]{4,3,2,1,0:T(8,128)(2,1)}, u32[]{:S(2)}) %copy-start.2) | copy-done | bytes 884760
  5.8 0.6 weights.1.table
  6.4 2.3 %collective-permute-done.1.right = bf16[32,16,128]{2,1,0:T(8,128)(2,1)S(1)} collective-permute-done((bf16[32,16,128]{2,1,0:T(8,128)(2,1)S(1)}, bf16[32,16,128]{2,1,0:T(8,128)(2,1)S(1)}, u32[]{:S(2)}, u32[]{:S(2)}) %collective-permute-start.1) | collective-permute-done | bytes 131104 | tf_op jit(solution)/shard_map/ppermute | solution.py:557
  8.7 0.6 planes.1
  9.3 1.4 %collective-permute-start.2 = (bf16[4,48,512]{2,1,0:T(8,128)(2,1)S(1)}, bf16[4,48,512]{2,1,0:T(8,128)(2,1)S(1)}, u32[]{:S(2)}, u32[]{:S(2)}) collective-permute-start(bf16[4,48,512]{2,1,0:T(8,128)(2,1)S(1)} %get-tuple-element.26), channel_id=1, source_target_pairs={{0,8},{8,16},{16,24},{24,32},{32,40},{40,48},{48,56},{56,64},{64,7... | collective-permute-start | bytes 589832 | tf_op jit(solution)/shard_map/ppermute | solution.py:557
  10.7 6.5 %collective-permute-start.3 = (bf16[4,48,512]{2,1,0:T(8,128)(2,1)S(1)}, bf16[4,48,512]{2,1,0:T(8,128)(2,1)S(1)}, u32[]{:S(2)}, u32[]{:S(2)}) collective-permute-start(bf16[4,48,512]{2,1,0:T(8,128)(2,1)S(1)} %get-tuple-element.27), channel_id=1, source_target_pairs={{8,0},{16,8},{24,16},{32,24},{40,32},{48,40},{56,48},{64,56},{72,6... | collective-permute-start | bytes 589832 | tf_op jit(solution)/shard_map/ppermute | solution.py:557
  17.2 4.3 %middle.1 = (f32[4,8,96,256]{3,2,1,0:T(8,128)S(1)}, f32[8,256]{1,0:T(8,128)S(1)}) custom-call(bf16[4,8,48,768]{3,2,1,0:T(8,128)(2,1)S(1)} %get-tuple-element.24.planes, bf16[7680,256]{1,0:T(8,128)(2,1)S(1)} %weights.1.table), custom_call_target="tpu_custom_call" | custom-call | flops 6000000000 | bytes 10000000 | tf_op jit(solution)/shard_map/middle/pallas_call | solution.py:192
  21.6 0.7 collective-permute-done.2.above
  22.3 0.0 copy-start.12
  22.3 0.9 edges.1
  23.3 4.7 %collective-permute-start.5 = (bf16[4,3,96,256]{3,2,1,0:T(8,128)(2,1)S(1)}, bf16[4,3,96,256]{3,2,1,0:T(8,128)(2,1)S(1)}, u32[]{:S(2)}, u32[]{:S(2)}) collective-permute-start(bf16[4,3,96,256]{3,2,1,0:T(8,128)(2,1)S(1)} %get-tuple-element.31), channel_id=1, source_target_pairs={{8,0},{16,8},{24,16},{32,24},{40,32},{48,40},{56,48},{64,56},{72,6... | collective-permute-start | bytes 1769480 | tf_op jit(solution)/shard_map/ppermute | solution.py:557
  27.9 22.5 %all_to_all.33 = f32[256,1,128]{2,1,0:T(1,128)S(1)} all-to-all(f32[256,1,128]{2,1,0:T(1,128)S(1)} %bitcast.32), channel_id=1, replica_groups=mesh['rows'=32,'cols'=8] {'rows','cols'}, dimensions={0} | all-to-all | bytes 262144 | tf_op jit(solution)/shard_map/all_to_all | solution.py:561
  50.5 0.0 copy-start.9
  50.5 0.0 copy-start.10
  50.6 6.0 %second.1 = (f32[4,4,96,256]{3,2,1,0:T(8,128)S(1)}, f32[256,128]{1,0:T(8,128)S(1)}, bf16[4,3,96,256]{3,2,1,0:T(8,128)(2,1)S(1)}, bf16[4,2,96,256]{3,2,1,0:T(8,128)(2,1)S(1)}) custom-call(f32[4,8,96,256]{3,2,1,0:T(8,128)S(1)} %get-tuple-element.25.inner, f32[4,2,96,256]{3,2,1,0:T(8,128)S(1)} %get-tuple-element.29.outer, ...), custom_call_target="tpu_custom_call" | custom-call | flops 6000000000 | bytes 12000000 | tf_op jit(solution)/shard_map/second/pallas_call | solution.py:414
  56.6 1.1 %collective-permute-start.7 = (bf16[4,3,96,256]{3,2,1,0:T(8,128)(2,1)S(1)}, bf16[4,3,96,256]{3,2,1,0:T(8,128)(2,1)S(1)}, u32[]{:S(2)}, u32[]{:S(2)}) collective-permute-start(bf16[4,3,96,256]{3,2,1,0:T(8,128)(2,1)S(1)} %get-tuple-element.35), channel_id=1, source_target_pairs={{8,0},{16,8},{24,16},{32,24},{40,32},{48,40},{56,48},{64,56},{72,6... | collective-permute-start | bytes 1769480 | tf_op jit(solution)/shard_map/ppermute | solution.py:557
  57.6 0.5 collective-permute-start.6
  58.1 20.3 %all_to_all.34 = f32[256,1,128]{2,1,0:T(1,128)S(1)} all-to-all(f32[256,1,128]{2,1,0:T(1,128)S(1)} %bitcast.31), channel_id=1, replica_groups=mesh['rows'=32,'cols'=8] {'rows','cols'}, dimensions={0} | all-to-all | bytes 262144 | tf_op jit(solution)/shard_map/all_to_all | solution.py:561
  78.5 2.6 %third.1 = (bf16[4,4,48,512]{3,2,1,0:T(8,128)(2,1)S(1)}, f32[256,128]{1,0:T(8,128)S(1)}) custom-call(f32[4,4,96,256]{3,2,1,0:T(8,128)S(1)} %get-tuple-element.33.inner, bf16[4,2,96,256]{3,2,1,0:T(8,128)(2,1)S(1)} %collective-permute-done.6.above, bf16[4,3,96,256]{3,2,1,0:T(8,128)(2,1)S(1)} %collective-permute-done.7.below, f32[256,128]{1,0:T(8,128)S(1)} %bitcast.33, ...), custom_call_target="tpu_custom_call" | custom-call | flops 2000000000 | bytes 8000000 | tf_op jit(solution)/shard_map/third/pallas_call | solution.py:483
  81.1 19.9 %all_to_all.35 = f32[256,1,128]{2,1,0:T(1,128)S(1)} all-to-all(f32[256,1,128]{2,1,0:T(1,128)S(1)} %bitcast.34), channel_id=1, replica_groups=mesh['rows'=32,'cols'=8] {'rows','cols'}, dimensions={0} | all-to-all | bytes 262144 | tf_op jit(solution)/shard_map/all_to_all | solution.py:561
  101.0 2.3 %last.1 = bf16[4,2,32,40]{3,2,1,0:T(8,128)(2,1)} custom-call(bf16[4,4,48,512]{3,2,1,0:T(8,128)(2,1)S(1)} %get-tuple-element.37.level, f32[256,128]{1,0:T(8,128)S(1)} %bitcast.35, f32[1,512]{1,0:T(1,128)S(1)} %bitcast.40, f32[1,512]{1,0:T(1,128)S(1)} %bitcast.41, bf16[3,9,32,512]{3,2,1,0:T(8,128)(2,1)S(1)} %bitcast.38), custom_call_target="tpu_custom_call" | custom-call | flops 1000000000 | bytes 4000000 | tf_op jit(solution)/shard_map/last/pallas_call | solution.py:535
  (29 shorter events, 0.1 us)
Async XLA Ops:
  0.0 1.3 %copy-start = (bf16[4,8,160,128]{3,2,1,0:T(8,128)(2,1)S(1)}, bf16[4,8,160,128]{3,2,1,0:T(8,128)(2,1)}, u32[]{:S(2)}) copy-start(bf16[4,8,160,128]{3,2,1,0:T(8,128)(2,1)} %param.12) | copy-start | bytes 3932164
  1.4 5.0 %collective-permute-start = (bf16[32,16,128]{2,1,0:T(8,128)(2,1)S(1)}, bf16[32,16,128]{2,1,0:T(8,128)(2,1)S(1)}, u32[]{:S(2)}, u32[]{:S(2)}) collective-permute-start(bf16[32,16,128]{2,1,0:T(8,128)(2,1)S(1)} %get-tuple-element.22), channel_id=1, source_target_pairs={{0,1},{1,2},{2,3},{3,4},{4,5},{5,6},{6,7},{7,0},{8,9},{9,10},{10,1... | collective-permute-start | bytes 393224 | tf_op jit(solution)/shard_map/ppermute | solution.py:557
  4.0 4.7 %collective-permute-start.1 = (bf16[32,16,128]{2,1,0:T(8,128)(2,1)S(1)}, bf16[32,16,128]{2,1,0:T(8,128)(2,1)S(1)}, u32[]{:S(2)}, u32[]{:S(2)}) collective-permute-start(bf16[32,16,128]{2,1,0:T(8,128)(2,1)S(1)} %get-tuple-element.23), channel_id=1, source_target_pairs={{1,0},{2,1},{3,2},{4,3},{5,4},{6,5},{7,6},{0,7},{9,8},{10,9},{11,1... | collective-permute-start | bytes 393224 | tf_op jit(solution)/shard_map/ppermute | solution.py:557
  4.6 1.2 %copy-start.2 = (bf16[3,3,3,128,128]{4,3,2,1,0:T(8,128)(2,1)S(1)}, bf16[3,3,3,128,128]{4,3,2,1,0:T(8,128)(2,1)}, u32[]{:S(2)}) copy-start(bf16[3,3,3,128,128]{4,3,2,1,0:T(8,128)(2,1)} %param.13) | copy-start | bytes 2654212
  5.8 2.9 %copy-start.1 = (bf16[4,8,160,128]{3,2,1,0:T(8,128)(2,1)S(1)}, bf16[4,8,160,128]{3,2,1,0:T(8,128)(2,1)}, u32[]{:S(2)}) copy-start(bf16[4,8,160,128]{3,2,1,0:T(8,128)(2,1)} %param.12) | copy-start | bytes 3932164
  9.3 13.0 %collective-permute-start.2 = (bf16[4,48,512]{2,1,0:T(8,128)(2,1)S(1)}, bf16[4,48,512]{2,1,0:T(8,128)(2,1)S(1)}, u32[]{:S(2)}, u32[]{:S(2)}) collective-permute-start(bf16[4,48,512]{2,1,0:T(8,128)(2,1)S(1)} %get-tuple-element.26), channel_id=1, source_target_pairs={{0,8},{8,16},{16,24},{24,32},{32,40},{40,48},{48,56},{56,64},{64,7... | collective-permute-start | bytes 589832 | tf_op jit(solution)/shard_map/ppermute | solution.py:557
  10.7 11.6 %collective-permute-start.3 = (bf16[4,48,512]{2,1,0:T(8,128)(2,1)S(1)}, bf16[4,48,512]{2,1,0:T(8,128)(2,1)S(1)}, u32[]{:S(2)}, u32[]{:S(2)}) collective-permute-start(bf16[4,48,512]{2,1,0:T(8,128)(2,1)S(1)} %get-tuple-element.27), channel_id=1, source_target_pairs={{8,0},{16,8},{24,16},{32,24},{40,32},{48,40},{56,48},{64,56},{72,6... | collective-permute-start | bytes 589832 | tf_op jit(solution)/shard_map/ppermute | solution.py:557
  22.3 28.2 %copy-start.3 = (bf16[3,3,3,256,256]{4,3,2,1,0:T(8,128)(2,1)S(1)}, bf16[3,3,3,256,256]{4,3,2,1,0:T(8,128)(2,1)}, u32[]{:S(2)}) copy-start(bf16[3,3,3,256,256]{4,3,2,1,0:T(8,128)(2,1)} %param.15) | copy-start | bytes 10616836
  22.3 28.2 %copy-start.6 = (bf16[3,3,128,256]{3,2,1,0:T(8,128)(2,1)S(1)}, bf16[3,3,128,256]{3,2,1,0:T(8,128)(2,1)}, u32[]{:S(2)}) copy-start(bf16[3,3,128,256]{3,2,1,0:T(8,128)(2,1)} %param.14) | copy-start | bytes 1769476
  22.3 28.2 %copy-start.11 = (f32[128]{0:T(128)S(1)}, f32[128]{0:T(128)}, u32[]{:S(2)}) copy-start(f32[128]{0:T(128)} %param.18) | copy-start | bytes 1540
  22.3 28.2 %copy-start.12 = (f32[128]{0:T(128)S(1)}, f32[128]{0:T(128)}, u32[]{:S(2)}) copy-start(f32[128]{0:T(128)} %param.19) | copy-start | bytes 1540
  23.3 27.2 %collective-permute-start.5 = (bf16[4,3,96,256]{3,2,1,0:T(8,128)(2,1)S(1)}, bf16[4,3,96,256]{3,2,1,0:T(8,128)(2,1)S(1)}, u32[]{:S(2)}, u32[]{:S(2)}) collective-permute-start(bf16[4,3,96,256]{3,2,1,0:T(8,128)(2,1)S(1)} %get-tuple-element.31), channel_id=1, source_target_pairs={{8,0},{16,8},{24,16},{32,24},{40,32},{48,40},{56,48},{64,56},{72,6... | collective-permute-start | bytes 1769480 | tf_op jit(solution)/shard_map/ppermute | solution.py:557
  27.9 22.5 %collective-permute-start.4 = (bf16[4,2,96,256]{3,2,1,0:T(8,128)(2,1)S(1)}, bf16[4,2,96,256]{3,2,1,0:T(8,128)(2,1)S(1)}, u32[]{:S(2)}, u32[]{:S(2)}) collective-permute-start(bf16[4,2,96,256]{3,2,1,0:T(8,128)(2,1)S(1)} %get-tuple-element.30), channel_id=1, source_target_pairs={{0,8},{8,16},{16,24},{24,32},{32,40},{40,48},{48,56},{56,64},{64,7... | collective-permute-start | bytes 1179656 | tf_op jit(solution)/shard_map/ppermute | solution.py:557
  50.5 27.9 %copy-start.4 = (bf16[3,3,256,512]{3,2,1,0:T(8,128)(2,1)S(1)}, bf16[3,3,256,512]{3,2,1,0:T(8,128)(2,1)}, u32[]{:S(2)}) copy-start(bf16[3,3,256,512]{3,2,1,0:T(8,128)(2,1)} %param.16) | copy-start | bytes 7077892
  50.5 27.9 %copy-start.9 = (f32[256]{0:T(256)S(1)}, f32[256]{0:T(256)}, u32[]{:S(2)}) copy-start(f32[256]{0:T(256)} %param.20) | copy-start | bytes 3076
  50.5 27.9 %copy-start.10 = (f32[256]{0:T(256)S(1)}, f32[256]{0:T(256)}, u32[]{:S(2)}) copy-start(f32[256]{0:T(256)} %param.21) | copy-start | bytes 3076
  56.6 21.9 %collective-permute-start.7 = (bf16[4,3,96,256]{3,2,1,0:T(8,128)(2,1)S(1)}, bf16[4,3,96,256]{3,2,1,0:T(8,128)(2,1)S(1)}, u32[]{:S(2)}, u32[]{:S(2)}) collective-permute-start(bf16[4,3,96,256]{3,2,1,0:T(8,128)(2,1)S(1)} %get-tuple-element.35), channel_id=1, source_target_pairs={{8,0},{16,8},{24,16},{32,24},{40,32},{48,40},{56,48},{64,56},{72,6... | collective-permute-start | bytes 1769480 | tf_op jit(solution)/shard_map/ppermute | solution.py:557
  57.6 20.8 %collective-permute-start.6 = (bf16[4,2,96,256]{3,2,1,0:T(8,128)(2,1)S(1)}, bf16[4,2,96,256]{3,2,1,0:T(8,128)(2,1)S(1)}, u32[]{:S(2)}, u32[]{:S(2)}) collective-permute-start(bf16[4,2,96,256]{3,2,1,0:T(8,128)(2,1)S(1)} %get-tuple-element.34), channel_id=1, source_target_pairs={{0,8},{8,16},{16,24},{24,32},{32,40},{40,48},{48,56},{56,64},{64,7... | collective-permute-start | bytes 1179656 | tf_op jit(solution)/shard_map/ppermute | solution.py:557
  78.5 22.6 %copy-start.5 = (bf16[3,3,3,512,32]{3,4,2,1,0:T(8,128)(2,1)S(1)}, bf16[3,3,3,512,32]{3,4,2,1,0:T(8,128)(2,1)}, u32[]{:S(2)}) copy-start(bf16[3,3,3,512,32]{3,4,2,1,0:T(8,128)(2,1)} %param.17) | copy-start | bytes 2654212
  78.5 22.5 %copy-start.7 = (f32[512]{0:T(512)S(1)}, f32[512]{0:T(512)}, u32[]{:S(2)}) copy-start(f32[512]{0:T(512)} %param.22) | copy-start | bytes 6148
  78.5 22.5 %copy-start.8 = (f32[512]{0:T(512)S(1)}, f32[512]{0:T(512)}, u32[]{:S(2)}) copy-start(f32[512]{0:T(512)} %param.23) | copy-start | bytes 6148

commit v8 on v7

--- a/solution.py
+++ b/solution.py
@@ -98,7 +98,7 @@
         compiler_params=params(4),
         cost_estimate=cost(0, 4e5),
         name="cut",
-    )(features.reshape(FRAMES * ROWS, COLS, C1))
+    )(pltpu.with_memory_space_constraint(features.reshape(FRAMES * ROWS, COLS, C1), pltpu.HBM))
 
 
 def planes_kernel(left, own, right, planes, top, bottom, line):

time: 103 us -> 103 us (level)
  local copies, waits for them, and re-layouts: 2.54 us -> 1.23 us
    unnamed x26 -> x24, local copies, waits for them, and re-layouts: 2.54 us -> 1.23 us
where the time goes in v8:
time: 103 us
  blocking collectives  62.8 us (61%)
  Pallas kernels  18.3 us (18%)
  starting transfers between devices  17.4 us (17%)
  waiting for transfers between devices  2.99 us (3%)
  local copies, waits for them, and re-layouts  1.23 us (1%)
    all_to_all x3, blocking collectives, everywhere(): return lax.all_to_all(share, AXES, 0, 0, tiled=True)  62.8 us
    ppermute x4, starting transfers between devices, from_both(): lax.ppermute(first, axis, backward(axis))  12.9 us
    pallas_call x1, Pallas kernels, second_level(): pl.pallas_call(functools.partial(second_kernel, members=float(devices * F...  6 us
    ppermute x4, starting transfers between devices, from_both(): lax.ppermute(last, axis, forward(axis))  4.51 us
    pallas_call x1, Pallas kernels, middle(): pl.pallas_call(middle_kernel, out_shape=(shape((FRAMES, ROWS, 2 * Q, 2 *...  4.35 us
    pallas_call x1, Pallas kernels, third_level(): pl.pallas_call(functools.partial(third_kernel, members=float(devices * FR...  2.6 us
    ppermute x4, waiting for transfers between devices, from_both(): lax.ppermute(first, axis, backward(axis))  2.27 us
    pallas_call x1, Pallas kernels, last_level(): pl.pallas_call(functools.partial(last_kernel, members=float(devices * FRA...  2.25 us
  transfers between devices with their start and end apart: 8, of which 2 were waited for; matrix products, arithmetic and copies ran while one was open for 0% of the time, Pallas kernels for 5%

profile of v8, /device:TPU:1, one launch (start us, length us, event | category | flops | bytes accessed | tf_op | source)
XLA Modules:
  0.0 102.9 jit_solution(939650031497268402)
XLA Ops:
  0.0 1.0 cut.1
  1.0 2.6 %collective-permute-start = (bf16[32,16,128]{2,1,0:T(8,128)(2,1)S(1)}, bf16[32,16,128]{2,1,0:T(8,128)(2,1)S(1)}, u32[]{:S(2)}, u32[]{:S(2)}) collective-permute-start(bf16[32,16,128]{2,1,0:T(8,128)(2,1)S(1)} %get-tuple-element.22), channel_id=1, source_target_pairs={{0,1},{1,2},{2,3},{3,4},{4,5},{5,6},{6,7},{7,0},{8,9},{9,10},{10,1... | collective-permute-start | bytes 393224 | tf_op jit(solution)/shard_map/ppermute | solution.py:557
  3.6 0.7 collective-permute-start.1
  4.3 1.2 %copy-done.1 = bf16[3,3,3,128,128]{4,3,2,1,0:T(8,128)(2,1)S(1)} copy-done((bf16[3,3,3,128,128]{4,3,2,1,0:T(8,128)(2,1)S(1)}, bf16[3,3,3,128,128]{4,3,2,1,0:T(8,128)(2,1)}, u32[]{:S(2)}) %copy-start.1) | copy-done | bytes 884760
  5.4 0.6 weights.1.table
  6.0 2.3 %collective-permute-done.1.right = bf16[32,16,128]{2,1,0:T(8,128)(2,1)S(1)} collective-permute-done((bf16[32,16,128]{2,1,0:T(8,128)(2,1)S(1)}, bf16[32,16,128]{2,1,0:T(8,128)(2,1)S(1)}, u32[]{:S(2)}, u32[]{:S(2)}) %collective-permute-start.1) | collective-permute-done | bytes 131104 | tf_op jit(solution)/shard_map/ppermute | solution.py:557
  8.3 0.6 planes.1
  8.9 1.4 %collective-permute-start.2 = (bf16[4,48,512]{2,1,0:T(8,128)(2,1)S(1)}, bf16[4,48,512]{2,1,0:T(8,128)(2,1)S(1)}, u32[]{:S(2)}, u32[]{:S(2)}) collective-permute-start(bf16[4,48,512]{2,1,0:T(8,128)(2,1)S(1)} %get-tuple-element.26), channel_id=1, source_target_pairs={{0,8},{8,16},{16,24},{24,32},{32,40},{40,48},{48,56},{56,64},{64,7... | collective-permute-start | bytes 589832 | tf_op jit(solution)/shard_map/ppermute | solution.py:557
  10.4 6.5 %collective-permute-start.3 = (bf16[4,48,512]{2,1,0:T(8,128)(2,1)S(1)}, bf16[4,48,512]{2,1,0:T(8,128)(2,1)S(1)}, u32[]{:S(2)}, u32[]{:S(2)}) collective-permute-start(bf16[4,48,512]{2,1,0:T(8,128)(2,1)S(1)} %get-tuple-element.27), channel_id=1, source_target_pairs={{8,0},{16,8},{24,16},{32,24},{40,32},{48,40},{56,48},{64,56},{72,6... | collective-permute-start | bytes 589832 | tf_op jit(solution)/shard_map/ppermute | solution.py:557
  16.8 4.3 %middle.1 = (f32[4,8,96,256]{3,2,1,0:T(8,128)S(1)}, f32[8,256]{1,0:T(8,128)S(1)}) custom-call(bf16[4,8,48,768]{3,2,1,0:T(8,128)(2,1)S(1)} %get-tuple-element.24.planes, bf16[7680,256]{1,0:T(8,128)(2,1)S(1)} %weights.1.table), custom_call_target="tpu_custom_call" | custom-call | flops 6000000000 | bytes 10000000 | tf_op jit(solution)/shard_map/middle/pallas_call | solution.py:192
  21.2 0.7 collective-permute-done.2.above
  21.9 0.0 copy-start.11
  21.9 0.9 edges.1
  22.9 4.7 %collective-permute-start.5 = (bf16[4,3,96,256]{3,2,1,0:T(8,128)(2,1)S(1)}, bf16[4,3,96,256]{3,2,1,0:T(8,128)(2,1)S(1)}, u32[]{:S(2)}, u32[]{:S(2)}) collective-permute-start(bf16[4,3,96,256]{3,2,1,0:T(8,128)(2,1)S(1)} %get-tuple-element.31), channel_id=1, source_target_pairs={{8,0},{16,8},{24,16},{32,24},{40,32},{48,40},{56,48},{64,56},{72,6... | collective-permute-start | bytes 1769480 | tf_op jit(solution)/shard_map/ppermute | solution.py:557
  27.6 22.5 %all_to_all.33 = f32[256,1,128]{2,1,0:T(1,128)S(1)} all-to-all(f32[256,1,128]{2,1,0:T(1,128)S(1)} %bitcast.32), channel_id=1, replica_groups=mesh['rows'=32,'cols'=8] {'rows','cols'}, dimensions={0} | all-to-all | bytes 262144 | tf_op jit(solution)/shard_map/all_to_all | solution.py:561
  50.2 0.0 copy-start.3
  50.2 0.0 copy-start.9
  50.2 6.0 %second.1 = (f32[4,4,96,256]{3,2,1,0:T(8,128)S(1)}, f32[256,128]{1,0:T(8,128)S(1)}, bf16[4,3,96,256]{3,2,1,0:T(8,128)(2,1)S(1)}, bf16[4,2,96,256]{3,2,1,0:T(8,128)(2,1)S(1)}) custom-call(f32[4,8,96,256]{3,2,1,0:T(8,128)S(1)} %get-tuple-element.25.inner, f32[4,2,96,256]{3,2,1,0:T(8,128)S(1)} %get-tuple-element.29.outer, ...), custom_call_target="tpu_custom_call" | custom-call | flops 6000000000 | bytes 12000000 | tf_op jit(solution)/shard_map/second/pallas_call | solution.py:414
  56.2 1.1 %collective-permute-start.7 = (bf16[4,3,96,256]{3,2,1,0:T(8,128)(2,1)S(1)}, bf16[4,3,96,256]{3,2,1,0:T(8,128)(2,1)S(1)}, u32[]{:S(2)}, u32[]{:S(2)}) collective-permute-start(bf16[4,3,96,256]{3,2,1,0:T(8,128)(2,1)S(1)} %get-tuple-element.35), channel_id=1, source_target_pairs={{8,0},{16,8},{24,16},{32,24},{40,32},{48,40},{56,48},{64,56},{72,6... | collective-permute-start | bytes 1769480 | tf_op jit(solution)/shard_map/ppermute | solution.py:557
  57.3 0.5 collective-permute-start.6
  57.7 20.3 %all_to_all.34 = f32[256,1,128]{2,1,0:T(1,128)S(1)} all-to-all(f32[256,1,128]{2,1,0:T(1,128)S(1)} %bitcast.31), channel_id=1, replica_groups=mesh['rows'=32,'cols'=8] {'rows','cols'}, dimensions={0} | all-to-all | bytes 262144 | tf_op jit(solution)/shard_map/all_to_all | solution.py:561
  78.1 2.6 %third.1 = (bf16[4,4,48,512]{3,2,1,0:T(8,128)(2,1)S(1)}, f32[256,128]{1,0:T(8,128)S(1)}) custom-call(f32[4,4,96,256]{3,2,1,0:T(8,128)S(1)} %get-tuple-element.33.inner, bf16[4,2,96,256]{3,2,1,0:T(8,128)(2,1)S(1)} %collective-permute-done.6.above, bf16[4,3,96,256]{3,2,1,0:T(8,128)(2,1)S(1)} %collective-permute-done.7.below, f32[256,128]{1,0:T(8,128)S(1)} %bitcast.33, ...), custom_call_target="tpu_custom_call" | custom-call | flops 2000000000 | bytes 8000000 | tf_op jit(solution)/shard_map/third/pallas_call | solution.py:483
  80.7 19.9 %all_to_all.35 = f32[256,1,128]{2,1,0:T(1,128)S(1)} all-to-all(f32[256,1,128]{2,1,0:T(1,128)S(1)} %bitcast.34), channel_id=1, replica_groups=mesh['rows'=32,'cols'=8] {'rows','cols'}, dimensions={0} | all-to-all | bytes 262144 | tf_op jit(solution)/shard_map/all_to_all | solution.py:561
  100.6 2.3 %last.1 = bf16[4,2,32,40]{3,2,1,0:T(8,128)(2,1)} custom-call(bf16[4,4,48,512]{3,2,1,0:T(8,128)(2,1)S(1)} %get-tuple-element.37.level, f32[256,128]{1,0:T(8,128)S(1)} %bitcast.35, f32[1,512]{1,0:T(1,128)S(1)} %bitcast.40, f32[1,512]{1,0:T(1,128)S(1)} %bitcast.41, bf16[3,9,32,512]{3,2,1,0:T(8,128)(2,1)S(1)} %bitcast.38), custom_call_target="tpu_custom_call" | custom-call | flops 1000000000 | bytes 4000000 | tf_op jit(solution)/shard_map/last/pallas_call | solution.py:535
  (27 shorter events, 0.1 us)
Async XLA Ops:
  1.0 5.0 %collective-permute-start = (bf16[32,16,128]{2,1,0:T(8,128)(2,1)S(1)}, bf16[32,16,128]{2,1,0:T(8,128)(2,1)S(1)}, u32[]{:S(2)}, u32[]{:S(2)}) collective-permute-start(bf16[32,16,128]{2,1,0:T(8,128)(2,1)S(1)} %get-tuple-element.22), channel_id=1, source_target_pairs={{0,1},{1,2},{2,3},{3,4},{4,5},{5,6},{6,7},{7,0},{8,9},{9,10},{10,1... | collective-permute-start | bytes 393224 | tf_op jit(solution)/shard_map/ppermute | solution.py:557
  3.6 4.7 %collective-permute-start.1 = (bf16[32,16,128]{2,1,0:T(8,128)(2,1)S(1)}, bf16[32,16,128]{2,1,0:T(8,128)(2,1)S(1)}, u32[]{:S(2)}, u32[]{:S(2)}) collective-permute-start(bf16[32,16,128]{2,1,0:T(8,128)(2,1)S(1)} %get-tuple-element.23), channel_id=1, source_target_pairs={{1,0},{2,1},{3,2},{4,3},{5,4},{6,5},{7,6},{0,7},{9,8},{10,9},{11,1... | collective-permute-start | bytes 393224 | tf_op jit(solution)/shard_map/ppermute | solution.py:557
  4.3 1.2 %copy-start.1 = (bf16[3,3,3,128,128]{4,3,2,1,0:T(8,128)(2,1)S(1)}, bf16[3,3,3,128,128]{4,3,2,1,0:T(8,128)(2,1)}, u32[]{:S(2)}) copy-start(bf16[3,3,3,128,128]{4,3,2,1,0:T(8,128)(2,1)} %param.13) | copy-start | bytes 2654212
  5.4 2.9 %copy-start = (bf16[4,8,160,128]{3,2,1,0:T(8,128)(2,1)S(1)}, bf16[4,8,160,128]{3,2,1,0:T(8,128)(2,1)}, u32[]{:S(2)}) copy-start(bf16[4,8,160,128]{3,2,1,0:T(8,128)(2,1)} %param.12) | copy-start | bytes 3932164
  8.9 13.0 %collective-permute-start.2 = (bf16[4,48,512]{2,1,0:T(8,128)(2,1)S(1)}, bf16[4,48,512]{2,1,0:T(8,128)(2,1)S(1)}, u32[]{:S(2)}, u32[]{:S(2)}) collective-permute-start(bf16[4,48,512]{2,1,0:T(8,128)(2,1)S(1)} %get-tuple-element.26), channel_id=1, source_target_pairs={{0,8},{8,16},{16,24},{24,32},{32,40},{40,48},{48,56},{56,64},{64,7... | collective-permute-start | bytes 589832 | tf_op jit(solution)/shard_map/ppermute | solution.py:557
  10.4 11.6 %collective-permute-start.3 = (bf16[4,48,512]{2,1,0:T(8,128)(2,1)S(1)}, bf16[4,48,512]{2,1,0:T(8,128)(2,1)S(1)}, u32[]{:S(2)}, u32[]{:S(2)}) collective-permute-start(bf16[4,48,512]{2,1,0:T(8,128)(2,1)S(1)} %get-tuple-element.27), channel_id=1, source_target_pairs={{8,0},{16,8},{24,16},{32,24},{40,32},{48,40},{56,48},{64,56},{72,6... | collective-permute-start | bytes 589832 | tf_op jit(solution)/shard_map/ppermute | solution.py:557
  21.9 28.2 %copy-start.2 = (bf16[3,3,3,256,256]{4,3,2,1,0:T(8,128)(2,1)S(1)}, bf16[3,3,3,256,256]{4,3,2,1,0:T(8,128)(2,1)}, u32[]{:S(2)}) copy-start(bf16[3,3,3,256,256]{4,3,2,1,0:T(8,128)(2,1)} %param.15) | copy-start | bytes 10616836
  21.9 28.2 %copy-start.5 = (bf16[3,3,128,256]{3,2,1,0:T(8,128)(2,1)S(1)}, bf16[3,3,128,256]{3,2,1,0:T(8,128)(2,1)}, u32[]{:S(2)}) copy-start(bf16[3,3,128,256]{3,2,1,0:T(8,128)(2,1)} %param.14) | copy-start | bytes 1769476
  21.9 28.2 %copy-start.10 = (f32[128]{0:T(128)S(1)}, f32[128]{0:T(128)}, u32[]{:S(2)}) copy-start(f32[128]{0:T(128)} %param.18) | copy-start | bytes 1540
  21.9 28.2 %copy-start.11 = (f32[128]{0:T(128)S(1)}, f32[128]{0:T(128)}, u32[]{:S(2)}) copy-start(f32[128]{0:T(128)} %param.19) | copy-start | bytes 1540
  22.9 27.2 %collective-permute-start.5 = (bf16[4,3,96,256]{3,2,1,0:T(8,128)(2,1)S(1)}, bf16[4,3,96,256]{3,2,1,0:T(8,128)(2,1)S(1)}, u32[]{:S(2)}, u32[]{:S(2)}) collective-permute-start(bf16[4,3,96,256]{3,2,1,0:T(8,128)(2,1)S(1)} %get-tuple-element.31), channel_id=1, source_target_pairs={{8,0},{16,8},{24,16},{32,24},{40,32},{48,40},{56,48},{64,56},{72,6... | collective-permute-start | bytes 1769480 | tf_op jit(solution)/shard_map/ppermute | solution.py:557
  27.6 22.5 %collective-permute-start.4 = (bf16[4,2,96,256]{3,2,1,0:T(8,128)(2,1)S(1)}, bf16[4,2,96,256]{3,2,1,0:T(8,128)(2,1)S(1)}, u32[]{:S(2)}, u32[]{:S(2)}) collective-permute-start(bf16[4,2,96,256]{3,2,1,0:T(8,128)(2,1)S(1)} %get-tuple-element.30), channel_id=1, source_target_pairs={{0,8},{8,16},{16,24},{24,32},{32,40},{40,48},{48,56},{56,64},{64,7... | collective-permute-start | bytes 1179656 | tf_op jit(solution)/shard_map/ppermute | solution.py:557
  50.2 27.9 %copy-start.3 = (bf16[3,3,256,512]{3,2,1,0:T(8,128)(2,1)S(1)}, bf16[3,3,256,512]{3,2,1,0:T(8,128)(2,1)}, u32[]{:S(2)}) copy-start(bf16[3,3,256,512]{3,2,1,0:T(8,128)(2,1)} %param.16) | copy-start | bytes 7077892
  50.2 27.9 %copy-start.8 = (f32[256]{0:T(256)S(1)}, f32[256]{0:T(256)}, u32[]{:S(2)}) copy-start(f32[256]{0:T(256)} %param.20) | copy-start | bytes 3076
  50.2 27.9 %copy-start.9 = (f32[256]{0:T(256)S(1)}, f32[256]{0:T(256)}, u32[]{:S(2)}) copy-start(f32[256]{0:T(256)} %param.21) | copy-start | bytes 3076
  56.2 21.9 %collective-permute-start.7 = (bf16[4,3,96,256]{3,2,1,0:T(8,128)(2,1)S(1)}, bf16[4,3,96,256]{3,2,1,0:T(8,128)(2,1)S(1)}, u32[]{:S(2)}, u32[]{:S(2)}) collective-permute-start(bf16[4,3,96,256]{3,2,1,0:T(8,128)(2,1)S(1)} %get-tuple-element.35), channel_id=1, source_target_pairs={{8,0},{16,8},{24,16},{32,24},{40,32},{48,40},{56,48},{64,56},{72,6... | collective-permute-start | bytes 1769480 | tf_op jit(solution)/shard_map/ppermute | solution.py:557
  57.3 20.8 %collective-permute-start.6 = (bf16[4,2,96,256]{3,2,1,0:T(8,128)(2,1)S(1)}, bf16[4,2,96,256]{3,2,1,0:T(8,128)(2,1)S(1)}, u32[]{:S(2)}, u32[]{:S(2)}) collective-permute-start(bf16[4,2,96,256]{3,2,1,0:T(8,128)(2,1)S(1)} %get-tuple-element.34), channel_id=1, source_target_pairs={{0,8},{8,16},{16,24},{24,32},{32,40},{40,48},{48,56},{56,64},{64,7... | collective-permute-start | bytes 1179656 | tf_op jit(solution)/shard_map/ppermute | solution.py:557
  78.1 22.6 %copy-start.4 = (bf16[3,3,3,512,32]{3,4,2,1,0:T(8,128)(2,1)S(1)}, bf16[3,3,3,512,32]{3,4,2,1,0:T(8,128)(2,1)}, u32[]{:S(2)}) copy-start(bf16[3,3,3,512,32]{3,4,2,1,0:T(8,128)(2,1)} %param.17) | copy-start | bytes 2654212
  78.1 22.5 %copy-start.6 = (f32[512]{0:T(512)S(1)}, f32[512]{0:T(512)}, u32[]{:S(2)}) copy-start(f32[512]{0:T(512)} %param.22) | copy-start | bytes 6148
  78.1 22.5 %copy-start.7 = (f32[512]{0:T(512)S(1)}, f32[512]{0:T(512)}, u32[]{:S(2)}) copy-start(f32[512]{0:T(512)} %param.23) | copy-start | bytes 6148
